TPU v7x, 32 devices: a whole 2x2x4 slice. The times are simulated.
32 devices in a mesh: narrow: 4 (over x, core), wide: 8 (over z, y).
Axes of the slice: x: 2, y: 2, z: 4, core: 2. Of those that a mesh axis runs over, the one named last changes fastest.
Arguments:
- inputs: bfloat16 [4, 1024, 768], P('narrow', 'wide'), may hold values from -6 to 6
- segment_ids: int32 [4, 1024], P('narrow', 'wide'), may hold values from 0 to 3, as said below
- gain_attn: float32 [768], replicated, may hold values from 0.1 to 1.9
- w_query: bfloat16 [768, 768], replicated, may hold values from -0.0546875 to 0.0546875
- w_key: bfloat16 [768, 768], replicated, may hold values from -0.21875 to 0.21875
- w_value: bfloat16 [768, 768], replicated, may hold values from -0.21875 to 0.21875
- w_out: bfloat16 [768, 768], replicated, may hold values from -2.5 to 2.5
- gain_ffn: float32 [768], replicated, may hold values from 0.1 to 1.9
- w_gate: bfloat16 [768, 2048], replicated, may hold values from -0.21875 to 0.21875
- w_up: bfloat16 [768, 2048], replicated, may hold values from -0.21875 to 0.21875
- w_down: bfloat16 [2048, 768], replicated, may hold values from -0.125 to 0.125
- bias_table: float32 [32, 12], replicated, may hold values from -4 to 4
- cotangent: bfloat16 [4, 1024, 768], P('narrow', 'wide'), may hold values from -6 to 6
Outputs:
- output: bfloat16 [4, 1024, 768], P('narrow', 'wide')
- input_grad: float32 [4, 1024, 768], P('narrow', 'wide')
- grad_gain_attn: float32 [768], replicated
- grad_w_query: float32 [768, 768], P('wide', 'narrow')
- grad_w_key: float32 [768, 768], P('wide', 'narrow')
- grad_w_value: float32 [768, 768], P('wide', 'narrow')
- grad_w_out: float32 [768, 768], P('wide', 'narrow')
- grad_gain_ffn: float32 [768], replicated
- grad_w_gate: float32 [768, 2048], P('wide', 'narrow')
- grad_w_up: float32 [768, 2048], P('wide', 'narrow')
- grad_w_down: float32 [2048, 768], P('wide', 'narrow')
- grad_bias_table: float32 [32, 12], replicated
Inputs may be any that keep to these rules, and one draw needn't show every extreme that they name: `segment_ids`: each row holds groups 1, 2 and 3 in this order, then padding (0) of 1 to 32 tokens at its end; group 1 ends within the first 64 tokens, group 3 has 1 to 32 tokens and so lies within the last 64 tokens.
All inputs are finite; a program needn't handle non-finite values.
Results may differ from a plain program's by a relative error of at most 0.02.
Values may be sent and summed in bfloat16 or wider, within the bound.
No kernel may reach another device: no remote copies, remote signals or barrier semaphores. Data moves between devices by JAX's collectives and lax.ppermute only.
A program may use at most 128 MiB of HBM per device.

v0:
```python
import functools

import jax
import jax.numpy as jnp
import numpy as np
from jax import lax
from jax.experimental import pallas as pl
from jax.experimental.pallas import tpu as pltpu
from jax.sharding import PartitionSpec as P

cutoffs = (1, 2, 3, 4, 5, 6, 7, 8, 12, 16, 23, 32, 46, 64, 91)
epsilon = 1e-06
masked_score = -1000000000.0
highest = lax.Precision.HIGHEST
axes = ("narrow", "wide")
groups = 4
bf16 = jnp.bfloat16
f32 = jnp.float32


def dot(left, right, left_dim, right_dim):
    return lax.dot_general(
        left, right, (((left_dim,), (right_dim,)), ((), ())), preferred_element_type=f32
    )


class Layout:
    def __init__(self, narrow, wide):
        self.narrow = narrow
        self.wide = wide
        self.s_count = wide // (groups * 2)

    def index(self, x, c, g, s, y):
        return (x * 2 + c) * self.wide + (g * self.s_count + s) * 2 + y

    def send(self, block, target):
        route = []
        for x in range(self.narrow // 2):
            for c in range(2):
                for g in range(groups):
                    for s in range(self.s_count):
                        for y in range(2):
                            route.append(
                                (self.index(x, c, g, s, y), self.index(*target(x, c, g, s, y)))
                            )
        return lax.ppermute(block, axes, route)

    def turned(self, block, d):
        return self.send(block, lambda x, c, g, s, y: (x, y, g ^ d, s, c))

    def core(self, block):
        return self.send(block, lambda x, c, g, s, y: (x, 1 - c, g, s, y))

    def across(self, block):
        return self.send(block, lambda x, c, g, s, y: (x ^ 1, c, g, s, y))

    def wide_bit(self, block, bit):
        def target(x, c, g, s, y):
            w = ((g * self.s_count + s) * 2 + y) ^ (1 << bit)
            return (x, c, w // (2 * self.s_count), (w // 2) % self.s_count, w % 2)

        return self.send(block, target)


def rms_scale(values):
    return lax.rsqrt(jnp.mean(values * values, axis=-1, keepdims=True) + epsilon)


def bucket_row(span, half_count):
    offset = lax.broadcasted_iota(jnp.int32, (1, span), 1) - span // 2
    distance = jnp.abs(offset)
    bucket = jnp.where(offset > 0, half_count, 0)
    for cutoff in cutoffs:
        bucket = bucket + jnp.where(distance >= cutoff, 1, 0)
    return bucket


def cost(microseconds):
    return pl.CostEstimate(
        flops=int(microseconds * 1.15e9), bytes_accessed=1024, transcendentals=0
    )


def kernel_call(
    body, name, smem, inputs, outputs, scratch=(), in_hbm=(), staged=(), mebibytes=4, us=3
):
    n_smem, n_in, n_out = len(smem), len(inputs), len(outputs)

    def kernel(*refs):
        given = refs[n_smem : n_smem + n_in]
        outs = refs[n_smem + n_in : n_smem + n_in + n_out]
        rest = refs[n_smem + n_in + n_out :]
        buffers = dict(zip(staged, rest[: len(staged)]))
        arrivals = {}
        for at, i in enumerate(staged):
            arrivals[i] = pltpu.make_async_copy(given[i], buffers[i], rest[-1].at[at])
            arrivals[i].start()

        def get(i):
            if i in arrivals:
                arrivals.pop(i).wait()
            return buffers.get(i, given[i])

        body(refs[:n_smem], get, outs, *rest[len(staged) : len(rest) - (1 if staged else 0)])
        for i in staged:
            get(i)

    hbm = pl.BlockSpec(memory_space=pltpu.HBM)
    vmem = pl.BlockSpec(memory_space=pltpu.VMEM)
    copies = [pltpu.SemaphoreType.DMA((len(staged),))] if staged else []
    return pl.pallas_call(
        kernel,
        out_shape=outputs,
        in_specs=[pl.BlockSpec(memory_space=pltpu.SMEM)] * n_smem
        + [hbm if i in in_hbm or i in staged else vmem for i in range(n_in)],
        out_specs=[hbm if ("out", i) in in_hbm else vmem for i in range(n_out)],
        scratch_shapes=[pltpu.VMEM(inputs[i].shape, inputs[i].dtype) for i in staged]
        + list(scratch)
        + copies,
        compiler_params=pltpu.CompilerParams(vmem_limit_bytes=mebibytes * 2**20),
        cost_estimate=cost(us),
        name=name,
    )(*smem, *inputs)


def shaped(dtype, *shape):
    return jax.ShapeDtypeStruct(shape, dtype)


def group_window(group, local):
    start = (group * local) // 128 * 128
    return pl.multiple_of(start, 128), (group * local) % 128 != 0


def pack_body(smem, get, outs, sems):
    tokens_ref, segment_ref = get(0), get(1)
    packet, spare = outs[0], sems[0]
    tok, width = tokens_ref.shape
    copy = pltpu.make_async_copy(tokens_ref, packet.at[pl.ds(0, tok)], sems[1].at[0])
    copy.start()
    row = jnp.broadcast_to(segment_ref[...].astype(f32), (spare.shape[0], tok))
    spare[:, :tok] = row.astype(bf16)
    spare[:, tok:] = jnp.zeros((spare.shape[0], width - tok), bf16)
    more = pltpu.make_async_copy(spare, packet.at[pl.ds(tok, spare.shape[0])], sems[1].at[1])
    more.start()
    more.wait()
    copy.wait()


def packed(tokens, segment_ids):
    tok, width = tokens.shape
    return kernel_call(
        lambda smem, get, outs, *scratch: pack_body(smem, get, outs, scratch),
        "pack",
        [],
        [tokens, segment_ids],
        [shaped(bf16, tok + 16, width)],
        scratch=[pltpu.VMEM((16, width), bf16), pltpu.SemaphoreType.DMA((2,))],
        in_hbm=(0, ("out", 0)),
        staged=(1,),
        mebibytes=2,
        us=1,
    )[0]


def bias_body(smem, get, outs):
    place, table = smem
    (rows_ref,) = outs
    span = rows_ref.shape[1]
    heads = table.shape[1] // groups
    buckets = bucket_row(span, table.shape[0] // 2)
    for h in range(heads):
        head = place[0] * heads + h
        row = jnp.full((1, span), table[0, head], f32)
        for b in range(1, table.shape[0]):
            row = jnp.where(buckets == b, table[b, head], row)
        rows_ref[h : h + 1, :] = row


def bias_rows(place, table, span):
    return kernel_call(bias_body, "bias_rows", [place, table], [], [shaped(f32, 8, span)], us=1)[0]


def project(place, tokens, segment_ids, gain, w_query, w_key, w_value):
    tok, width = tokens.shape
    span = -(-(3 * width // groups + 1) // 128) * 128
    return kernel_call(
        project_body,
        "project",
        [place],
        [tokens, segment_ids, gain, w_query, w_key, w_value],
        [shaped(bf16, tok, span)] * 4 + [shaped(bf16, tok, width)],
        scratch=[pltpu.VMEM((3, tok, width), bf16)],
        staged=(0, 1, 3, 4, 5),
        mebibytes=10,
        us=4,
    )


def forward_body(
    smem, get, outs, weight_scr, normed_scr, kv_scr, segk, strip, s_scr, p_scr, sems, *, blocks, chunk
):
    (place,) = smem
    ctx = outs[0:4]
    q_ref, k_ref, v_ref, o_ref, normed_ref, p_hbm = outs[4:10]
    group, core, s_own = place[0], place[1], place[2]
    tok = 128
    head_size = 64
    s_count = blocks // 8
    width = normed_scr.shape[1]
    local = q_ref.shape[1]
    seq = blocks * tok
    chunks = seq // chunk
    window, late = group_window(group, local)
    for i in range(3):
        both = get(10 + i)[:, pl.ds(window, -(-local // 128) * 128)]
        weight_scr[:, i * local : (i + 1) * local] = jnp.where(
            late, both[:, both.shape[1] - local :], both[:, :local]
        )
    gain = get(9)[...]

    def block_of(d, e, k):
        return (((group ^ d) * s_count + (s_own ^ e)) * 2) + (core if k == 0 else 1 - core)

    def load_chunk(e):
        for k in range(2):
            for d in range(4):
                raw = get(k * 4 + d)
                values = raw[e, :tok, :].astype(f32)
                slot = k * 4 + d
                normed_scr[slot * tok : (slot + 1) * tok, :] = (
                    values * rms_scale(values) * gain
                ).astype(bf16)
                start = pl.multiple_of(block_of(d, e, k) * tok, tok)
                segk[0:1, pl.ds(start, tok)] = raw[e, tok : tok + 1, :tok].astype(f32)
        kv_scr[...] = dot(normed_scr[...], weight_scr[:, local:], 1, 0).astype(bf16)
        for k in range(2):
            for d in range(4):
                slot = k * 4 + d
                start = pl.multiple_of(block_of(d, e, k) * tok, tok)
                rows = kv_scr[slot * tok : (slot + 1) * tok, :]
                k_ref[pl.ds(start, tok), :] = rows[:, :local]
                v_ref[pl.ds(start, tok), :] = rows[:, local:]

    load_chunk(0)
    normed_ref[...] = normed_scr[: 4 * tok, :]
    q_ref[...] = dot(normed_scr[: 4 * tok, :], weight_scr[:, :local], 1, 0).astype(bf16)
    if s_count > 1:

        @pl.loop(1, s_count)
        def _(e):
            load_chunk(e)

    def p_copy(slot, h, d):
        return pltpu.make_async_copy(
            p_scr.at[slot], p_hbm.at[h, :, pl.ds(d * tok, tok), :], sems.at[slot]
        )

    heads = local // head_size
    rows_at_once = 32
    pending = {}
    span = 4 * tok
    for h in range(heads):
        cols = slice(h * head_size, (h + 1) * head_size)
        bias_row = get(8)[h : h + 1, :]
        spread = jnp.broadcast_to(bias_row, (tok, span))
        near = pltpu.roll(spread, 0, 1, stride=1, stride_axis=0)
        strip[:, tok * (blocks - 2) : tok * (blocks + 1)] = near[:, tok : 4 * tok]
        strip[:, : tok * (blocks - 2)] = jnp.broadcast_to(
            bias_row[:, :1], (tok, tok * (blocks - 2))
        )
        strip[:, tok * (blocks + 1) :] = jnp.broadcast_to(
            bias_row[:, span - 1 :], (tok, tok * (blocks - 2))
        )
        for d in range(4):
            query_block = block_of(d, 0, 0)
            strip_base = tok * (blocks - 1) - query_block * tok
            seg_row = get(d)[0, tok : tok + 1, :tok].astype(f32)
            seg_col = jnp.transpose(jnp.broadcast_to(seg_row, (tok, tok)))[:, :1]
            slot = (h * 4 + d) % 2
            if slot in pending:
                pending.pop(slot).wait()
            queries = q_ref[d * tok : (d + 1) * tok, cols]
            if chunks == 1:
                s_scr[slot] = dot(queries, k_ref[:, cols], 1, 1)
                for r in range(0, tok, rows_at_once):
                    rows = slice(r, r + rows_at_once)
                    bias = strip[rows, pl.ds(pl.multiple_of(strip_base, tok), seq)]
                    scores = s_scr[slot, rows, :] + bias
                    scores = jnp.where(seg_col[rows] == segk[0:1, :], scores, masked_score)
                    top = jnp.max(scores, axis=1, keepdims=True)
                    exps = jnp.exp(scores - top)
                    total = jnp.sum(exps, axis=1, keepdims=True)
                    p_scr[slot, 0, rows, :] = (exps * (1.0 / total)).astype(bf16)
                weighted = jnp.dot(
                    p_scr[slot, 0], v_ref[:, cols], preferred_element_type=f32
                )
            else:
                def score_chunk(i, top):
                    start = pl.multiple_of(i * chunk, chunk)
                    scores = dot(queries, k_ref[pl.ds(start, chunk), cols], 1, 1)
                    base = pl.multiple_of(strip_base + start, tok)
                    scores = scores + strip[:, pl.ds(base, chunk)]
                    same = seg_col == segk[0:1, pl.ds(start, chunk)]
                    scores = jnp.where(same, scores, masked_score)
                    s_scr[0, :, pl.ds(start, chunk)] = scores
                    return jnp.maximum(top, jnp.max(scores, axis=1, keepdims=True))

                top = lax.fori_loop(
                    0, chunks, score_chunk, jnp.full((tok, 1), -3e38, f32)
                )

                def exp_chunk(i, total):
                    start = pl.multiple_of(i * chunk, chunk)
                    exps = jnp.exp(s_scr[0, :, pl.ds(start, chunk)] - top)
                    s_scr[0, :, pl.ds(start, chunk)] = exps
                    return total + jnp.sum(exps, axis=1, keepdims=True)

                total = lax.fori_loop(0, chunks, exp_chunk, jnp.zeros((tok, 1), f32))
                inverse = 1.0 / total

                def weigh_chunk(i, weighted):
                    start = pl.multiple_of(i * chunk, chunk)
                    low = (s_scr[0, :, pl.ds(start, chunk)] * inverse).astype(bf16)
                    p_scr[slot, i] = low
                    return weighted + jnp.dot(
                        low, v_ref[pl.ds(start, chunk), cols], preferred_element_type=f32
                    )

                weighted = lax.fori_loop(
                    0, chunks, weigh_chunk, jnp.zeros((tok, head_size), f32)
                )
            copy = p_copy(slot, h, d)
            copy.start()
            pending[slot] = copy
            o_ref[d * tok : (d + 1) * tok, cols] = weighted
            ctx[d][:, cols] = weighted.astype(bf16)
    for copy in pending.values():
        copy.wait()


def attention_forward(place, own, other, bias, gain, w_query, w_key, w_value):
    s_count, rows, width = own[0].shape
    tok = rows - 16
    local = width // groups
    blocks = 8 * s_count
    seq = blocks * tok
    chunk = min(seq, 1024)
    shapes = (
        [shaped(bf16, tok, local)] * 4
        + [shaped(bf16, 4 * tok, local)]
        + [shaped(bf16, seq, local)] * 2
        + [shaped(f32, 4 * tok, local), shaped(bf16, 4 * tok, width)]
        + [shaped(bf16, local // 64, seq // chunk, 4 * tok, chunk)]
    )
    return kernel_call(
        functools.partial(forward_body, blocks=blocks, chunk=chunk),
        "attention_forward",
        [place],
        [*own, *other, bias, gain, w_query, w_key, w_value],
        shapes,
        scratch=[
            pltpu.VMEM((width, 3 * local), bf16),
            pltpu.VMEM((8 * tok, width), bf16),
            pltpu.VMEM((8 * tok, 2 * local), bf16),
            pltpu.VMEM((8, seq), f32),
            pltpu.VMEM((tok, (2 * blocks - 1) * tok), f32),
            pltpu.VMEM((2 if seq == chunk else 1, tok, seq), f32),
            pltpu.VMEM((2, seq // chunk, tok, chunk), bf16),
            pltpu.SemaphoreType.DMA((2,)),
        ],
        in_hbm=(("out", 9),),
        staged=tuple(range(8)) if s_count == 1 else (),
        mebibytes=12 if s_count == 1 else 60,
        us=25,
    )


def backward_body(
    smem, get, outs, p_scr, ds_scr, dctx_scr, strip, dq_scr, kv_scr, rows_scr, sems, *, blocks, chunk
):
    (place,) = smem
    p_hbm = get(8)
    dq = outs[0:4]
    keep_ref, send_ref, table_ref = outs[4:7]
    group, core, s_own = place[0], place[1], place[2]
    tok = 128
    head_size = 64
    seq = blocks * tok
    chunks = seq // chunk
    s_count = blocks // 8

    def p_copy(h, i, slot):
        return pltpu.make_async_copy(p_hbm.at[h, i], p_scr.at[slot], sems.at[slot])

    p_copy(0, 0, 0).start()
    for d in range(4):
        dctx_scr[d * tok : (d + 1) * tok, :] = get(d)[...]
    q_ref, k_ref, v_ref, o_ref = get(4), get(5), get(6), get(7)
    heads = q_ref.shape[1] // head_size
    rows_scr[...] = jnp.zeros_like(rows_scr)
    rows_at_once = 32
    for h in range(heads):
        cols = slice(h * head_size, (h + 1) * head_size)
        strip[...] = jnp.zeros_like(strip)
        out_grad = dctx_scr[:, cols]
        delta = jnp.sum(out_grad.astype(f32) * o_ref[:, cols], axis=1, keepdims=True)

        def run_chunk(i, h=h, cols=cols, out_grad=out_grad, delta=delta):
            start = pl.multiple_of(i * chunk, chunk)
            slot = (h * chunks + i) % 2
            following = h * chunks + i + 1

            @pl.when(following < heads * chunks)
            def _():
                p_copy(following // chunks, following % chunks, 1 - slot).start()

            p_copy(h, i, slot).wait()
            keys = k_ref[pl.ds(start, chunk), cols]
            values = v_ref[pl.ds(start, chunk), cols]
            for d in range(4):
                query_block = ((group ^ d) * s_count + s_own) * 2 + core
                base = pl.multiple_of(tok * (blocks - 1) - query_block * tok + start, tok)
                prob_grad = dot(out_grad[d * tok : (d + 1) * tok], values, 1, 1)
                for r in range(0, tok, rows_at_once):
                    rows = slice(d * tok + r, d * tok + r + rows_at_once)
                    here = prob_grad[r : r + rows_at_once] - delta[rows]
                    low = (p_scr[slot, rows, :].astype(f32) * here).astype(bf16)
                    ds_scr[rows, :] = low
                    strip[r : r + rows_at_once, pl.ds(base, chunk)] += low.astype(f32)
            scores_grad = ds_scr[...]
            part = jnp.dot(scores_grad, keys, preferred_element_type=f32)
            if chunks == 1:
                dq_scr[:, cols] = part
            else:
                dq_scr[:, cols] += part
            queries = q_ref[:, cols]
            kv_scr[0, pl.ds(start, chunk), :] = dot(scores_grad, queries, 0, 0).astype(bf16)
            kv_scr[1, pl.ds(start, chunk), :] = dot(p_scr[slot], out_grad, 0, 0).astype(bf16)

        if chunks == 1:
            run_chunk(0)
        else:
            dq_scr[:, cols] = jnp.zeros((4 * tok, head_size), f32)
            pl.loop(0, chunks)(run_chunk)

        def place_rows(e, h=h, cols=cols):
            for d in range(4):
                for k, target in ((0, keep_ref), (1, send_ref)):
                    block = ((group ^ d) * s_count + (s_own ^ e)) * 2 + (core if k == 0 else 1 - core)
                    start = pl.multiple_of(block * tok, tok)
                    width = heads * head_size
                    target[e, d, :, cols] = kv_scr[0, pl.ds(start, tok), :]
                    shifted = slice(width + h * head_size, width + (h + 1) * head_size)
                    target[e, d, :, shifted] = kv_scr[1, pl.ds(start, tok), :]

        if s_count == 1:
            place_rows(0)
        else:
            pl.loop(0, s_count)(place_rows)
        near = strip[:, tok * (blocks - 2) : tok * (blocks + 1)]
        left = jnp.zeros((1, tok), f32)
        right = jnp.zeros((1, tok), f32)
        for t in range(blocks - 2):
            left = left + jnp.sum(strip[:, t * tok : (t + 1) * tok], axis=0, keepdims=True)
            far = (blocks + 1 + t) * tok
            right = right + jnp.sum(strip[:, far : far + tok], axis=0, keepdims=True)
        rows_scr[h : h + 1, :] = jnp.concatenate([left, jnp.zeros((1, 2 * tok), f32), right], axis=1)
        spread = jnp.concatenate([jnp.zeros((tok, tok), f32), near], axis=1)
        skewed = spread[:8]
        for j in range(1, tok // 8):
            skewed = skewed + pltpu.roll(spread[8 * j : 8 * j + 8], 4 * tok - 8 * j, 1)
        row = lax.broadcasted_iota(jnp.int32, skewed.shape, 0)
        for step in (1, 2, 4):
            moved = pltpu.roll(skewed, 4 * tok - step, 1)
            skewed = jnp.where((row & step) != 0, moved, skewed)
        rows_scr[h : h + 1, :] += jnp.sum(skewed, axis=0, keepdims=True)
    for d in range(4):
        dq[d][...] = dq_scr[d * tok : (d + 1) * tok, :].astype(bf16)
    span = 4 * tok
    bucket_count = 2 * (len(cutoffs) + 1)
    buckets = bucket_row(span, bucket_count // 2)
    sums = rows_scr[...]
    lane = lax.broadcasted_iota(jnp.int32, (8, tok), 1)
    table = jnp.zeros((8, tok), f32)
    for b in range(bucket_count):
        picked = jnp.where(buckets == b, sums, 0.0)
        table = jnp.where(lane == b, jnp.sum(picked, axis=1, keepdims=True), table)
    table_ref[...] = table


def attention_backward(place, dctx, q, k, v, o, p):
    tok, local = dctx[0].shape
    seq = k.shape[0]
    blocks = seq // tok
    s_count = blocks // 8
    chunk = p.shape[3]
    shapes = (
        [shaped(bf16, tok, local)] * 4
        + [shaped(bf16, s_count, 4, tok, 2 * local)] * 2
        + [shaped(f32, 8, tok)]
    )
    return kernel_call(
        functools.partial(backward_body, blocks=blocks, chunk=chunk),
        "attention_backward",
        [place],
        [*dctx, q, k, v, o, p],
        shapes,
        scratch=[
            pltpu.VMEM((2, 4 * tok, chunk), bf16),
            pltpu.VMEM((4 * tok, chunk), bf16),
            pltpu.VMEM((4 * tok, local), bf16),
            pltpu.VMEM((tok, (2 * blocks - 1) * tok), f32),
            pltpu.VMEM((4 * tok, local), f32),
            pltpu.VMEM((2, seq, 64), bf16),
            pltpu.VMEM((8, 4 * tok), f32),
            pltpu.SemaphoreType.DMA((2,)),
        ],
        in_hbm=(8,),
        mebibytes=11 if s_count == 1 else 60,
        us=20,
    )


def ffn_forward_body(smem, get, outs):
    (place,) = smem
    middle_ref, left_ref, act_ref, slope_ref = outs
    count = 4
    w_out, w_gate, w_up = get(6), get(7), get(8)
    group = place[0]
    tok, width = middle_ref.shape
    local = width // groups
    total = get(4)[...].astype(f32)
    for d in range(4):
        start = pl.multiple_of((group ^ d) * local, local)
        total = total + dot(get(d)[...], w_out[pl.ds(start, local), :], 1, 0)
    middle_ref[...] = total
    normed = (total * rms_scale(total) * get(5)[...]).astype(bf16)
    left_ref[:, :width] = normed
    step = w_gate.shape[1] // count
    for i in range(count):
        cols = slice(i * step, (i + 1) * step)
        gate = dot(normed, w_gate[:, cols], 1, 0)
        up = dot(normed, w_up[:, cols], 1, 0)
        root = 0.7978845608028654
        square = gate * gate
        bend = jnp.tanh(root * (gate + 0.044715 * (gate * square)))
        act = 0.5 * gate * (1.0 + bend)
        slope = 0.5 * (1.0 + bend) + 0.5 * gate * (1.0 - bend * bend) * (
            root * (1.0 + 3.0 * 0.044715 * square)
        )
        act_ref[:, cols] = act
        slope_ref[:, cols] = up * slope
        left_ref[:, width + i * step : width + (i + 1) * step] = (act * up).astype(bf16)


def ffn_forward(place, ctx, tokens, gain, w_out, w_gate, w_up):
    tok, width = tokens.shape
    ff = w_gate.shape[1]
    return kernel_call(
        ffn_forward_body,
        "ffn_forward",
        [place],
        [*ctx, tokens, gain, w_out, w_gate, w_up],
        [
            shaped(f32, tok, width),
            shaped(bf16, tok, width + ff),
            shaped(f32, tok, ff),
            shaped(f32, tok, ff),
        ],
        us=14,
    )


def ffn_backward_body(smem, get, outs, gate_scr, up_scr, attn_scr):
    (place,) = smem
    out_ref, grad_ref, gain_grad_ref = outs[0:3]
    dctx = outs[3:7]
    mine_ref, near_ref, far_gate_ref, far_up_ref = outs[7:11]
    count = 4
    w_down, w_gate, w_up, w_out = get(10), get(11), get(12), get(13)
    group, core, across = place[0], place[1], place[4]
    tok, width = grad_ref.shape
    ff = w_gate.shape[1]
    local = width // groups
    quarter = ff // 4
    cot = get(0)[...]
    step = ff // count
    act_ref, slope_ref = get(3), get(4)
    normed_grad = jnp.zeros((tok, width), f32)
    for i in range(count):
        cols = slice(i * step, (i + 1) * step)
        hidden_grad = dot(cot, w_down[cols, :], 1, 1)
        gate = (hidden_grad * slope_ref[:, cols]).astype(bf16)
        up = (hidden_grad * act_ref[:, cols]).astype(bf16)
        gate_scr[:, cols] = gate
        up_scr[:, cols] = up
        normed_grad = (
            normed_grad + dot(gate, w_gate[:, cols], 1, 1) + dot(up, w_up[:, cols], 1, 1)
        )
    def quarter_of(ref, x, c):
        return ref[:, pl.ds(pl.multiple_of((x * 2 + c) * quarter, quarter), quarter)]

    mine_ref[:, :quarter] = quarter_of(gate_scr, across, core)
    mine_ref[:, quarter : 2 * quarter] = quarter_of(up_scr, across, core)
    near_ref[:, :quarter] = quarter_of(gate_scr, across, 1 - core)
    near_ref[:, quarter : 2 * quarter] = quarter_of(up_scr, across, 1 - core)
    for ref, source in ((far_gate_ref, gate_scr), (far_up_ref, up_scr)):
        ref[:, :quarter] = quarter_of(source, 1 - across, core)
        ref[:, quarter : 2 * quarter] = quarter_of(source, 1 - across, 1 - core)
    middle = get(1)[...]
    scale = rms_scale(middle)
    unit = middle * scale
    scaled = normed_grad * get(5)[...]
    gain_grad_ref[...] = jnp.sum(normed_grad * unit, axis=0, keepdims=True)
    middle_grad = cot.astype(f32) + scale * (
        scaled - unit * jnp.mean(unit * scaled, axis=1, keepdims=True)
    )
    grad_ref[...] = middle_grad
    attn = middle_grad.astype(bf16)
    attn_scr[...] = attn
    for d in range(4):
        start = pl.multiple_of((group ^ d) * local, local)
        dctx[d][...] = dot(attn, w_out[pl.ds(start, local), :], 1, 1).astype(bf16)
    at = 2 * quarter
    for ref, which in ((mine_ref, across), (near_ref, across), (far_up_ref, 1 - across)):
        for d in range(4):
            ref[:, at + d * local : at + (d + 1) * local] = get(6 + d)[...]
        start = pl.multiple_of(which * (width // 2), width // 2)
        ref[:, at + width :] = attn_scr[:, pl.ds(start, width // 2)]
    out_ref[...] = (middle + dot(get(2)[:, width:], w_down[...], 1, 0)).astype(bf16)


def ffn_backward(place, cot, middle, hidden, act, slope, gain, ctx, w_down, w_gate, w_up, w_out):
    tok, width = cot.shape
    ff = w_gate.shape[1]
    local = width // groups
    return kernel_call(
        ffn_backward_body,
        "ffn_backward",
        [place],
        [cot, middle, hidden, act, slope, gain, *ctx, w_down, w_gate, w_up, w_out],
        [shaped(bf16, tok, width), shaped(f32, tok, width), shaped(f32, 1, width)]
        + [shaped(bf16, tok, local)] * 4
        + [shaped(bf16, tok, ff // 2 + width + width // 2)] * 2
        + [shaped(bf16, tok, ff // 2), shaped(bf16, tok, ff // 2 + width + width // 2)],
        scratch=[
            pltpu.VMEM((tok, ff), bf16),
            pltpu.VMEM((tok, ff), bf16),
            pltpu.VMEM((tok, width), bf16),
        ],
        mebibytes=6,
        us=6,
    )


def split_rows(total, wide, odd, kept_ref, sent_ref, cols):
    block = total.shape[0] // wide
    for i in range(wide // 2):
        even_rows = total[2 * i * block : (2 * i + 1) * block, :]
        odd_rows = total[(2 * i + 1) * block : (2 * i + 2) * block, :]
        kept_ref[i, :, cols] = jnp.where(odd, odd_rows, even_rows)
        sent_ref[i, :, cols] = jnp.where(odd, even_rows, odd_rows).astype(bf16)


def down_grad_body(smem, get, outs, left_scr, right_scr, total_scr, *, wide):
    (place,) = smem
    kept_ref, sent_ref = outs
    core, odd = place[1], place[3] == 1
    tok, half = get(4).shape
    local = half // 2
    for i in range(4):
        rows = slice(i * tok, (i + 1) * tok)
        left_scr[rows, :] = get(i)[:, 2 * half :]
        both = get(4 + i)[...]
        right_scr[rows, :] = jnp.where(core == 0, both[:, :local], both[:, local:])
    total_scr[...] = dot(left_scr[...], right_scr[...], 0, 0)
    split_rows(total_scr, wide, odd, kept_ref, sent_ref, slice(None))


def down_grad(place, lefts, rights, wide):
    tok, half = rights[0].shape
    ff = lefts[0].shape[1] - 2 * half
    shape = (wide // 2, ff // wide, half // 2)
    return kernel_call(
        functools.partial(down_grad_body, wide=wide),
        "down_grad",
        [place],
        [*lefts, *rights],
        [shaped(f32, *shape), shaped(bf16, *shape)],
        scratch=[
            pltpu.VMEM((4 * tok, ff), bf16),
            pltpu.VMEM((4 * tok, half // 2), bf16),
            pltpu.VMEM((ff, half // 2), f32),
        ],
        mebibytes=6,
        us=8,
    )


def gate_grad_body(smem, get, outs, left_scr, right_scr, total_scr, *, wide):
    (place,) = smem
    tok, width = left_scr.shape[0] // 4, left_scr.shape[1]
    quarter = right_scr.shape[1]
    for i in range(4):
        rows = slice(i * tok, (i + 1) * tok)
        left_scr[rows, :] = get(i)[:, :width]
        at = quarter if i == 3 else 0
        right_scr[rows, :] = get(4 + i)[:, at : at + quarter]
    total_scr[...] = dot(left_scr[...], right_scr[...], 0, 0)
    split_rows(total_scr, wide, place[3] == 1, *outs, slice(None))


def gate_grad(place, lefts, rights, width, wide):
    tok = lefts[0].shape[0]
    quarter = rights[2].shape[1] // 2
    shape = (wide // 2, width // wide, quarter)
    return kernel_call(
        functools.partial(gate_grad_body, wide=wide),
        "gate_grad",
        [place],
        [*lefts, *rights],
        [shaped(f32, *shape), shaped(bf16, *shape)],
        scratch=[
            pltpu.VMEM((4 * tok, width), bf16),
            pltpu.VMEM((4 * tok, quarter), bf16),
            pltpu.VMEM((width, quarter), f32),
        ],
        mebibytes=5,
        us=2,
    )


def up_grad_body(
    smem, get, outs, left_scr, right_scr, ctx_scr, attn_scr, total_scr, out_scr, *, wide
):
    (place,) = smem
    group, core, odd = place[0], place[1], place[3] == 1
    tok, width = left_scr.shape[0] // 4, left_scr.shape[1]
    local = width // groups
    quarter = right_scr.shape[1]
    for i in range(4):
        rows = slice(i * tok, (i + 1) * tok)
        left_scr[rows, :] = get(i)[:, :width]
        at = 0 if i == 2 else quarter
        right_scr[rows, :] = get(4 + i)[:, at : at + quarter]
        ctx_scr[rows, :] = get(4 + i)[:, 2 * quarter : 2 * quarter + width]
        both = get(4 + i)[:, 2 * quarter + width :]
        attn_scr[rows, :] = jnp.where(core == 0, both[:, :local], both[:, local:])
    total_scr[...] = dot(left_scr[...], right_scr[...], 0, 0)
    split_rows(total_scr, wide, odd, *outs, slice(0, quarter))
    turned = dot(ctx_scr[...], attn_scr[...], 0, 0)
    for d in range(4):
        start = pl.multiple_of((group ^ d) * local, local)
        out_scr[pl.ds(start, local), :] = turned[d * local : (d + 1) * local]
    split_rows(out_scr, wide, odd, *outs, slice(quarter, quarter + local))


def up_grad(place, lefts, rights, width, wide):
    tok = lefts[0].shape[0]
    quarter = (rights[0].shape[1] - width - width // 2) // 2
    local = width // groups
    shape = (wide // 2, width // wide, quarter + local)
    return kernel_call(
        functools.partial(up_grad_body, wide=wide),
        "up_grad",
        [place],
        [*lefts, *rights],
        [shaped(f32, *shape), shaped(bf16, *shape)],
        scratch=[
            pltpu.VMEM((4 * tok, width), bf16),
            pltpu.VMEM((4 * tok, quarter), bf16),
            pltpu.VMEM((4 * tok, width), bf16),
            pltpu.VMEM((4 * tok, local), bf16),
            pltpu.VMEM((width, quarter), f32),
            pltpu.VMEM((width, local), f32),
        ],
        mebibytes=8,
        us=3,
    )


def collect_body(smem, get, outs):
    local = outs[0].shape[1] // 3
    for d in range(4):
        outs[d][:, :local] = get(d)[...]
    for d in range(4):
        total = get(4)[d].astype(f32) + get(5)[d].astype(f32)
        outs[d][:, local:] = total.astype(bf16)


def collect(dq, kept, received):
    tok, local = dq[0].shape
    return kernel_call(
        collect_body,
        "collect",
        [],
        [*dq, kept, received],
        [shaped(bf16, tok, 3 * local)] * 4,
        us=2,
    )


def qkv_grad_body(smem, get, outs, grad_scr, total_scr):
    (place,) = smem
    kept_ref, sent_ref, small_ref = outs
    group, core = place[0], place[1]
    width, span = total_scr.shape
    local = span // 3
    tok = grad_scr.shape[0] // 4
    for d in range(4):
        grad_scr[d * tok : (d + 1) * tok, :] = get(d)[...]
    total_scr[...] = dot(get(4)[...], grad_scr[...], 0, 0)
    quarter = width // 4
    for i in range(2):
        for ref, which in ((sent_ref, 1 - core), (kept_ref, core)):
            start = pl.multiple_of((2 * i + which) * quarter, quarter)
            ref[i] = total_scr[pl.ds(start, quarter), :].astype(ref.dtype)
    window, late = group_window(group, local)
    ones = jnp.ones((8, local), bf16)
    gain_grad = jnp.zeros((8, width), f32)
    for i in range(3):
        both = get(8 + i)[:, pl.ds(window, -(-local // 128) * 128)]
        weight = jnp.where(late, both[:, both.shape[1] - local :], both[:, :local])
        product = total_scr[:, i * local : (i + 1) * local] * weight.astype(f32)
        high = product.astype(bf16)
        rest = (product - high.astype(f32)).astype(bf16)
        gain_grad = gain_grad + dot(ones, high, 1, 1) + dot(ones, rest, 1, 1)
    gain_grad = gain_grad[0:1] / get(5)[...]
    ffn_gain = get(6)[...]
    lanes = 128
    rows = width // lanes
    for i in range(rows):
        small_ref[i : i + 1, :] = gain_grad[:, i * lanes : (i + 1) * lanes]
        small_ref[rows + i : rows + i + 1, :] = ffn_gain[:, i * lanes : (i + 1) * lanes]
    heads = (small_ref.shape[0] - 2 * rows) // groups
    table = get(7)[:heads, :]
    for i in range(groups):
        at = 2 * rows + i * heads
        small_ref[at : at + heads, :] = jnp.where(group == i, table, 0.0)


def qkv_grad(place, grads, normed, gain, gain_grad, table, head_count, w_query, w_key, w_value):
    rows, width = normed.shape
    span = grads[0].shape[1]
    return kernel_call(
        qkv_grad_body,
        "qkv_grad",
        [place],
        [*grads, normed, gain, gain_grad, table, w_query, w_key, w_value],
        [
            shaped(f32, 2, width // 4, span),
            shaped(bf16, 2, width // 4, span),
            shaped(f32, 2 * width // 128 + head_count, 128),
        ],
        scratch=[pltpu.VMEM((rows, span), bf16), pltpu.VMEM((width, span), f32)],
        mebibytes=7,
        us=4,
    )


def input_grad_body(smem, get, outs):
    (place,) = smem
    group = place[0]
    weights = [get(7 + i) for i in range(3)]
    local = get(0).shape[1] // 3
    window = -(-local // 128) * 128
    tok = get(0).shape[0]
    spare = jnp.zeros((tok, window - local), bf16)
    normed_grad = None
    for d in range(4):
        start, late = group_window(group ^ d, local)
        grads = get(d)[...]
        for i in range(3):
            part = grads[:, i * local : (i + 1) * local]
            part = jnp.where(
                late,
                jnp.concatenate([spare, part], axis=1),
                jnp.concatenate([part, spare], axis=1),
            )
            product = dot(part, weights[i][:, pl.ds(start, window)], 1, 1)
            normed_grad = product if normed_grad is None else normed_grad + product
    values = get(4)[...].astype(f32)
    scale = rms_scale(values)
    unit = values * scale
    scaled = normed_grad * get(5)[...]
    outs[0][...] = get(6)[...] + scale * (
        scaled - unit * jnp.mean(unit * scaled, axis=1, keepdims=True)
    )


def final_input_grad(place, grads, tokens, gain, middle_grad, w_query, w_key, w_value):
    return kernel_call(
        input_grad_body,
        "input_grad",
        [place],
        [*grads, tokens, gain, middle_grad, w_query, w_key, w_value],
        [shaped(f32, *tokens.shape)],
        staged=(0, 1, 2, 3, 4, 6),
        mebibytes=6,
        us=4,
    )[0]


def add_split_body(smem, get, outs, *, bit, splits):
    (place,) = smem
    kept, received = get(0), get(1)
    if kept.shape[0] == 1:
        total = kept[0].astype(f32) + received[0].astype(f32)
        at = 0
        for i, span in enumerate(splits):
            outs[i][...] = total[:, at : at + span]
            at += span
        return
    odd = ((place[5] >> bit) & 1) == 1
    for i in range(kept.shape[0] // 2):
        even_rows = kept[2 * i].astype(f32) + received[2 * i].astype(f32)
        odd_rows = kept[2 * i + 1].astype(f32) + received[2 * i + 1].astype(f32)
        outs[1][i] = jnp.where(odd, even_rows, odd_rows).astype(bf16)
        outs[0][i] = jnp.where(odd, odd_rows, even_rows)


def wide_sum(layout, place, kept, sent, bit, splits, name, us, first=()):
    received = layout.wide_bit(sent, bit)
    kept = after(kept, first)
    remaining, block, columns = kept.shape
    if remaining == 1:
        outputs = [shaped(f32, block, span) for span in splits]
    else:
        shape = (remaining // 2, block, columns)
        outputs = [shaped(f32, *shape), shaped(bf16, *shape)]
    return kernel_call(
        functools.partial(add_split_body, bit=bit + 1, splits=splits),
        f"{name}_sum",
        [place],
        [kept, received],
        outputs,
        us=us,
    )


def after(values, done):
    return lax.optimization_barrier((values, done))[0]


def halved(block, axis, keep):
    return (
        lax.dynamic_index_in_dim(block, keep, axis, keepdims=False),
        lax.dynamic_index_in_dim(block, 1 - keep, axis, keepdims=False),
    )


def on_device(
    inputs,
    segment_ids,
    gain_attn,
    w_query,
    w_key,
    w_value,
    w_out,
    gain_ffn,
    w_gate,
    w_up,
    w_down,
    bias_table,
    cotangent,
):
    layout = Layout(lax.axis_size("narrow"), lax.axis_size("wide"))
    s_count = layout.s_count
    tokens = inputs[0]
    out_grad = cotangent[0]
    tok, width = tokens.shape
    local = width // groups
    ff = w_gate.shape[1]
    bucket_count, head_count = bias_table.shape
    narrow = lax.axis_index("narrow")
    wide = lax.axis_index("wide")
    core = narrow % 2
    across = narrow // 2
    group = wide // (2 * s_count)
    s_own = (wide // 2) % s_count
    y_own = wide % 2
    place = jnp.stack([group, core, s_own, y_own, across, wide]).astype(jnp.int32)
    gain_attn = gain_attn[None]
    gain_ffn = gain_ffn[None]

    packet = packed(tokens, segment_ids)
    own = [layout.turned(packet, d)[None] for d in range(3)]
    own.append(layout.wide_bit(own[2], layout.wide.bit_length() - 3))
    for d in range(4):
        size = 1
        while size < s_count:
            own[d] = jnp.concatenate([own[d], layout.wide_bit(own[d], size.bit_length())], axis=0)
            size *= 2
    bias = bias_rows(place, bias_table, 4 * tok)
    own = after(own, bias)
    other = [layout.core(block) for block in own]

    def half_cols(block, which):
        return lax.dynamic_slice_in_dim(block, which * (block.shape[1] // 2), block.shape[1] // 2, 1)

    cot_own = half_cols(out_grad, across)
    cot_across = layout.across(half_cols(out_grad, 1 - across))
    cot_parts = [cot_own, layout.core(cot_own), cot_across, layout.core(cot_across)]

    outs = attention_forward(
        place, own, other, bias, gain_attn, w_query, w_key, w_value
    )
    ctx_parts = outs[:4]
    q_own, k_all, v_all, o_own, normed_own, probs = outs[4:]
    ctx = [layout.turned(ctx_parts[d], d) for d in range(4)]
    ctx = after(ctx, cot_parts)

    middle, left, act, slope = ffn_forward(place, ctx, tokens, gain_ffn, w_out, w_gate, w_up)
    left_across = layout.across(left)
    left_core = layout.core(left)
    back = ffn_backward(
        place, out_grad, middle, left, act, slope, gain_ffn, ctx, w_down, w_gate, w_up, w_out
    )
    output, middle_grad, grad_gain_ffn = back[0:3]
    dctx = [layout.turned(back[3 + d], d) for d in range(4)]
    mine, near, far_gate, far_up = back[7:11]
    near = layout.core(near)
    far_gate = layout.across(far_gate)
    far_up = layout.across(far_up)
    dctx = after(dctx, left_across)

    back = attention_backward(place, dctx, q_own, k_all, v_all, o_own, probs)
    dq, kept, sent, table_rows = back[:4], back[4], back[5], back[6]
    received = layout.core(sent)
    left_across = after(left_across, sent)
    lefts = [left, left_core, left_across, layout.core(left_across)]
    down_kept, down_sent = down_grad(place, lefts, cot_parts, layout.wide)
    size = s_count
    while size > 1:
        size //= 2
        total = kept.astype(f32) + received.astype(f32)
        kept = total[:size]
        received = layout.wide_bit(total[size:].astype(bf16), size.bit_length())
    received = after(received, down_sent)
    low_grads = collect(dq, kept[0], received[0])
    returned = [layout.turned(low_grads[d], d) for d in range(4)]

    far_gate = after(far_gate, down_sent)
    far_gate_both = layout.core(far_gate)
    lefts = after(lefts, low_grads)
    gate_kept, gate_sent = gate_grad(
        place, lefts, [mine, near, far_gate, far_gate_both], width, layout.wide
    )
    normed_own = after(normed_own, gate_sent)

    qkv_kept, qkv_sent, small = qkv_grad(
        place,
        low_grads,
        normed_own,
        gain_attn,
        grad_gain_ffn,
        table_rows,
        head_count,
        w_query,
        w_key,
        w_value,
    )
    far_up = after(far_up, qkv_sent)
    far_up_both = layout.core(far_up)
    up_kept, up_sent = up_grad(place, lefts, [mine, near, far_up, far_up_both], width, layout.wide)

    rows = width // layout.wide
    part = qkv_kept + layout.core(qkv_sent).astype(f32)
    part = part.reshape(2, s_count, 2, rows, 3 * local)
    kept, sent = halved(part, 0, across)
    part = kept + layout.across(sent.astype(bf16)).astype(f32)
    kept, sent = halved(part, 1, y_own)
    part = kept + layout.wide_bit(sent.astype(bf16), 0).astype(f32)
    size = s_count
    bit = 1
    while size > 1:
        size //= 2
        part = part.reshape(size, 2, rows, 3 * local)
        kept, sent = halved(part, 1, (s_own >> (bit - 1)) & 1)
        part = kept + layout.wide_bit(sent.astype(bf16), bit).astype(f32)
        bit += 1
    part = part.reshape(rows, 3 * local).astype(bf16)
    final_qkv = layout.send(part, lambda x, c, g, s, y: (g // 2, g % 2, x * 2 + c, s, y)).astype(f32)

    input_grad = final_input_grad(
        place, returned, tokens, gain_attn, middle_grad, w_query, w_key, w_value
    )
    quarter_ff = ff // layout.narrow
    bits = layout.wide.bit_length() - 1
    down, gate, up = (down_kept, down_sent), (gate_kept, gate_sent), (up_kept, up_sent)
    for bit in range(bits):
        down = wide_sum(layout, place, *down, bit, (local,), "down", 6)
        gate = wide_sum(layout, place, *gate, bit, (quarter_ff,), "gate", 8)
        first = returned if bit == 0 else (input_grad, down, gate) if bit == bits - 1 else ()
        up = wide_sum(layout, place, *up, bit, (quarter_ff, local), "up", 12, first)
        if bit == 0:
            small = after(small, up)
    (final_down,), (final_gate,), (final_up, final_out) = down, gate, up

    for bit in range(bits):
        small = small + layout.wide_bit(small, bit)
    small = small + layout.across(small)
    small = small + layout.core(small)
    gain_rows = width // 128
    sum_gain_attn = small[:gain_rows].reshape(width)
    sum_gain_ffn = small[gain_rows : 2 * gain_rows].reshape(width)
    sum_table = small[2 * gain_rows :, :bucket_count].T

    return (
        output[None],
        input_grad[None],
        sum_gain_attn,
        final_qkv[:, :local],
        final_qkv[:, local : 2 * local],
        final_qkv[:, 2 * local :],
        final_out,
        sum_gain_ffn,
        final_gate,
        final_up,
        final_down,
        sum_table,
    )


def solution(mesh):
    tokens = P("narrow", "wide", None)
    share = P("wide", "narrow")
    return jax.shard_map(
        on_device,
        mesh=mesh,
        in_specs=(tokens, P("narrow", "wide")) + (P(),) * 10 + (tokens,),
        out_specs=(
            tokens,
            tokens,
            P(),
            share,
            share,
            share,
            share,
            P(),
            share,
            share,
            share,
            P(),
        ),
        check_vma=False,
    )
```

profile of v0, /device:TPU:2, one launch (start us, length us, event | category | flops | bytes accessed | tf_op | source)
XLA Modules:
  0.0 194.1 jit_solution(18399656106825865017)
XLA Ops:
  2.9 2.7 %collective-permute-start.2 = (bf16[144,768]{1,0:T(8,128)(2,1)}, bf16[144,768]{1,0:T(8,128)(2,1)S(1)}, u32[]{:S(2)}, u32[]{:S(2)}) collective-permute-start(bf16[144,768]{1,0:T(8,128)(2,1)} %pack.1), channel_id=1, source_target_pairs={{0,4},{1,12},{2,6},{3,14},{4,0},{5,8},{6,2},{7,10},{8,5},{9,13},{1... | collective-permute-start | bytes 663560 | tf_op jit(solution)/shard_map/ppermute | solution.py:46
  8.8 8.2 %collective-permute-done.2 = bf16[144,768]{1,0:T(8,128)(2,1)S(1)} collective-permute-done((bf16[144,768]{1,0:T(8,128)(2,1)}, bf16[144,768]{1,0:T(8,128)(2,1)S(1)}, u32[]{:S(2)}, u32[]{:S(2)}) %collective-permute-start.2) | collective-permute-done | bytes 221216 | tf_op jit(solution)/shard_map/ppermute | solution.py:46
  19.1 5.2 %collective-permute-done.3.refs_4_ = bf16[1,144,768]{2,1,0:T(8,128)(2,1)S(1)} collective-permute-done((bf16[1,144,768]{2,1,0:T(8,128)(2,1)S(1)}, bf16[1,144,768]{2,1,0:T(8,128)(2,1)S(1)}, u32[]{:S(2)}, u32[]{:S(2)}) %collective-permute-start.3) | collective-permute-done | bytes 221216 | tf_op jit(solution)/shard_map/ppermute | solution.py:46
  27.3 4.1 %collective-permute-done.13.refs_7_ = bf16[128,384]{1,0:T(8,128)(2,1)S(1)} collective-permute-done((bf16[128,384]{1,0:T(8,128)(2,1)S(1)}, bf16[128,384]{1,0:T(8,128)(2,1)S(1)}, u32[]{:S(2)}, u32[]{:S(2)}) %collective-permute-start.13) | collective-permute-done | bytes 98336 | tf_op jit(solution)/shard_map/ppermute | solution.py:46
  36.8 14.8 %attention_forward.1 = (bf16[128,192]{1,0:T(8,128)(2,1)S(1)}, bf16[128,192]{1,0:T(8,128)(2,1)S(1)}, bf16[128,192]{1,0:T(8,128)(2,1)S(1)}, bf16[128,192]{1,0:T(8,...) custom-call(s32[6]{0:T(128)S(1)} %stack.24.refs_0_, ...), custom_call_target="tpu_custom_call" | custom-call | flops 28750000128 | bytes 1024 | tf_op jit(solution)/shard_map/attention_forward/pallas_call | solution.py:111
  51.6 2.3 %collective-permute-start.10 = (bf16[128,192]{1,0:T(8,128)(2,1)S(1)}, bf16[128,192]{1,0:T(8,128)(2,1)S(1)}, u32[]{:S(2)}, u32[]{:S(2)}) collective-permute-start(bf16[128,192]{1,0:T(8,128)(2,1)S(1)} %get-tuple-element.101), channel_id=1, source_target_pairs={{0,4},{1,12},{2,6},{3,14},{4,0},{5,8},{6,2},{7,10},{8,5},{9,13},{1... | collective-permute-start | bytes 147464 | tf_op jit(solution)/shard_map/ppermute | solution.py:46
  56.6 1.7 collective-permute-done.10.refs_3_.refs_9_
  58.3 2.6 %collective-permute-done.11.refs_4_.refs_10_ = bf16[128,192]{1,0:T(8,128)(2,1)S(1)} collective-permute-done((bf16[128,192]{1,0:T(8,128)(2,1)S(1)}, bf16[128,192]{1,0:T(8,128)(2,1)S(1)}, u32[]{:S(2)}, u32[]{:S(2)}) %collective-permute-start.11) | collective-permute-done | bytes 49184 | tf_op jit(solution)/shard_map/ppermute | solution.py:46
  61.5 2.6 %ffn_forward.1 = (f32[128,768]{1,0:T(8,128)S(1)}, bf16[128,2816]{1,0:T(8,128)(2,1)S(1)}, f32[128,2048]{1,0:T(8,128)S(1)}, f32[128,2048]{1,0:T(8,128)S(1)}) custom-call(s32[6]{0:T(128)S(1)} %stack.24.refs_0_, bf16[128,192]{1,0:T(8,128)(2,1)S(1)} %collective-permute-done.8.refs_1_.refs_7_, bf16[128,192]{1,0:T(8,128)(2,1)S(1)} %collective-permute-done.9.refs_2_.refs_8_, ...), custom_call_target="tpu_custom_call" | custom-call | flops 16099999744 | bytes 1024 | tf_op jit(solution)/shard_map/ffn_forward/pallas_call | solution.py:111
  64.8 5.6 %ffn_backward.1 = (bf16[128,768]{1,0:T(8,128)(2,1)}, f32[128,768]{1,0:T(8,128)S(1)}, f32[1,768]{1,0:T(1,128)S(1)}, bf16[128,192]{1,0:T(8,128)(2,1)S(1)}, bf16[12...) custom-call(s32[6]{0:T(128)S(1)} %stack.24.refs_0_, ...), custom_call_target="tpu_custom_call" | custom-call | flops 6899999744 | bytes 1024 | tf_op jit(solution)/shard_map/ffn_backward/pallas_call | solution.py:111
  72.3 2.4 %collective-permute-start.17 = (bf16[128,192]{1,0:T(8,128)(2,1)S(1)}, bf16[128,192]{1,0:T(8,128)(2,1)S(1)}, u32[]{:S(2)}, u32[]{:S(2)}) collective-permute-start(bf16[128,192]{1,0:T(8,128)(2,1)S(1)} %get-tuple-element.114), channel_id=1, source_target_pairs={{0,4},{1,12},{2,6},{3,14},{4,0},{5,8},{6,2},{7,10},{8,5},{9,13},{1... | collective-permute-start | bytes 147464 | tf_op jit(solution)/shard_map/ppermute | solution.py:46
  76.2 4.5 %collective-permute-start.21 = (bf16[128,2816]{1,0:T(8,128)(2,1)S(1)}, bf16[128,2816]{1,0:T(8,128)(2,1)S(1)}, u32[]{:S(2)}, u32[]{:S(2)}) collective-permute-start(bf16[128,2816]{1,0:T(8,128)(2,1)S(1)} %get-tuple-element.140.refs_3_.refs_1_), channel_id=1, source_target_pairs={{0,8},{1,9},{2,10},{3,11},{4,12},{5,13},{6,14},{7,15},{8,0},{9,1},... | collective-permute-start | bytes 2162696 | tf_op jit(solution)/shard_map/ppermute | solution.py:46
  82.5 7.1 %attention_backward.1 = (bf16[128,192]{1,0:T(8,128)(2,1)S(1)}, bf16[128,192]{1,0:T(8,128)(2,1)S(1)}, bf16[128,192]{1,0:T(8,128)(2,1)S(1)}, bf16[128,192]{1,0:T(8...) custom-call(s32[6]{0:T(128)S(1)} %stack.24.refs_0_, ...), custom_call_target="tpu_custom_call" | custom-call | flops 23000000512 | bytes 1024 | tf_op jit(solution)/shard_map/attention_backward/pallas_call | solution.py:111
  89.6 3.7 %collective-permute-start.22 = (bf16[128,2816]{1,0:T(8,128)(2,1)S(1)}, bf16[128,2816]{1,0:T(8,128)(2,1)S(1)}, u32[]{:S(2)}, u32[]{:S(2)}) collective-permute-start(bf16[128,2816]{1,0:T(8,128)(2,1)S(1)} %collective-permute-done.19.refs_3_), channel_id=1, source_target_pairs={{0,8},{1,9},{2,10},{3,11},{4,12},{5,13},{6,14},{7,15},{8,0},{9,1},... | collective-permute-start | bytes 2162696 | tf_op jit(solution)/shard_map/ppermute | solution.py:46
  98.1 2.9 %collective-permute-start.23 = (bf16[128,576]{1,0:T(8,128)(2,1)}, bf16[128,576]{1,0:T(8,128)(2,1)}, u32[]{:S(2)}, u32[]{:S(2)}) collective-permute-start(bf16[128,576]{1,0:T(8,128)(2,1)} %get-tuple-element.134.refs_1_), channel_id=1, source_target_pairs={{0,0},{1,8},{2,2},{3,10},{4,4},{5,12},{6,6},{7,14},{8,1},{9,9},{10... | collective-permute-start | bytes 442376 | tf_op jit(solution)/shard_map/ppermute | solution.py:46
  101.0 2.0 %collective-permute-start.25 = (bf16[128,576]{1,0:T(8,128)(2,1)}, bf16[128,576]{1,0:T(8,128)(2,1)}, u32[]{:S(2)}, u32[]{:S(2)}) collective-permute-start(bf16[128,576]{1,0:T(8,128)(2,1)} %get-tuple-element.136.refs_3_), channel_id=1, source_target_pairs={{0,4},{1,12},{2,6},{3,14},{4,0},{5,8},{6,2},{7,10},{8,5},{9,13},{1... | collective-permute-start | bytes 442376 | tf_op jit(solution)/shard_map/ppermute | solution.py:46
  103.0 2.4 %collective-permute-start.26 = (bf16[128,576]{1,0:T(8,128)(2,1)}, bf16[128,576]{1,0:T(8,128)(2,1)}, u32[]{:S(2)}, u32[]{:S(2)}) collective-permute-start(bf16[128,576]{1,0:T(8,128)(2,1)} %get-tuple-element.137.refs_4_), channel_id=1, source_target_pairs={{0,6},{1,14},{2,4},{3,12},{4,2},{5,10},{6,0},{7,8},{8,7},{9,15},{1... | collective-permute-start | bytes 442376 | tf_op jit(solution)/shard_map/ppermute | solution.py:46
  111.5 4.6 %collective-permute-done.25.refs_3_ = bf16[128,576]{1,0:T(8,128)(2,1)} collective-permute-done((bf16[128,576]{1,0:T(8,128)(2,1)}, bf16[128,576]{1,0:T(8,128)(2,1)}, u32[]{:S(2)}, u32[]{:S(2)}) %collective-permute-start.25) | collective-permute-done | bytes 147488 | tf_op jit(solution)/shard_map/ppermute | solution.py:46
  119.2 5.2 %input_grad.1 = f32[128,768]{1,0:T(8,128)} custom-call(s32[6]{0:T(128)S(1)} %stack.24.refs_0_, bf16[128,576]{1,0:T(8,128)(2,1)} %collective-permute-done.23.refs_1_, bf16[128,576]{1,0:T(8,128)(2,1)} %collective-permute-done.24.refs_2_, bf16[128,576]{1,0:T(8,128)(2,1)} %collective-permute-done.25.refs_3_, bf16[128,576]{1,0:T(8,128)(2,1)} %collective-permute-done.26.refs_4_, ...), custom_call_target="tpu_custom_call" | custom-call | flops 4600000000 | bytes 1024 | tf_op jit(solution)/shard_map/input_grad/pallas_call | solution.py:111
  124.4 1.8 gate_grad.1
  128.2 4.0 %collective-permute-start.44 = (bf16[2,256,192]{2,1,0:T(8,128)(2,1)S(1)}, bf16[2,256,192]{2,1,0:T(8,128)(2,1)S(1)}, u32[]{:S(2)}, u32[]{:S(2)}) collective-permute-start(bf16[2,256,192]{2,1,0:T(8,128)(2,1)S(1)} %get-tuple-element.166), channel_id=1, source_target_pairs={{0,2},{1,3},{2,0},{3,1},{4,6},{5,7},{6,4},{7,5},{8,10},{9,11},{10,... | collective-permute-start | bytes 589832 | tf_op jit(solution)/shard_map/ppermute | solution.py:46
  132.1 3.3 %qkv_grad.1 = (f32[2,192,576]{2,1,0:T(8,128)S(1)}, bf16[2,192,576]{2,1,0:T(8,128)(2,1)S(1)}, f32[24,128]{1,0:T(8,128)S(1)}) custom-call(s32[6]{0:T(128)S(1)} %stack.24.refs_0_, bf16[128,576]{1,0:T(8,128)(2,1)} %get-tuple-element.134.refs_1_, bf16[128,576]{1,0:T(8,128)(2,1)} %get-tuple-element.135.refs_2_, bf16[128,576]{1,0:T(8,128)(2,1)} %get-tuple-element.136.refs_3_, ...), custom_call_target="tpu_custom_call" | custom-call | flops 4600000000 | bytes 1024 | tf_op jit(solution)/shard_map/qkv_grad/pallas_call | solution.py:111
  137.3 1.9 collective-permute-start.45
  143.2 2.1 %up_grad.1 = (f32[4,96,704]{2,1,0:T(8,128)S(1)}, bf16[4,96,704]{2,1,0:T(8,128)(2,1)S(1)}) custom-call(s32[6]{0:T(128)S(1)} %stack.24.refs_0_, bf16[128,2816]{1,0:T(8,128)(2,1)S(1)} %get-tuple-element.140.refs_3_.refs_1_, bf16[128,2816]{1,0:T(8,128)(2,1)S(1)} %copy-done.13, bf16[128,2816]{1,0:T(8,128)(2,1)S(1)} %copy-done.11, ...), custom_call_target="tpu_custom_call" | custom-call | flops 3449999872 | bytes 1024 | tf_op jit(solution)/shard_map/up_grad/pallas_call | solution.py:111
  150.0 9.6 %collective-permute-done.32.refs_2_ = bf16[4,96,704]{2,1,0:T(8,128)(2,1)S(1)} collective-permute-done((bf16[4,96,704]{2,1,0:T(8,128)(2,1)S(1)}, bf16[4,96,704]{2,1,0:T(8,128)(2,1)S(1)}, u32[]{:S(2)}, u32[]{:S(2)}) %collective-permute-start.32) | collective-permute-done | bytes 540704 | tf_op jit(solution)/shard_map/ppermute | solution.py:46
  165.7 2.1 %collective-permute-start.48 = (bf16[1,96,512]{2,1,0:T(8,128)(2,1)S(1)}, bf16[1,96,512]{2,1,0:T(8,128)(2,1)S(1)}, u32[]{:S(2)}, u32[]{:S(2)}) collective-permute-start(bf16[1,96,512]{2,1,0:T(8,128)(2,1)S(1)} %get-tuple-element.173), channel_id=1, source_target_pairs={{0,4},{1,5},{2,6},{3,7},{4,0},{5,1},{6,2},{7,3},{8,12},{9,13},{10,... | collective-permute-start | bytes 294920 | tf_op jit(solution)/shard_map/ppermute | solution.py:46
  169.2 3.4 %collective-permute-start.41 = (bf16[96,576]{1,0:T(8,128)(2,1)S(1)}, bf16[96,576]{1,0:T(8,128)(2,1)S(1)}, u32[]{:S(2)}, u32[]{:S(2)}) collective-permute-start(bf16[96,576]{1,0:T(8,128)(2,1)S(1)} %fusion.3), channel_id=1, source_target_pairs={{0,0},{1,1},{2,8},{3,9},{4,16},{5,17},{6,24},{7,25},{8,2},{9,3},{1... | collective-permute-start | bytes 331784 | tf_op jit(solution)/shard_map/ppermute | solution.py:46
  172.7 1.7 collective-permute-start.36
  176.4 2.2 %collective-permute-done.41 = bf16[96,576]{1,0:T(8,128)(2,1)S(1)} collective-permute-done((bf16[96,576]{1,0:T(8,128)(2,1)S(1)}, bf16[96,576]{1,0:T(8,128)(2,1)S(1)}, u32[]{:S(2)}, u32[]{:S(2)}) %collective-permute-start.41) | collective-permute-done | bytes 110624 | tf_op jit(solution)/shard_map/ppermute | solution.py:46
  180.0 3.4 %collective-permute-done.42.refs_2_ = bf16[2,96,704]{2,1,0:T(8,128)(2,1)S(1)} collective-permute-done((bf16[2,96,704]{2,1,0:T(8,128)(2,1)S(1)}, bf16[2,96,704]{2,1,0:T(8,128)(2,1)S(1)}, u32[]{:S(2)}, u32[]{:S(2)}) %collective-permute-start.42) | collective-permute-done | bytes 270368 | tf_op jit(solution)/shard_map/ppermute | solution.py:46
  184.0 2.4 %collective-permute-start.49 = (bf16[1,96,704]{2,1,0:T(8,128)(2,1)S(1)}, bf16[1,96,704]{2,1,0:T(8,128)(2,1)S(1)}, u32[]{:S(2)}, u32[]{:S(2)}) collective-permute-start(bf16[1,96,704]{2,1,0:T(8,128)(2,1)S(1)} %get-tuple-element.175), channel_id=1, source_target_pairs={{0,4},{1,5},{2,6},{3,7},{4,0},{5,1},{6,2},{7,3},{8,12},{9,13},{10,... | collective-permute-start | bytes 405512 | tf_op jit(solution)/shard_map/ppermute | solution.py:46
  187.0 5.9 %collective-permute-done.49.refs_2_ = bf16[1,96,704]{2,1,0:T(8,128)(2,1)S(1)} collective-permute-done((bf16[1,96,704]{2,1,0:T(8,128)(2,1)S(1)}, bf16[1,96,704]{2,1,0:T(8,128)(2,1)S(1)}, u32[]{:S(2)}, u32[]{:S(2)}) %collective-permute-start.49) | collective-permute-done | bytes 135200 | tf_op jit(solution)/shard_map/ppermute | solution.py:46
  (196 shorter events, 64.8 us)
Async XLA Ops:
  2.9 14.0 %collective-permute-start.2 = (bf16[144,768]{1,0:T(8,128)(2,1)}, bf16[144,768]{1,0:T(8,128)(2,1)S(1)}, u32[]{:S(2)}, u32[]{:S(2)}) collective-permute-start(bf16[144,768]{1,0:T(8,128)(2,1)} %pack.1), channel_id=1, source_target_pairs={{0,4},{1,12},{2,6},{3,14},{4,0},{5,8},{6,2},{7,10},{8,5},{9,13},{1... | collective-permute-start | bytes 663560 | tf_op jit(solution)/shard_map/ppermute | solution.py:46
  5.6 13.5 %collective-permute-start = (bf16[144,768]{1,0:T(8,128)(2,1)}, bf16[144,768]{1,0:T(8,128)(2,1)S(1)}, u32[]{:S(2)}, u32[]{:S(2)}) collective-permute-start(bf16[144,768]{1,0:T(8,128)(2,1)} %pack.1), channel_id=1, source_target_pairs={{0,0},{1,8},{2,2},{3,10},{4,4},{5,12},{6,6},{7,14},{8,1},{9,9},{10... | collective-permute-start | bytes 663560 | tf_op jit(solution)/shard_map/ppermute | solution.py:46
  7.2 11.9 %collective-permute-start.1 = (bf16[144,768]{1,0:T(8,128)(2,1)}, bf16[144,768]{1,0:T(8,128)(2,1)S(1)}, u32[]{:S(2)}, u32[]{:S(2)}) collective-permute-start(bf16[144,768]{1,0:T(8,128)(2,1)} %pack.1), channel_id=1, source_target_pairs={{0,2},{1,10},{2,0},{3,8},{4,6},{5,14},{6,4},{7,12},{8,3},{9,11},{1... | collective-permute-start | bytes 663560 | tf_op jit(solution)/shard_map/ppermute | solution.py:46
  17.0 7.3 %collective-permute-start.3 = (bf16[1,144,768]{2,1,0:T(8,128)(2,1)S(1)}, bf16[1,144,768]{2,1,0:T(8,128)(2,1)S(1)}, u32[]{:S(2)}, u32[]{:S(2)}) collective-permute-start(bf16[1,144,768]{2,1,0:T(8,128)(2,1)S(1)} %bitcast.43), channel_id=1, source_target_pairs={{0,2},{1,3},{2,0},{3,1},{4,6},{5,7},{6,4},{7,5},{8,10},{9,11},{10,... | collective-permute-start | bytes 663560 | tf_op jit(solution)/shard_map/ppermute | solution.py:46
  24.2 7.2 %collective-permute-start.4 = (bf16[1,144,768]{2,1,0:T(8,128)(2,1)S(1)}, bf16[1,144,768]{2,1,0:T(8,128)(2,1)}, u32[]{:S(2)}, u32[]{:S(2)}) collective-permute-start(bf16[1,144,768]{2,1,0:T(8,128)(2,1)S(1)} %bitcast.46), channel_id=1, source_target_pairs={{0,8},{1,9},{2,10},{3,11},{4,12},{5,13},{6,14},{7,15},{8,0},{9,1},... | collective-permute-start | bytes 663560 | tf_op jit(solution)/shard_map/ppermute | solution.py:46
  24.2 7.7 %collective-permute-start.5 = (bf16[1,144,768]{2,1,0:T(8,128)(2,1)S(1)}, bf16[1,144,768]{2,1,0:T(8,128)(2,1)}, u32[]{:S(2)}, u32[]{:S(2)}) collective-permute-start(bf16[1,144,768]{2,1,0:T(8,128)(2,1)S(1)} %bitcast.48), channel_id=1, source_target_pairs={{0,8},{1,9},{2,10},{3,11},{4,12},{5,13},{6,14},{7,15},{8,0},{9,1},... | collective-permute-start | bytes 663560 | tf_op jit(solution)/shard_map/ppermute | solution.py:46
  31.5 24.7 %collective-permute-start.12 = (bf16[128,384]{1,0:T(8,128)(2,1)S(1)}, bf16[128,384]{1,0:T(8,128)(2,1)S(1)}, u32[]{:S(2)}, u32[]{:S(2)}) collective-permute-start(bf16[128,384]{1,0:T(8,128)(2,1)S(1)} %get-tuple-element.191.refs_5_), channel_id=1, source_target_pairs={{0,8},{1,9},{2,10},{3,11},{4,12},{5,13},{6,14},{7,15},{8,0},{9,1},... | collective-permute-start | bytes 294920 | tf_op jit(solution)/shard_map/ppermute | solution.py:46
  31.5 25.1 %collective-permute-start.14 = (bf16[128,384]{1,0:T(8,128)(2,1)S(1)}, bf16[128,384]{1,0:T(8,128)(2,1)S(1)}, u32[]{:S(2)}, u32[]{:S(2)}) collective-permute-start(bf16[128,384]{1,0:T(8,128)(2,1)S(1)} %collective-permute-done.13.refs_7_), channel_id=1, source_target_pairs={{0,8},{1,9},{2,10},{3,11},{4,12},{5,13},{6,14},{7,15},{8,0},{9,1},... | collective-permute-start | bytes 294920 | tf_op jit(solution)/shard_map/ppermute | solution.py:46
  64.2 18.4 %collective-permute-start.19 = (bf16[128,2816]{1,0:T(8,128)(2,1)S(1)}, bf16[128,2816]{1,0:T(8,128)(2,1)S(1)}, u32[]{:S(2)}, u32[]{:S(2)}) collective-permute-start(bf16[128,2816]{1,0:T(8,128)(2,1)S(1)} %get-tuple-element.140.refs_3_.refs_1_), channel_id=1, source_target_pairs={{0,16},{1,17},{2,18},{3,19},{4,20},{5,21},{6,22},{7,23},{8,24},{9,... | collective-permute-start | bytes 2162696 | tf_op jit(solution)/shard_map/ppermute | solution.py:46
  71.7 8.9 %collective-permute-start.16 = (bf16[128,192]{1,0:T(8,128)(2,1)S(1)}, bf16[128,192]{1,0:T(8,128)(2,1)S(1)}, u32[]{:S(2)}, u32[]{:S(2)}) collective-permute-start(bf16[128,192]{1,0:T(8,128)(2,1)S(1)} %get-tuple-element.113), channel_id=1, source_target_pairs={{0,2},{1,10},{2,0},{3,8},{4,6},{5,14},{6,4},{7,12},{8,3},{9,11},{1... | collective-permute-start | bytes 147464 | tf_op jit(solution)/shard_map/ppermute | solution.py:46
  72.3 8.4 %collective-permute-start.17 = (bf16[128,192]{1,0:T(8,128)(2,1)S(1)}, bf16[128,192]{1,0:T(8,128)(2,1)S(1)}, u32[]{:S(2)}, u32[]{:S(2)}) collective-permute-start(bf16[128,192]{1,0:T(8,128)(2,1)S(1)} %get-tuple-element.114), channel_id=1, source_target_pairs={{0,4},{1,12},{2,6},{3,14},{4,0},{5,8},{6,2},{7,10},{8,5},{9,13},{1... | collective-permute-start | bytes 147464 | tf_op jit(solution)/shard_map/ppermute | solution.py:46
  76.2 18.6 %collective-permute-start.21 = (bf16[128,2816]{1,0:T(8,128)(2,1)S(1)}, bf16[128,2816]{1,0:T(8,128)(2,1)S(1)}, u32[]{:S(2)}, u32[]{:S(2)}) collective-permute-start(bf16[128,2816]{1,0:T(8,128)(2,1)S(1)} %get-tuple-element.140.refs_3_.refs_1_), channel_id=1, source_target_pairs={{0,8},{1,9},{2,10},{3,11},{4,12},{5,13},{6,14},{7,15},{8,0},{9,1},... | collective-permute-start | bytes 2162696 | tf_op jit(solution)/shard_map/ppermute | solution.py:46
  93.3 12.1 %collective-permute-start.28 = (bf16[128,1024]{1,0:T(8,128)(2,1)S(1)}, bf16[128,1024]{1,0:T(8,128)(2,1)S(1)}, u32[]{:S(2)}, u32[]{:S(2)}) collective-permute-start(bf16[128,1024]{1,0:T(8,128)(2,1)S(1)} %get-tuple-element.146), channel_id=1, source_target_pairs={{0,16},{1,17},{2,18},{3,19},{4,20},{5,21},{6,22},{7,23},{8,24},{9,... | collective-permute-start | bytes 786440 | tf_op jit(solution)/shard_map/ppermute | solution.py:46
  98.1 8.8 %collective-permute-start.23 = (bf16[128,576]{1,0:T(8,128)(2,1)}, bf16[128,576]{1,0:T(8,128)(2,1)}, u32[]{:S(2)}, u32[]{:S(2)}) collective-permute-start(bf16[128,576]{1,0:T(8,128)(2,1)} %get-tuple-element.134.refs_1_), channel_id=1, source_target_pairs={{0,0},{1,8},{2,2},{3,10},{4,4},{5,12},{6,6},{7,14},{8,1},{9,9},{10... | collective-permute-start | bytes 442376 | tf_op jit(solution)/shard_map/ppermute | solution.py:46
  101.0 8.8 %collective-permute-start.24 = (bf16[128,576]{1,0:T(8,128)(2,1)}, bf16[128,576]{1,0:T(8,128)(2,1)}, u32[]{:S(2)}, u32[]{:S(2)}) collective-permute-start(bf16[128,576]{1,0:T(8,128)(2,1)} %get-tuple-element.135.refs_2_), channel_id=1, source_target_pairs={{0,2},{1,10},{2,0},{3,8},{4,6},{5,14},{6,4},{7,12},{8,3},{9,11},{1... | collective-permute-start | bytes 442376 | tf_op jit(solution)/shard_map/ppermute | solution.py:46
  101.0 15.1 %collective-permute-start.25 = (bf16[128,576]{1,0:T(8,128)(2,1)}, bf16[128,576]{1,0:T(8,128)(2,1)}, u32[]{:S(2)}, u32[]{:S(2)}) collective-permute-start(bf16[128,576]{1,0:T(8,128)(2,1)} %get-tuple-element.136.refs_3_), channel_id=1, source_target_pairs={{0,4},{1,12},{2,6},{3,14},{4,0},{5,8},{6,2},{7,10},{8,5},{9,13},{1... | collective-permute-start | bytes 442376 | tf_op jit(solution)/shard_map/ppermute | solution.py:46
  103.0 13.9 %collective-permute-start.26 = (bf16[128,576]{1,0:T(8,128)(2,1)}, bf16[128,576]{1,0:T(8,128)(2,1)}, u32[]{:S(2)}, u32[]{:S(2)}) collective-permute-start(bf16[128,576]{1,0:T(8,128)(2,1)} %get-tuple-element.137.refs_4_), channel_id=1, source_target_pairs={{0,6},{1,14},{2,4},{3,12},{4,2},{5,10},{6,0},{7,8},{8,7},{9,15},{1... | collective-permute-start | bytes 442376 | tf_op jit(solution)/shard_map/ppermute | solution.py:46
  105.4 19.0 %collective-permute-start.27 = (bf16[128,2176]{1,0:T(8,128)(2,1)}, bf16[128,2176]{1,0:T(8,128)(2,1)}, u32[]{:S(2)}, u32[]{:S(2)}) collective-permute-start(bf16[128,2176]{1,0:T(8,128)(2,1)} %get-tuple-element.145), channel_id=1, source_target_pairs={{0,8},{1,9},{2,10},{3,11},{4,12},{5,13},{6,14},{7,15},{8,0},{9,1},... | collective-permute-start | bytes 1671176 | tf_op jit(solution)/shard_map/ppermute | solution.py:46
  106.9 28.6 %collective-permute-start.30 = (bf16[128,2176]{1,0:T(8,128)(2,1)}, bf16[128,2176]{1,0:T(8,128)(2,1)S(1)}, u32[]{:S(2)}, u32[]{:S(2)}) collective-permute-start(bf16[128,2176]{1,0:T(8,128)(2,1)} %copy-done.16), channel_id=1, source_target_pairs={{0,16},{1,17},{2,18},{3,19},{4,20},{5,21},{6,22},{7,23},{8,24},{9,... | collective-permute-start | bytes 1671176 | tf_op jit(solution)/shard_map/ppermute | solution.py:46
  109.9 17.6 %collective-permute-start.43 = (bf16[4,256,192]{2,1,0:T(8,128)(2,1)}, bf16[4,256,192]{2,1,0:T(8,128)(2,1)S(1)}, u32[]{:S(2)}, u32[]{:S(2)}) collective-permute-start(bf16[4,256,192]{2,1,0:T(8,128)(2,1)} %copy-done.17), channel_id=1, source_target_pairs={{0,1},{1,0},{2,3},{3,2},{4,5},{5,4},{6,7},{7,6},{8,9},{9,8},{10,11... | collective-permute-start | bytes 1179656 | tf_op jit(solution)/shard_map/ppermute | solution.py:46
  116.1 8.3 %collective-permute-start.29 = (bf16[128,1024]{1,0:T(8,128)(2,1)S(1)}, bf16[128,1024]{1,0:T(8,128)(2,1)S(1)}, u32[]{:S(2)}, u32[]{:S(2)}) collective-permute-start(bf16[128,1024]{1,0:T(8,128)(2,1)S(1)} %collective-permute-done.28.refs_7_), channel_id=1, source_target_pairs={{0,8},{1,9},{2,10},{3,11},{4,12},{5,13},{6,14},{7,15},{8,0},{9,1},... | collective-permute-start | bytes 786440 | tf_op jit(solution)/shard_map/ppermute | solution.py:46
  126.2 13.0 %collective-permute-start.46 = (bf16[4,96,512]{2,1,0:T(8,128)(2,1)S(1)}, bf16[4,96,512]{2,1,0:T(8,128)(2,1)S(1)}, u32[]{:S(2)}, u32[]{:S(2)}) collective-permute-start(bf16[4,96,512]{2,1,0:T(8,128)(2,1)S(1)} %get-tuple-element.148), channel_id=1, source_target_pairs={{0,1},{1,0},{2,3},{3,2},{4,5},{5,4},{6,7},{7,6},{8,9},{9,8},{10,11... | collective-permute-start | bytes 1179656 | tf_op jit(solution)/shard_map/ppermute | solution.py:46
  128.2 8.5 %collective-permute-start.44 = (bf16[2,256,192]{2,1,0:T(8,128)(2,1)S(1)}, bf16[2,256,192]{2,1,0:T(8,128)(2,1)S(1)}, u32[]{:S(2)}, u32[]{:S(2)}) collective-permute-start(bf16[2,256,192]{2,1,0:T(8,128)(2,1)S(1)} %get-tuple-element.166), channel_id=1, source_target_pairs={{0,2},{1,3},{2,0},{3,1},{4,6},{5,7},{6,4},{7,5},{8,10},{9,11},{10,... | collective-permute-start | bytes 589832 | tf_op jit(solution)/shard_map/ppermute | solution.py:46
  135.5 7.7 %collective-permute-start.31 = (bf16[128,2176]{1,0:T(8,128)(2,1)S(1)}, bf16[128,2176]{1,0:T(8,128)(2,1)S(1)}, u32[]{:S(2)}, u32[]{:S(2)}) collective-permute-start(bf16[128,2176]{1,0:T(8,128)(2,1)S(1)} %collective-permute-done.30.refs_7_), channel_id=1, source_target_pairs={{0,8},{1,9},{2,10},{3,11},{4,12},{5,13},{6,14},{7,15},{8,0},{9,1},... | collective-permute-start | bytes 1671176 | tf_op jit(solution)/shard_map/ppermute | solution.py:46
  137.3 10.0 %collective-permute-start.45 = (bf16[1,256,192]{2,1,0:T(8,128)(2,1)S(1)}, bf16[1,256,192]{2,1,0:T(8,128)(2,1)S(1)}, u32[]{:S(2)}, u32[]{:S(2)}) collective-permute-start(bf16[1,256,192]{2,1,0:T(8,128)(2,1)S(1)} %get-tuple-element.168), channel_id=1, source_target_pairs={{0,4},{1,5},{2,6},{3,7},{4,0},{5,1},{6,2},{7,3},{8,12},{9,13},{10,... | collective-permute-start | bytes 294920 | tf_op jit(solution)/shard_map/ppermute | solution.py:46
  140.6 24.4 %collective-permute-start.47 = (bf16[2,96,512]{2,1,0:T(8,128)(2,1)S(1)}, bf16[2,96,512]{2,1,0:T(8,128)(2,1)S(1)}, u32[]{:S(2)}, u32[]{:S(2)}) collective-permute-start(bf16[2,96,512]{2,1,0:T(8,128)(2,1)S(1)} %get-tuple-element.171), channel_id=1, source_target_pairs={{0,2},{1,3},{2,0},{3,1},{4,6},{5,7},{6,4},{7,5},{8,10},{9,11},{10,... | collective-permute-start | bytes 589832 | tf_op jit(solution)/shard_map/ppermute | solution.py:46
  146.3 13.3 %collective-permute-start.32 = (bf16[4,96,704]{2,1,0:T(8,128)(2,1)S(1)}, bf16[4,96,704]{2,1,0:T(8,128)(2,1)S(1)}, u32[]{:S(2)}, u32[]{:S(2)}) collective-permute-start(bf16[4,96,704]{2,1,0:T(8,128)(2,1)S(1)} %get-tuple-element.158), channel_id=1, source_target_pairs={{0,1},{1,0},{2,3},{3,2},{4,5},{5,4},{6,7},{7,6},{8,9},{9,8},{10,11... | collective-permute-start | bytes 1622024 | tf_op jit(solution)/shard_map/ppermute | solution.py:46
  161.7 7.5 %collective-permute-start.40 = (bf16[1,96,576]{2,1,0:T(8,128)(2,1)S(1)}, bf16[1,96,576]{2,1,0:T(8,128)(2,1)S(1)}, u32[]{:S(2)}, u32[]{:S(2)}) collective-permute-start(bf16[1,96,576]{2,1,0:T(8,128)(2,1)S(1)} %fusion.2), channel_id=1, source_target_pairs={{0,1},{1,0},{2,3},{3,2},{4,5},{5,4},{6,7},{7,6},{8,9},{9,8},{10,11... | collective-permute-start | bytes 331784 | tf_op jit(solution)/shard_map/ppermute | solution.py:46
  165.7 8.8 %collective-permute-start.48 = (bf16[1,96,512]{2,1,0:T(8,128)(2,1)S(1)}, bf16[1,96,512]{2,1,0:T(8,128)(2,1)S(1)}, u32[]{:S(2)}, u32[]{:S(2)}) collective-permute-start(bf16[1,96,512]{2,1,0:T(8,128)(2,1)S(1)} %get-tuple-element.173), channel_id=1, source_target_pairs={{0,4},{1,5},{2,6},{3,7},{4,0},{5,1},{6,2},{7,3},{8,12},{9,13},{10,... | collective-permute-start | bytes 294920 | tf_op jit(solution)/shard_map/ppermute | solution.py:46
  169.2 9.4 %collective-permute-start.41 = (bf16[96,576]{1,0:T(8,128)(2,1)S(1)}, bf16[96,576]{1,0:T(8,128)(2,1)S(1)}, u32[]{:S(2)}, u32[]{:S(2)}) collective-permute-start(bf16[96,576]{1,0:T(8,128)(2,1)S(1)} %fusion.3), channel_id=1, source_target_pairs={{0,0},{1,1},{2,8},{3,9},{4,16},{5,17},{6,24},{7,25},{8,2},{9,3},{1... | collective-permute-start | bytes 331784 | tf_op jit(solution)/shard_map/ppermute | solution.py:46
  175.7 7.8 %collective-permute-start.42 = (bf16[2,96,704]{2,1,0:T(8,128)(2,1)S(1)}, bf16[2,96,704]{2,1,0:T(8,128)(2,1)S(1)}, u32[]{:S(2)}, u32[]{:S(2)}) collective-permute-start(bf16[2,96,704]{2,1,0:T(8,128)(2,1)S(1)} %get-tuple-element.160), channel_id=1, source_target_pairs={{0,2},{1,3},{2,0},{3,1},{4,6},{5,7},{6,4},{7,5},{8,10},{9,11},{10,... | collective-permute-start | bytes 811016 | tf_op jit(solution)/shard_map/ppermute | solution.py:46
  184.0 8.8 %collective-permute-start.49 = (bf16[1,96,704]{2,1,0:T(8,128)(2,1)S(1)}, bf16[1,96,704]{2,1,0:T(8,128)(2,1)S(1)}, u32[]{:S(2)}, u32[]{:S(2)}) collective-permute-start(bf16[1,96,704]{2,1,0:T(8,128)(2,1)S(1)} %get-tuple-element.175), channel_id=1, source_target_pairs={{0,4},{1,5},{2,6},{3,7},{4,0},{5,1},{6,2},{7,3},{8,12},{9,13},{10,... | collective-permute-start | bytes 405512 | tf_op jit(solution)/shard_map/ppermute | solution.py:46
  (62 other events, 483.9 us)
where the time goes:
time: 198 us; the launch traced here: 194 us
  starting transfers between devices  67.1 us (34%)
  waiting for transfers between devices  54.9 us (28%)
  Pallas kernels  53.5 us (27%)
  local copies, waits for them, and re-layouts  16 us (8%)
    ppermute x50, starting transfers between devices, send(): return lax.ppermute(block, axes, route)  67.1 us
    ppermute x50, waiting for transfers between devices, send(): return lax.ppermute(block, axes, route)  54.9 us
    pallas_call x21, Pallas kernels, kernel_call(): pl.pallas_call(kernel, out_shape=outputs, in_specs=[pl.BlockSpec(memory_s...  53.5 us
    unnamed x90, local copies, waits for them, and re-layouts  13.9 us
  transfers between devices with their start and end apart: 50, of which 18 were waited for; matrix products, arithmetic and copies ran while one was open for 2% of the time, Pallas kernels for 25%

commit v1 on v0

--- a/solution.py
+++ b/solution.py
@@ -85,14 +85,17 @@
     body, name, smem, inputs, outputs, scratch=(), in_hbm=(), staged=(), mebibytes=4, us=3
 ):
     n_smem, n_in, n_out = len(smem), len(inputs), len(outputs)
+    ins = [i for i in staged if not isinstance(i, tuple)]
+    leaving = [i[1] for i in staged if isinstance(i, tuple)]
 
     def kernel(*refs):
         given = refs[n_smem : n_smem + n_in]
-        outs = refs[n_smem + n_in : n_smem + n_in + n_out]
+        results = refs[n_smem + n_in : n_smem + n_in + n_out]
         rest = refs[n_smem + n_in + n_out :]
-        buffers = dict(zip(staged, rest[: len(staged)]))
+        buffers = dict(zip(ins, rest))
+        drafts = dict(zip(leaving, rest[len(ins) :]))
         arrivals = {}
-        for at, i in enumerate(staged):
+        for at, i in enumerate(ins):
             arrivals[i] = pltpu.make_async_copy(given[i], buffers[i], rest[-1].at[at])
             arrivals[i].start()
 
@@ -101,9 +104,18 @@
                 arrivals.pop(i).wait()
             return buffers.get(i, given[i])
 
+        outs = [drafts.get(i, results[i]) for i in range(n_out)]
         body(refs[:n_smem], get, outs, *rest[len(staged) : len(rest) - (1 if staged else 0)])
-        for i in staged:
+        for i in ins:
             get(i)
+        departures = [
+            pltpu.make_async_copy(drafts[i], results[i], rest[-1].at[len(ins) + at])
+            for at, i in enumerate(leaving)
+        ]
+        for copy in departures:
+            copy.start()
+        for copy in departures:
+            copy.wait()
 
     hbm = pl.BlockSpec(memory_space=pltpu.HBM)
     vmem = pl.BlockSpec(memory_space=pltpu.VMEM)
@@ -112,9 +124,10 @@
         kernel,
         out_shape=outputs,
         in_specs=[pl.BlockSpec(memory_space=pltpu.SMEM)] * n_smem
-        + [hbm if i in in_hbm or i in staged else vmem for i in range(n_in)],
-        out_specs=[hbm if ("out", i) in in_hbm else vmem for i in range(n_out)],
-        scratch_shapes=[pltpu.VMEM(inputs[i].shape, inputs[i].dtype) for i in staged]
+        + [hbm if i in in_hbm or i in ins else vmem for i in range(n_in)],
+        out_specs=[hbm if ("out", i) in in_hbm or i in leaving else vmem for i in range(n_out)],
+        scratch_shapes=[pltpu.VMEM(inputs[i].shape, inputs[i].dtype) for i in ins]
+        + [pltpu.VMEM(outputs[i].shape, outputs[i].dtype) for i in leaving]
         + list(scratch)
         + copies,
         compiler_params=pltpu.CompilerParams(vmem_limit_bytes=mebibytes * 2**20),
@@ -132,33 +145,25 @@
     return pl.multiple_of(start, 128), (group * local) % 128 != 0
 
 
-def pack_body(smem, get, outs, sems):
-    tokens_ref, segment_ref = get(0), get(1)
-    packet, spare = outs[0], sems[0]
-    tok, width = tokens_ref.shape
-    copy = pltpu.make_async_copy(tokens_ref, packet.at[pl.ds(0, tok)], sems[1].at[0])
-    copy.start()
-    row = jnp.broadcast_to(segment_ref[...].astype(f32), (spare.shape[0], tok))
-    spare[:, :tok] = row.astype(bf16)
-    spare[:, tok:] = jnp.zeros((spare.shape[0], width - tok), bf16)
-    more = pltpu.make_async_copy(spare, packet.at[pl.ds(tok, spare.shape[0])], sems[1].at[1])
-    more.start()
-    more.wait()
-    copy.wait()
+def pack_body(smem, get, outs):
+    (packet,) = outs
+    tok, width = get(0).shape
+    row = jnp.broadcast_to(get(1)[...].astype(f32), (packet.shape[0] - tok, tok))
+    packet[tok:, :tok] = row.astype(bf16)
+    packet[tok:, tok:] = jnp.zeros((packet.shape[0] - tok, width - tok), bf16)
+    packet[:tok, :] = get(0)[...]
 
 
 def packed(tokens, segment_ids):
     tok, width = tokens.shape
     return kernel_call(
-        lambda smem, get, outs, *scratch: pack_body(smem, get, outs, scratch),
+        pack_body,
         "pack",
         [],
         [tokens, segment_ids],
         [shaped(bf16, tok + 16, width)],
-        scratch=[pltpu.VMEM((16, width), bf16), pltpu.SemaphoreType.DMA((2,))],
-        in_hbm=(0, ("out", 0)),
-        staged=(1,),
-        mebibytes=2,
+        staged=(0, 1),
+        mebibytes=60,
         us=1,
     )[0]
 
@@ -197,27 +202,71 @@
     )
 
 
-def forward_body(
-    smem, get, outs, weight_scr, normed_scr, kv_scr, segk, strip, s_scr, p_scr, sems, *, blocks, chunk
-):
+def project_body(smem, get, outs, weight_scr, normed_scr, all_scr, *, count):
+    (place,) = smem
+    kv_ref, q_ref, normed_ref = outs
+    group = place[0]
+    tok = q_ref.shape[1]
+    s_count = kv_ref.shape[1]
+    local = q_ref.shape[2]
+    window, late = group_window(group, local)
+    for i in range(3):
+        both = get(count + 1 + i)[:, pl.ds(window, -(-local // 128) * 128)]
+        weight_scr[:, i * local : (i + 1) * local] = jnp.where(
+            late, both[:, both.shape[1] - local :], both[:, :local]
+        )
+    gain = get(count)[...]
+    for e in range(s_count):
+        for d in range(count):
+            values = get(d)[e, :tok, :].astype(f32)
+            normed_scr[d * tok : (d + 1) * tok, :] = (values * rms_scale(values) * gain).astype(bf16)
+        all_scr[...] = dot(normed_scr[...], weight_scr[...], 1, 0).astype(bf16)
+        for d in range(count):
+            rows = all_scr[d * tok : (d + 1) * tok, :]
+            kv_ref[d, e, :, : 2 * local] = rows[:, local:]
+            row = jnp.broadcast_to(get(d)[e, tok : tok + 1, :tok].astype(f32), (tok, tok))
+            kv_ref[d, e, :, 2 * local :] = jnp.transpose(row).astype(bf16)
+            if e == 0:
+                q_ref[d] = rows[:, :local]
+                normed_ref[d * tok : (d + 1) * tok, :] = normed_scr[d * tok : (d + 1) * tok, :]
+
+
+def project(place, blocks, gain, w_query, w_key, w_value):
+    s_count, rows, width = blocks[0].shape
+    tok = rows - 16
+    local = width // groups
+    count = len(blocks)
+    return kernel_call(
+        functools.partial(project_body, count=count),
+        "project",
+        [place],
+        [*blocks, gain, w_query, w_key, w_value],
+        [
+            shaped(bf16, count, s_count, tok, 2 * local + tok),
+            shaped(bf16, count, tok, local),
+            shaped(bf16, count * tok, width),
+        ],
+        scratch=[
+            pltpu.VMEM((width, 3 * local), bf16),
+            pltpu.VMEM((count * tok, width), bf16),
+            pltpu.VMEM((count * tok, 3 * local), bf16),
+        ],
+        mebibytes=8,
+        us=3,
+    )
+
+
+def forward_body(smem, get, outs, segk, strip, s_scr, p_scr, sems, *, blocks, chunk):
     (place,) = smem
     ctx = outs[0:4]
-    q_ref, k_ref, v_ref, o_ref, normed_ref, p_hbm = outs[4:10]
+    q_ref, k_ref, v_ref, o_ref, p_hbm = outs[4:9]
     group, core, s_own = place[0], place[1], place[2]
     tok = 128
     head_size = 64
     s_count = blocks // 8
-    width = normed_scr.shape[1]
     local = q_ref.shape[1]
     seq = blocks * tok
     chunks = seq // chunk
-    window, late = group_window(group, local)
-    for i in range(3):
-        both = get(10 + i)[:, pl.ds(window, -(-local // 128) * 128)]
-        weight_scr[:, i * local : (i + 1) * local] = jnp.where(
-            late, both[:, both.shape[1] - local :], both[:, :local]
-        )
-    gain = get(9)[...]
 
     def block_of(d, e, k):
         return (((group ^ d) * s_count + (s_own ^ e)) * 2) + (core if k == 0 else 1 - core)
@@ -225,26 +274,16 @@
     def load_chunk(e):
         for k in range(2):
             for d in range(4):
-                raw = get(k * 4 + d)
-                values = raw[e, :tok, :].astype(f32)
-                slot = k * 4 + d
-                normed_scr[slot * tok : (slot + 1) * tok, :] = (
-                    values * rms_scale(values) * gain
-                ).astype(bf16)
+                source, at = (get(2 * k), d) if d < 3 else (get(2 * k + 1), 0)
                 start = pl.multiple_of(block_of(d, e, k) * tok, tok)
-                segk[0:1, pl.ds(start, tok)] = raw[e, tok : tok + 1, :tok].astype(f32)
-        kv_scr[...] = dot(normed_scr[...], weight_scr[:, local:], 1, 0).astype(bf16)
-        for k in range(2):
-            for d in range(4):
-                slot = k * 4 + d
-                start = pl.multiple_of(block_of(d, e, k) * tok, tok)
-                rows = kv_scr[slot * tok : (slot + 1) * tok, :]
-                k_ref[pl.ds(start, tok), :] = rows[:, :local]
-                v_ref[pl.ds(start, tok), :] = rows[:, local:]
+                k_ref[pl.ds(start, tok), :] = source[at, e, :, :local]
+                v_ref[pl.ds(start, tok), :] = source[at, e, :, local : 2 * local]
+                row = jnp.transpose(source[at, e, :, 2 * local :].astype(f32))
+                segk[0:1, pl.ds(start, tok)] = row[0:1]
 
     load_chunk(0)
-    normed_ref[...] = normed_scr[: 4 * tok, :]
-    q_ref[...] = dot(normed_scr[: 4 * tok, :], weight_scr[:, :local], 1, 0).astype(bf16)
+    for d in range(4):
+        q_ref[d * tok : (d + 1) * tok, :] = get(4)[d] if d < 3 else get(5)[0]
     if s_count > 1:
 
         @pl.loop(1, s_count)
@@ -262,7 +301,7 @@
     span = 4 * tok
     for h in range(heads):
         cols = slice(h * head_size, (h + 1) * head_size)
-        bias_row = get(8)[h : h + 1, :]
+        bias_row = get(6)[h : h + 1, :]
         spread = jnp.broadcast_to(bias_row, (tok, span))
         near = pltpu.roll(spread, 0, 1, stride=1, stride_axis=0)
         strip[:, tok * (blocks - 2) : tok * (blocks + 1)] = near[:, tok : 4 * tok]
@@ -275,8 +314,8 @@
         for d in range(4):
             query_block = block_of(d, 0, 0)
             strip_base = tok * (blocks - 1) - query_block * tok
-            seg_row = get(d)[0, tok : tok + 1, :tok].astype(f32)
-            seg_col = jnp.transpose(jnp.broadcast_to(seg_row, (tok, tok)))[:, :1]
+            source, at = (get(0), d) if d < 3 else (get(1), 0)
+            seg_col = source[at, 0, :, 2 * local : 2 * local + 1].astype(f32)
             slot = (h * 4 + d) % 2
             if slot in pending:
                 pending.pop(slot).wait()
@@ -339,10 +378,9 @@
         copy.wait()
 
 
-def attention_forward(place, own, other, bias, gain, w_query, w_key, w_value):
-    s_count, rows, width = own[0].shape
-    tok = rows - 16
-    local = width // groups
+def attention_forward(place, kv, q, bias):
+    s_count, tok = kv[0].shape[1:3]
+    local = q[0].shape[2]
     blocks = 8 * s_count
     seq = blocks * tok
     chunk = min(seq, 1024)
@@ -350,29 +388,25 @@
         [shaped(bf16, tok, local)] * 4
         + [shaped(bf16, 4 * tok, local)]
         + [shaped(bf16, seq, local)] * 2
-        + [shaped(f32, 4 * tok, local), shaped(bf16, 4 * tok, width)]
+        + [shaped(f32, 4 * tok, local)]
         + [shaped(bf16, local // 64, seq // chunk, 4 * tok, chunk)]
     )
     return kernel_call(
         functools.partial(forward_body, blocks=blocks, chunk=chunk),
         "attention_forward",
         [place],
-        [*own, *other, bias, gain, w_query, w_key, w_value],
+        [*kv, *q, bias],
         shapes,
         scratch=[
-            pltpu.VMEM((width, 3 * local), bf16),
-            pltpu.VMEM((8 * tok, width), bf16),
-            pltpu.VMEM((8 * tok, 2 * local), bf16),
             pltpu.VMEM((8, seq), f32),
             pltpu.VMEM((tok, (2 * blocks - 1) * tok), f32),
             pltpu.VMEM((2 if seq == chunk else 1, tok, seq), f32),
             pltpu.VMEM((2, seq // chunk, tok, chunk), bf16),
             pltpu.SemaphoreType.DMA((2,)),
         ],
-        in_hbm=(("out", 9),),
-        staged=tuple(range(8)) if s_count == 1 else (),
-        mebibytes=12 if s_count == 1 else 60,
-        us=25,
+        in_hbm=(("out", 8),),
+        mebibytes=8 if s_count == 1 else 60,
+        us=10,
     )
 
 
@@ -517,14 +551,26 @@
             pltpu.SemaphoreType.DMA((2,)),
         ],
         in_hbm=(8,),
-        mebibytes=11 if s_count == 1 else 60,
-        us=20,
-    )
+        staged=tuple(("out", i) for i in range(6)) if s_count == 1 else (),
+        mebibytes=13 if s_count == 1 else 60,
+        us=7,
+    )
+
+
+def gated(gate, up):
+    root = 0.7978845608028654
+    square = gate * gate
+    bend = jnp.tanh(root * (gate + 0.044715 * (gate * square)))
+    act = 0.5 * gate * (1.0 + bend)
+    slope = 0.5 * (1.0 + bend) + 0.5 * gate * (1.0 - bend * bend) * (
+        root * (1.0 + 3.0 * 0.044715 * square)
+    )
+    return act, up * slope
 
 
 def ffn_forward_body(smem, get, outs):
     (place,) = smem
-    middle_ref, left_ref, act_ref, slope_ref = outs
+    middle_ref, normed_ref, hidden_ref, act_ref, slope_ref = outs
     count = 4
     w_out, w_gate, w_up = get(6), get(7), get(8)
     group = place[0]
@@ -536,22 +582,15 @@
         total = total + dot(get(d)[...], w_out[pl.ds(start, local), :], 1, 0)
     middle_ref[...] = total
     normed = (total * rms_scale(total) * get(5)[...]).astype(bf16)
-    left_ref[:, :width] = normed
+    normed_ref[...] = normed
     step = w_gate.shape[1] // count
     for i in range(count):
         cols = slice(i * step, (i + 1) * step)
-        gate = dot(normed, w_gate[:, cols], 1, 0)
         up = dot(normed, w_up[:, cols], 1, 0)
-        root = 0.7978845608028654
-        square = gate * gate
-        bend = jnp.tanh(root * (gate + 0.044715 * (gate * square)))
-        act = 0.5 * gate * (1.0 + bend)
-        slope = 0.5 * (1.0 + bend) + 0.5 * gate * (1.0 - bend * bend) * (
-            root * (1.0 + 3.0 * 0.044715 * square)
-        )
+        act, slope = gated(dot(normed, w_gate[:, cols], 1, 0), up)
         act_ref[:, cols] = act
-        slope_ref[:, cols] = up * slope
-        left_ref[:, width + i * step : width + (i + 1) * step] = (act * up).astype(bf16)
+        slope_ref[:, cols] = slope
+        hidden_ref[:, cols] = (act * up).astype(bf16)
 
 
 def ffn_forward(place, ctx, tokens, gain, w_out, w_gate, w_up):
@@ -564,26 +603,27 @@
         [*ctx, tokens, gain, w_out, w_gate, w_up],
         [
             shaped(f32, tok, width),
-            shaped(bf16, tok, width + ff),
+            shaped(bf16, tok, width),
+            shaped(bf16, tok, ff),
             shaped(f32, tok, ff),
             shaped(f32, tok, ff),
         ],
+        staged=(4,),
         us=14,
     )
 
 
-def ffn_backward_body(smem, get, outs, gate_scr, up_scr, attn_scr):
+def ffn_backward_body(smem, get, outs, attn_scr):
     (place,) = smem
     out_ref, grad_ref, gain_grad_ref = outs[0:3]
     dctx = outs[3:7]
-    mine_ref, near_ref, far_gate_ref, far_up_ref = outs[7:11]
+    mine_ref, far_ref = outs[7:9]
+    w_down, w_gate, w_up, w_out = get(10), get(11), get(12), get(13)
     count = 4
-    w_down, w_gate, w_up, w_out = get(10), get(11), get(12), get(13)
-    group, core, across = place[0], place[1], place[4]
+    group, across = place[0], place[4]
     tok, width = grad_ref.shape
     ff = w_gate.shape[1]
     local = width // groups
-    quarter = ff // 4
     cot = get(0)[...]
     step = ff // count
     act_ref, slope_ref = get(3), get(4)
@@ -593,21 +633,7 @@
         hidden_grad = dot(cot, w_down[cols, :], 1, 1)
         gate = (hidden_grad * slope_ref[:, cols]).astype(bf16)
         up = (hidden_grad * act_ref[:, cols]).astype(bf16)
-        gate_scr[:, cols] = gate
-        up_scr[:, cols] = up
-        normed_grad = (
-            normed_grad + dot(gate, w_gate[:, cols], 1, 1) + dot(up, w_up[:, cols], 1, 1)
-        )
-    def quarter_of(ref, x, c):
-        return ref[:, pl.ds(pl.multiple_of((x * 2 + c) * quarter, quarter), quarter)]
-
-    mine_ref[:, :quarter] = quarter_of(gate_scr, across, core)
-    mine_ref[:, quarter : 2 * quarter] = quarter_of(up_scr, across, core)
-    near_ref[:, :quarter] = quarter_of(gate_scr, across, 1 - core)
-    near_ref[:, quarter : 2 * quarter] = quarter_of(up_scr, across, 1 - core)
-    for ref, source in ((far_gate_ref, gate_scr), (far_up_ref, up_scr)):
-        ref[:, :quarter] = quarter_of(source, 1 - across, core)
-        ref[:, quarter : 2 * quarter] = quarter_of(source, 1 - across, 1 - core)
+        normed_grad = normed_grad + dot(gate, w_gate[:, cols], 1, 1) + dot(up, w_up[:, cols], 1, 1)
     middle = get(1)[...]
     scale = rms_scale(middle)
     unit = middle * scale
@@ -622,18 +648,16 @@
     for d in range(4):
         start = pl.multiple_of((group ^ d) * local, local)
         dctx[d][...] = dot(attn, w_out[pl.ds(start, local), :], 1, 1).astype(bf16)
-    at = 2 * quarter
-    for ref, which in ((mine_ref, across), (near_ref, across), (far_up_ref, 1 - across)):
+    for ref, which in ((mine_ref, across), (far_ref, 1 - across)):
         for d in range(4):
-            ref[:, at + d * local : at + (d + 1) * local] = get(6 + d)[...]
+            ref[:, d * local : (d + 1) * local] = get(6 + d)[...]
         start = pl.multiple_of(which * (width // 2), width // 2)
-        ref[:, at + width :] = attn_scr[:, pl.ds(start, width // 2)]
-    out_ref[...] = (middle + dot(get(2)[:, width:], w_down[...], 1, 0)).astype(bf16)
+        ref[:, width:] = attn_scr[:, pl.ds(start, width // 2)]
+    out_ref[...] = (middle + dot(get(2)[...], w_down[...], 1, 0)).astype(bf16)
 
 
 def ffn_backward(place, cot, middle, hidden, act, slope, gain, ctx, w_down, w_gate, w_up, w_out):
     tok, width = cot.shape
-    ff = w_gate.shape[1]
     local = width // groups
     return kernel_call(
         ffn_backward_body,
@@ -642,13 +666,8 @@
         [cot, middle, hidden, act, slope, gain, *ctx, w_down, w_gate, w_up, w_out],
         [shaped(bf16, tok, width), shaped(f32, tok, width), shaped(f32, 1, width)]
         + [shaped(bf16, tok, local)] * 4
-        + [shaped(bf16, tok, ff // 2 + width + width // 2)] * 2
-        + [shaped(bf16, tok, ff // 2), shaped(bf16, tok, ff // 2 + width + width // 2)],
-        scratch=[
-            pltpu.VMEM((tok, ff), bf16),
-            pltpu.VMEM((tok, ff), bf16),
-            pltpu.VMEM((tok, width), bf16),
-        ],
+        + [shaped(bf16, tok, width + width // 2)] * 2,
+        scratch=[pltpu.VMEM((tok, width), bf16)],
         mebibytes=6,
         us=6,
     )
@@ -663,91 +682,99 @@
         sent_ref[i, :, cols] = jnp.where(odd, even_rows, odd_rows).astype(bf16)
 
 
-def down_grad_body(smem, get, outs, left_scr, right_scr, total_scr, *, wide):
+def down_grad_body(smem, get, outs, cot_scr, hidden_scr, total_scr, *, wide):
     (place,) = smem
-    kept_ref, sent_ref = outs
-    core, odd = place[1], place[3] == 1
-    tok, half = get(4).shape
-    local = half // 2
+    kept_ref, sent_ref, gate_ref, up_ref, normed_scr = outs
+    odd = place[3] == 1
+    rows, quarter = hidden_scr.shape
+    tok = rows // 4
+    width = normed_scr.shape[1]
+    local = width // groups
     for i in range(4):
-        rows = slice(i * tok, (i + 1) * tok)
-        left_scr[rows, :] = get(i)[:, 2 * half :]
-        both = get(4 + i)[...]
-        right_scr[rows, :] = jnp.where(core == 0, both[:, :local], both[:, local:])
-    total_scr[...] = dot(left_scr[...], right_scr[...], 0, 0)
-    split_rows(total_scr, wide, odd, kept_ref, sent_ref, slice(None))
-
-
-def down_grad(place, lefts, rights, wide):
-    tok, half = rights[0].shape
-    ff = lefts[0].shape[1] - 2 * half
-    shape = (wide // 2, ff // wide, half // 2)
+        normed_scr[i * tok : (i + 1) * tok, :] = get(i)[...]
+        cot_scr[i * tok : (i + 1) * tok, :] = get(4 + i)[...]
+    start = pl.multiple_of((place[4] * 2 + place[1]) * quarter, quarter)
+    half = quarter // 2
+    for i in range(2):
+        cols = slice(i * half, (i + 1) * half)
+        part = pl.ds(pl.multiple_of(start + i * half, half), half)
+        up = dot(normed_scr[...], get(9)[:, part], 1, 0)
+        act, slope = gated(dot(normed_scr[...], get(8)[:, part], 1, 0), up)
+        hidden_scr[:, cols] = (act * up).astype(bf16)
+        hidden_grad = dot(cot_scr[...], get(10)[part, :], 1, 1)
+        gate_ref[:, cols] = (hidden_grad * slope).astype(bf16)
+        up_ref[:, cols] = (hidden_grad * act).astype(bf16)
+    total_scr[...] = dot(hidden_scr[...], cot_scr[...], 0, 0)
+    blocks = wide // groups
+    block = quarter // blocks
+    for i in range(wide // 2):
+        g, j = 2 * i // blocks, 2 * i % blocks
+        cols = slice(g * local, (g + 1) * local)
+        even_rows = total_scr[j * block : (j + 1) * block, cols]
+        odd_rows = total_scr[(j + 1) * block : (j + 2) * block, cols]
+        kept_ref[i] = jnp.where(odd, odd_rows, even_rows)
+        sent_ref[i] = jnp.where(odd, even_rows, odd_rows).astype(bf16)
+
+
+def down_grad(place, normed, cot, w_gate, w_up, w_down, wide):
+    tok, width = normed[0].shape
+    ff = w_gate.shape[1]
+    shape = (wide // 2, ff // wide, width // groups)
     return kernel_call(
         functools.partial(down_grad_body, wide=wide),
         "down_grad",
         [place],
-        [*lefts, *rights],
-        [shaped(f32, *shape), shaped(bf16, *shape)],
-        scratch=[
-            pltpu.VMEM((4 * tok, ff), bf16),
-            pltpu.VMEM((4 * tok, half // 2), bf16),
-            pltpu.VMEM((ff, half // 2), f32),
-        ],
-        mebibytes=6,
-        us=8,
-    )
-
-
-def gate_grad_body(smem, get, outs, left_scr, right_scr, total_scr, *, wide):
-    (place,) = smem
-    tok, width = left_scr.shape[0] // 4, left_scr.shape[1]
-    quarter = right_scr.shape[1]
-    for i in range(4):
-        rows = slice(i * tok, (i + 1) * tok)
-        left_scr[rows, :] = get(i)[:, :width]
-        at = quarter if i == 3 else 0
-        right_scr[rows, :] = get(4 + i)[:, at : at + quarter]
-    total_scr[...] = dot(left_scr[...], right_scr[...], 0, 0)
-    split_rows(total_scr, wide, place[3] == 1, *outs, slice(None))
-
-
-def gate_grad(place, lefts, rights, width, wide):
-    tok = lefts[0].shape[0]
-    quarter = rights[2].shape[1] // 2
-    shape = (wide // 2, width // wide, quarter)
-    return kernel_call(
-        functools.partial(gate_grad_body, wide=wide),
-        "gate_grad",
-        [place],
-        [*lefts, *rights],
-        [shaped(f32, *shape), shaped(bf16, *shape)],
+        [*normed, *cot, w_gate, w_up, w_down],
+        [shaped(f32, *shape), shaped(bf16, *shape)]
+        + [shaped(bf16, 4 * tok, ff // 4)] * 2
+        + [shaped(bf16, 4 * tok, width)],
         scratch=[
             pltpu.VMEM((4 * tok, width), bf16),
-            pltpu.VMEM((4 * tok, quarter), bf16),
-            pltpu.VMEM((width, quarter), f32),
+            pltpu.VMEM((4 * tok, ff // 4), bf16),
+            pltpu.VMEM((ff // 4, width), f32),
         ],
+        mebibytes=10,
+        us=1,
+    )
+
+
+def up_grad_body(smem, get, outs, total_scr, *, wide):
+    (place,) = smem
+    total_scr[...] = dot(get(0)[...], get(1)[...], 0, 0)
+    split_rows(total_scr, wide, place[3] == 1, *outs, slice(None))
+
+
+def up_grad(place, normed, grad, wide):
+    width = normed.shape[1]
+    quarter = grad.shape[1]
+    shape = (wide // 2, width // wide, quarter)
+    return kernel_call(
+        functools.partial(up_grad_body, wide=wide),
+        "up_grad",
+        [place],
+        [normed, grad],
+        [shaped(f32, *shape), shaped(bf16, *shape)],
+        scratch=[pltpu.VMEM((width, quarter), f32)],
         mebibytes=5,
-        us=2,
-    )
-
-
-def up_grad_body(
-    smem, get, outs, left_scr, right_scr, ctx_scr, attn_scr, total_scr, out_scr, *, wide
+        us=0.5,
+    )
+
+
+def gate_grad_body(
+    smem, get, outs, ctx_scr, attn_scr, total_scr, out_scr, *, wide
 ):
     (place,) = smem
     group, core, odd = place[0], place[1], place[3] == 1
-    tok, width = left_scr.shape[0] // 4, left_scr.shape[1]
+    rows, width = get(0).shape
+    tok = rows // 4
     local = width // groups
-    quarter = right_scr.shape[1]
+    quarter = total_scr.shape[1]
     for i in range(4):
         rows = slice(i * tok, (i + 1) * tok)
-        left_scr[rows, :] = get(i)[:, :width]
-        at = 0 if i == 2 else quarter
-        right_scr[rows, :] = get(4 + i)[:, at : at + quarter]
-        ctx_scr[rows, :] = get(4 + i)[:, 2 * quarter : 2 * quarter + width]
-        both = get(4 + i)[:, 2 * quarter + width :]
+        ctx_scr[rows, :] = get(2 + i)[:, :width]
+        both = get(2 + i)[:, width:]
         attn_scr[rows, :] = jnp.where(core == 0, both[:, :local], both[:, local:])
-    total_scr[...] = dot(left_scr[...], right_scr[...], 0, 0)
+    total_scr[...] = dot(get(0)[...], get(1)[...], 0, 0)
     split_rows(total_scr, wide, odd, *outs, slice(0, quarter))
     turned = dot(ctx_scr[...], attn_scr[...], 0, 0)
     for d in range(4):
@@ -756,27 +783,25 @@
     split_rows(out_scr, wide, odd, *outs, slice(quarter, quarter + local))
 
 
-def up_grad(place, lefts, rights, width, wide):
-    tok = lefts[0].shape[0]
-    quarter = (rights[0].shape[1] - width - width // 2) // 2
+def gate_grad(place, normed, grad, attn, wide):
+    rows, width = normed.shape
+    quarter = grad.shape[1]
     local = width // groups
     shape = (wide // 2, width // wide, quarter + local)
     return kernel_call(
-        functools.partial(up_grad_body, wide=wide),
-        "up_grad",
+        functools.partial(gate_grad_body, wide=wide),
+        "gate_grad",
         [place],
-        [*lefts, *rights],
+        [normed, grad, *attn],
         [shaped(f32, *shape), shaped(bf16, *shape)],
         scratch=[
-            pltpu.VMEM((4 * tok, width), bf16),
-            pltpu.VMEM((4 * tok, quarter), bf16),
-            pltpu.VMEM((4 * tok, width), bf16),
-            pltpu.VMEM((4 * tok, local), bf16),
+            pltpu.VMEM((rows, width), bf16),
+            pltpu.VMEM((rows, local), bf16),
             pltpu.VMEM((width, quarter), f32),
             pltpu.VMEM((width, local), f32),
         ],
         mebibytes=8,
-        us=3,
+        us=0.5,
     )
 
 
@@ -797,8 +822,28 @@
         [],
         [*dq, kept, received],
         [shaped(bf16, tok, 3 * local)] * 4,
-        us=2,
-    )
+        staged=tuple(range(6)),
+        us=0.5,
+    )
+
+
+def exact(small):
+    high = small.astype(bf16)
+    return high, (small - high.astype(f32)).astype(bf16)
+
+
+def attach(ref, rows, small):
+    high, low = exact(small)
+    ref[rows : rows + small.shape[0], : small.shape[1]] = high
+    ref[rows : rows + small.shape[0], small.shape[1] : 2 * small.shape[1]] = low
+
+
+def attached(ref, rows, small):
+    count, lanes = small.shape
+    high, low = exact(small)
+    theirs = ref[rows : rows + count, :lanes].astype(f32)
+    theirs = theirs + ref[rows : rows + count, lanes : 2 * lanes].astype(f32)
+    return high.astype(f32) + low.astype(f32) + theirs
 
 
 def qkv_grad_body(smem, get, outs, grad_scr, total_scr):
@@ -810,12 +855,14 @@
     tok = grad_scr.shape[0] // 4
     for d in range(4):
         grad_scr[d * tok : (d + 1) * tok, :] = get(d)[...]
-    total_scr[...] = dot(get(4)[...], grad_scr[...], 0, 0)
+    total_scr[...] = dot(get(4)[...], grad_scr[: 3 * tok, :], 0, 0)
+    total_scr[...] += dot(get(11)[...], grad_scr[3 * tok :, :], 0, 0)
     quarter = width // 4
     for i in range(2):
-        for ref, which in ((sent_ref, 1 - core), (kept_ref, core)):
-            start = pl.multiple_of((2 * i + which) * quarter, quarter)
-            ref[i] = total_scr[pl.ds(start, quarter), :].astype(ref.dtype)
+        start = pl.multiple_of((2 * i + core) * quarter, quarter)
+        kept_ref[i] = total_scr[pl.ds(start, quarter), :]
+        start = pl.multiple_of((2 * i + 1 - core) * quarter, quarter)
+        sent_ref[i * quarter : (i + 1) * quarter, :] = total_scr[pl.ds(start, quarter), :].astype(bf16)
     window, late = group_window(group, local)
     ones = jnp.ones((8, local), bf16)
     gain_grad = jnp.zeros((8, width), f32)
@@ -823,8 +870,7 @@
         both = get(8 + i)[:, pl.ds(window, -(-local // 128) * 128)]
         weight = jnp.where(late, both[:, both.shape[1] - local :], both[:, :local])
         product = total_scr[:, i * local : (i + 1) * local] * weight.astype(f32)
-        high = product.astype(bf16)
-        rest = (product - high.astype(f32)).astype(bf16)
+        high, rest = exact(product)
         gain_grad = gain_grad + dot(ones, high, 1, 1) + dot(ones, rest, 1, 1)
     gain_grad = gain_grad[0:1] / get(5)[...]
     ffn_gain = get(6)[...]
@@ -838,28 +884,91 @@
     for i in range(groups):
         at = 2 * rows + i * heads
         small_ref[at : at + heads, :] = jnp.where(group == i, table, 0.0)
-
-
-def qkv_grad(place, grads, normed, gain, gain_grad, table, head_count, w_query, w_key, w_value):
-    rows, width = normed.shape
+    sent_ref[2 * quarter :, :] = jnp.zeros((sent_ref.shape[0] - 2 * quarter, span), bf16)
+    attach(sent_ref, 2 * quarter, small_ref[...])
+
+
+def room(count):
+    return -(-count // 16) * 16
+
+
+def qkv_grad(
+    place, grads, normed_first, normed_last, gain, gain_grad, table, head_count, w_query, w_key, w_value
+):
+    rows, width = 4 * grads[0].shape[0], normed_first.shape[1]
     span = grads[0].shape[1]
+    count = 2 * width // 128 + head_count
     return kernel_call(
         qkv_grad_body,
         "qkv_grad",
         [place],
-        [*grads, normed, gain, gain_grad, table, w_query, w_key, w_value],
+        [*grads, normed_first, gain, gain_grad, table, w_query, w_key, w_value, normed_last],
         [
             shaped(f32, 2, width // 4, span),
-            shaped(bf16, 2, width // 4, span),
-            shaped(f32, 2 * width // 128 + head_count, 128),
+            shaped(bf16, width // 2 + room(count), span),
+            shaped(f32, count, 128),
         ],
         scratch=[pltpu.VMEM((rows, span), bf16), pltpu.VMEM((width, span), f32)],
         mebibytes=7,
-        us=4,
-    )
-
-
-def input_grad_body(smem, get, outs):
+        us=0.5,
+    )
+
+
+def qkv_sum_body(smem, get, outs, *, axis):
+    (place,) = smem
+    kept, small, received = get(0), get(1), get(2)
+    parts, rows, span = kept.shape
+    totals = [
+        kept[i] + received[i * rows : (i + 1) * rows, :].astype(f32) for i in range(parts)
+    ]
+    summed = attached(received, parts * rows, small[...])
+    if axis == "y":
+        for i in range(parts):
+            outs[0][i] = totals[i].astype(outs[0].dtype)
+        outs[1][...] = summed
+        return
+    kept_ref, sent_ref, small_ref = outs
+    small_ref[...] = summed
+    if axis == "core":
+        far = place[4] == 1
+        mine, theirs = jnp.where(far, totals[1], totals[0]), jnp.where(far, totals[0], totals[1])
+        blocks, block = kept_ref.shape[0], kept_ref.shape[1]
+        for i in range(blocks):
+            kept_ref[i] = mine[i * block : (i + 1) * block]
+        sent_ref[:rows, :] = theirs.astype(bf16)
+    else:
+        odd = place[3] == 1
+        for i in range(parts // 2):
+            kept_ref[i] = jnp.where(odd, totals[2 * i + 1], totals[2 * i])
+            theirs = jnp.where(odd, totals[2 * i], totals[2 * i + 1])
+            sent_ref[i * rows : (i + 1) * rows, :] = theirs.astype(bf16)
+    filled = sent_ref.shape[0] - room(small.shape[0])
+    sent_ref[filled:, :] = jnp.zeros((room(small.shape[0]), span), bf16)
+    attach(sent_ref, filled, summed)
+
+
+def qkv_sum(place, kept, small, received, axis, s_count, wide):
+    parts, rows, span = kept.shape
+    count = small.shape[0]
+    if axis == "core":
+        shape, sent = (2 * s_count, rows // (2 * s_count), span), rows
+    else:
+        shape, sent = (parts // 2, rows, span), parts // 2 * rows
+    if axis == "y":
+        outputs = [shaped(bf16 if s_count == 1 else f32, *kept.shape)]
+    else:
+        outputs = [shaped(f32, *shape), shaped(bf16, sent + room(count), span)]
+    return kernel_call(
+        functools.partial(qkv_sum_body, axis=axis),
+        f"qkv_sum_{axis}",
+        [place],
+        [kept, small, received],
+        outputs + [shaped(f32, count, 128)],
+        us=0.5,
+    )
+
+
+def input_grad_body(smem, get, outs, all_scr):
     (place,) = smem
     group = place[0]
     weights = [get(7 + i) for i in range(3)]
@@ -867,7 +976,7 @@
     window = -(-local // 128) * 128
     tok = get(0).shape[0]
     spare = jnp.zeros((tok, window - local), bf16)
-    normed_grad = None
+    all_scr[...] = jnp.zeros_like(all_scr)
     for d in range(4):
         start, late = group_window(group ^ d, local)
         grads = get(d)[...]
@@ -878,8 +987,10 @@
                 jnp.concatenate([spare, part], axis=1),
                 jnp.concatenate([part, spare], axis=1),
             )
-            product = dot(part, weights[i][:, pl.ds(start, window)], 1, 1)
-            normed_grad = product if normed_grad is None else normed_grad + product
+            all_scr[i, :, pl.ds(start, window)] += part
+    normed_grad = dot(all_scr[0], weights[0][...], 1, 1)
+    for i in range(1, 3):
+        normed_grad = normed_grad + dot(all_scr[i], weights[i][...], 1, 1)
     values = get(4)[...].astype(f32)
     scale = rms_scale(values)
     unit = values * scale
@@ -896,9 +1007,10 @@
         [place],
         [*grads, tokens, gain, middle_grad, w_query, w_key, w_value],
         [shaped(f32, *tokens.shape)],
+        scratch=[pltpu.VMEM((3, *tokens.shape), bf16)],
         staged=(0, 1, 2, 3, 4, 6),
         mebibytes=6,
-        us=4,
+        us=0.5,
     )[0]
 
 
@@ -909,7 +1021,7 @@
         total = kept[0].astype(f32) + received[0].astype(f32)
         at = 0
         for i, span in enumerate(splits):
-            outs[i][...] = total[:, at : at + span]
+            outs[i][...] = total[:, at : at + span].astype(outs[i].dtype)
             at += span
         return
     odd = ((place[5] >> bit) & 1) == 1
@@ -920,12 +1032,12 @@
         outs[0][i] = jnp.where(odd, odd_rows, even_rows)
 
 
-def wide_sum(layout, place, kept, sent, bit, splits, name, us, first=()):
+def wide_sum(layout, place, kept, sent, bit, splits, name, us, first=(), last=f32):
     received = layout.wide_bit(sent, bit)
     kept = after(kept, first)
     remaining, block, columns = kept.shape
     if remaining == 1:
-        outputs = [shaped(f32, block, span) for span in splits]
+        outputs = [shaped(last, block, span) for span in splits]
     else:
         shape = (remaining // 2, block, columns)
         outputs = [shaped(f32, *shape), shaped(bf16, *shape)]
@@ -937,6 +1049,16 @@
         outputs,
         us=us,
     )
+
+
+def turned_down_body(smem, get, outs):
+    outs[0][...] = jnp.transpose(get(0)[...].astype(f32))
+
+
+def turned_down(block):
+    return kernel_call(
+        turned_down_body, "down_out", [], [block], [shaped(f32, *block.shape[::-1])], us=1
+    )[0]
 
 
 def after(values, done):
@@ -992,67 +1114,59 @@
         while size < s_count:
             own[d] = jnp.concatenate([own[d], layout.wide_bit(own[d], size.bit_length())], axis=0)
             size *= 2
+    cot_across = layout.across(out_grad)
     bias = bias_rows(place, bias_table, 4 * tok)
-    own = after(own, bias)
-    other = [layout.core(block) for block in own]
-
-    def half_cols(block, which):
-        return lax.dynamic_slice_in_dim(block, which * (block.shape[1] // 2), block.shape[1] // 2, 1)
-
-    cot_own = half_cols(out_grad, across)
-    cot_across = layout.across(half_cols(out_grad, 1 - across))
-    cot_parts = [cot_own, layout.core(cot_own), cot_across, layout.core(cot_across)]
-
-    outs = attention_forward(
-        place, own, other, bias, gain_attn, w_query, w_key, w_value
-    )
+    kv_first, q_first, normed_first = project(place, own[:3], gain_attn, w_query, w_key, w_value)
+    kv_first = after(kv_first, (bias, cot_across))
+    kv_last, q_last, normed_last = project(place, own[3:], gain_attn, w_query, w_key, w_value)
+    kv = [kv_first, kv_last, layout.core(kv_first), layout.core(kv_last)]
+    outs = attention_forward(place, kv, [q_first, q_last], bias)
     ctx_parts = outs[:4]
-    q_own, k_all, v_all, o_own, normed_own, probs = outs[4:]
+    q_own, k_all, v_all, o_own, probs = outs[4:]
     ctx = [layout.turned(ctx_parts[d], d) for d in range(4)]
-    ctx = after(ctx, cot_parts)
-
-    middle, left, act, slope = ffn_forward(place, ctx, tokens, gain_ffn, w_out, w_gate, w_up)
-    left_across = layout.across(left)
-    left_core = layout.core(left)
+    cot = [out_grad, layout.core(out_grad), cot_across, layout.core(cot_across)]
+    ctx = after(ctx, cot)
+
+    middle, normed_ffn, hidden, act, slope = ffn_forward(
+        place, ctx, tokens, gain_ffn, w_out, w_gate, w_up
+    )
+    normed_across = layout.across(normed_ffn)
     back = ffn_backward(
-        place, out_grad, middle, left, act, slope, gain_ffn, ctx, w_down, w_gate, w_up, w_out
+        place, out_grad, middle, hidden, act, slope, gain_ffn, ctx, w_down, w_gate, w_up, w_out
     )
     output, middle_grad, grad_gain_ffn = back[0:3]
     dctx = [layout.turned(back[3 + d], d) for d in range(4)]
-    mine, near, far_gate, far_up = back[7:11]
-    near = layout.core(near)
-    far_gate = layout.across(far_gate)
-    far_up = layout.across(far_up)
-    dctx = after(dctx, left_across)
-
+    mine, far = back[7:9]
+    normed_near, normed_across = after((normed_ffn, normed_across), back[3:7])
+    normed_core = layout.core(normed_near)
+    normed = [normed_ffn, normed_core, normed_across, layout.core(normed_across)]
+    *down, gate, up, normed = down_grad(place, normed, cot, w_gate, w_up, w_down, layout.wide)
+
+    dctx = after(dctx, down)
     back = attention_backward(place, dctx, q_own, k_all, v_all, o_own, probs)
     dq, kept, sent, table_rows = back[:4], back[4], back[5], back[6]
     received = layout.core(sent)
-    left_across = after(left_across, sent)
-    lefts = [left, left_core, left_across, layout.core(left_across)]
-    down_kept, down_sent = down_grad(place, lefts, cot_parts, layout.wide)
     size = s_count
     while size > 1:
         size //= 2
         total = kept.astype(f32) + received.astype(f32)
         kept = total[:size]
         received = layout.wide_bit(total[size:].astype(bf16), size.bit_length())
-    received = after(received, down_sent)
-    low_grads = collect(dq, kept[0], received[0])
-    returned = [layout.turned(low_grads[d], d) for d in range(4)]
-
-    far_gate = after(far_gate, down_sent)
-    far_gate_both = layout.core(far_gate)
-    lefts = after(lefts, low_grads)
-    gate_kept, gate_sent = gate_grad(
-        place, lefts, [mine, near, far_gate, far_gate_both], width, layout.wide
-    )
-    normed_own = after(normed_own, gate_sent)
-
+
+    far, mine, up = after((far, mine, up), sent)
+    far = layout.across(far)
+    mine_core = layout.core(mine)
+    up = up_grad(place, normed, up, layout.wide)
+    quarter_ff = ff // layout.narrow
+    bits = layout.wide.bit_length() - 1
+    width_sum = functools.partial(wide_sum, layout, place)
+    down = width_sum(*down, 0, (local,), "down", 0.5, up, last=bf16)
+    low_grads = collect(dq, after(kept[0], down), received[0])
     qkv_kept, qkv_sent, small = qkv_grad(
         place,
         low_grads,
-        normed_own,
+        normed_first,
+        normed_last,
         gain_attn,
         grad_gain_ffn,
         table_rows,
@@ -1061,17 +1175,38 @@
         w_key,
         w_value,
     )
-    far_up = after(far_up, qkv_sent)
-    far_up_both = layout.core(far_up)
-    up_kept, up_sent = up_grad(place, lefts, [mine, near, far_up, far_up_both], width, layout.wide)
-
+    up = width_sum(*up, 0, (quarter_ff,), "up", 0.5, qkv_sent)
+    far = after(far, low_grads)
+    outs_parts = [mine, mine_core, far, layout.core(far)]
+    normed = after(normed, up[0])
+    gate = gate_grad(place, normed, gate, outs_parts, layout.wide)
+    low_grads = after(low_grads, gate[1])
+    returned = [layout.turned(low_grads[d], d) for d in range(4)]
+    down = width_sum(*down, 1, (local,), "down", 0.5, gate, last=bf16)
+    step = qkv_sum(
+        place, after(qkv_kept, down), small, layout.core(qkv_sent), "core", s_count, layout.wide
+    )
+    up = width_sum(*up, 1, (quarter_ff,), "up", 0.5, step)
+    for bit in range(2, bits):
+        down = width_sum(*down, bit, (local,), "down", 0.5, up, last=bf16)
+    step = qkv_sum(
+        place, after(step[0], down), step[2], layout.across(step[1]), "x", s_count, layout.wide
+    )
+    gate = width_sum(*gate, 0, (quarter_ff, local), "gate", 0.5, step)
+    middle_grad = after(middle_grad, gate)
+    input_grad = final_input_grad(
+        place, returned, tokens, gain_attn, middle_grad, w_query, w_key, w_value
+    )
+    for bit in range(2, bits):
+        up = width_sum(*up, bit, (quarter_ff,), "up", 0.5, input_grad)
+    part, small = qkv_sum(
+        place, after(step[0], up), step[2], layout.wide_bit(step[1], 0), "y", s_count, layout.wide
+    )
+    gate = width_sum(*gate, 1, (quarter_ff, local), "gate", 0.5, part)
+    small = after(small, gate[0])
+    for bit in range(2, bits):
+        gate = width_sum(*gate, bit, (quarter_ff, local), "gate", 0.5, part)
     rows = width // layout.wide
-    part = qkv_kept + layout.core(qkv_sent).astype(f32)
-    part = part.reshape(2, s_count, 2, rows, 3 * local)
-    kept, sent = halved(part, 0, across)
-    part = kept + layout.across(sent.astype(bf16)).astype(f32)
-    kept, sent = halved(part, 1, y_own)
-    part = kept + layout.wide_bit(sent.astype(bf16), 0).astype(f32)
     size = s_count
     bit = 1
     while size > 1:
@@ -1081,32 +1216,20 @@
         part = kept + layout.wide_bit(sent.astype(bf16), bit).astype(f32)
         bit += 1
     part = part.reshape(rows, 3 * local).astype(bf16)
-    final_qkv = layout.send(part, lambda x, c, g, s, y: (g // 2, g % 2, x * 2 + c, s, y)).astype(f32)
-
-    input_grad = final_input_grad(
-        place, returned, tokens, gain_attn, middle_grad, w_query, w_key, w_value
-    )
-    quarter_ff = ff // layout.narrow
-    bits = layout.wide.bit_length() - 1
-    down, gate, up = (down_kept, down_sent), (gate_kept, gate_sent), (up_kept, up_sent)
-    for bit in range(bits):
-        down = wide_sum(layout, place, *down, bit, (local,), "down", 6)
-        gate = wide_sum(layout, place, *gate, bit, (quarter_ff,), "gate", 8)
-        first = returned if bit == 0 else (input_grad, down, gate) if bit == bits - 1 else ()
-        up = wide_sum(layout, place, *up, bit, (quarter_ff, local), "up", 12, first)
-        if bit == 0:
-            small = after(small, up)
-    (final_down,), (final_gate,), (final_up, final_out) = down, gate, up
-
-    for bit in range(bits):
+
+    def to_owner(x, c, g, s, y):
+        return (g // 2, g % 2, x * 2 + c, s, y)
+
+    final_qkv = layout.send(part, to_owner).astype(f32)
+    final_down = turned_down(layout.send(down[0], to_owner)).T
+    (final_up,), (final_gate, final_out) = up, gate
+
+    for bit in range(1, bits):
         small = small + layout.wide_bit(small, bit)
-    small = small + layout.across(small)
-    small = small + layout.core(small)
     gain_rows = width // 128
     sum_gain_attn = small[:gain_rows].reshape(width)
     sum_gain_ffn = small[gain_rows : 2 * gain_rows].reshape(width)
     sum_table = small[2 * gain_rows :, :bucket_count].T
-
     return (
         output[None],
         input_grad[None],

time: 198 us -> 162 us (0.82)
  starting transfers between devices: 67.1 us -> 51.8 us
  local copies, waits for them, and re-layouts: 16 us -> 2.19 us
  waiting for transfers between devices: 54.9 us -> 47.3 us
  Pallas kernels: 53.5 us -> 56.6 us
    ppermute x50 -> x44, starting transfers between devices: 67.1 us -> 51.8 us  [send(): return lax.ppermute(block, axes, route)]
    unnamed x90 -> x25, local copies, waits for them, and re-layouts: 13.9 us -> 0.14 us
    ppermute x50 -> x44, waiting for transfers between devices: 54.9 us -> 47.3 us  [send(): return lax.ppermute(block, axes, route)]
    pallas_call x21 -> x27, Pallas kernels: 53.5 us -> 56.6 us  [kernel_call(): pl.pallas_call(kernel, out_shape=outputs, in_specs=[pl.BlockSpec(memory_s...]
  transfers between devices with their start and end apart: 50 -> 44, of which waited for: 18 -> 16; matrix products, arithmetic and copies ran while one was open for 2% -> 1% of each run, Pallas kernels for 25% -> 32%
where the time goes in v1:
time: 162 us; the launch traced here: 159 us
  Pallas kernels  56.6 us (35%)
  starting transfers between devices  51.8 us (32%)
  waiting for transfers between devices  47.3 us (29%)
  local copies, waits for them, and re-layouts  2.19 us (1%)
    pallas_call x27, Pallas kernels, kernel_call(): pl.pallas_call(kernel, out_shape=outputs, in_specs=[pl.BlockSpec(memory_s...  56.6 us
    ppermute x44, starting transfers between devices, send(): return lax.ppermute(block, axes, route)  51.8 us
    ppermute x44, waiting for transfers between devices, send(): return lax.ppermute(block, axes, route)  47.3 us
  transfers between devices with their start and end apart: 44, of which 16 were waited for; matrix products, arithmetic and copies ran while one was open for 1% of the time, Pallas kernels for 32%

profile of v1, /device:TPU:2, one launch (start us, length us, event | category | flops | bytes accessed | tf_op | source)
XLA Modules:
  0.0 159.0 jit_solution(5895353400265358496)
XLA Ops:
  0.7 1.7 %pack.1 = bf16[144,768]{1,0:T(8,128)(2,1)} custom-call(bf16[128,768]{1,0:T(8,128)(2,1)} %bitcast.22, s32[1,128]{1,0:T(1,128)} %refs_1_.2), custom_call_target="tpu_custom_call" | custom-call | flops 1150000000 | bytes 1024 | tf_op jit(solution)/shard_map/pack/pallas_call | solution.py:123
  2.4 2.7 %collective-permute-start.2 = (bf16[144,768]{1,0:T(8,128)(2,1)}, bf16[144,768]{1,0:T(8,128)(2,1)S(1)}, u32[]{:S(2)}, u32[]{:S(2)}) collective-permute-start(bf16[144,768]{1,0:T(8,128)(2,1)} %pack.1), channel_id=1, source_target_pairs={{0,4},{1,12},{2,6},{3,14},{4,0},{5,8},{6,2},{7,10},{8,5},{9,13},{1... | collective-permute-start | bytes 663560 | tf_op jit(solution)/shard_map/ppermute | solution.py:46
  9.8 6.6 %collective-permute-done.2 = bf16[144,768]{1,0:T(8,128)(2,1)S(1)} collective-permute-done((bf16[144,768]{1,0:T(8,128)(2,1)}, bf16[144,768]{1,0:T(8,128)(2,1)S(1)}, u32[]{:S(2)}, u32[]{:S(2)}) %collective-permute-start.2) | collective-permute-done | bytes 221216 | tf_op jit(solution)/shard_map/ppermute | solution.py:46
  17.4 2.2 %project.2 = (bf16[3,1,128,512]{3,2,1,0:T(8,128)(2,1)S(1)}, bf16[3,128,192]{2,1,0:T(8,128)(2,1)S(1)}, bf16[384,768]{1,0:T(8,128)(2,1)S(1)}) custom-call(s32[6]{0:T(128)S(1)} %stack.24.refs_0_, bf16[1,144,768]{2,1,0:T(8,128)(2,1)S(1)} %bitcast.33, bf16[1,144,768]{2,1,0:T(8,128)(2,1)S(1)} %bitcast.32, bf16[1,144,768]{2,1,0:T(8,128)(2,1)S(1)} %bitcast.31, ...), custom_call_target="tpu_custom_call" | custom-call | flops 3449999872 | bytes 1024 | tf_op jit(solution)/shard_map/project/pallas_call | solution.py:123
  19.8 3.9 %collective-permute-done.4.refs_1_ = bf16[1,144,768]{2,1,0:T(8,128)(2,1)S(1)} collective-permute-done((bf16[1,144,768]{2,1,0:T(8,128)(2,1)S(1)}, bf16[1,144,768]{2,1,0:T(8,128)(2,1)S(1)}, u32[]{:S(2)}, u32[]{:S(2)}) %collective-permute-start.4) | collective-permute-done | bytes 221216 | tf_op jit(solution)/shard_map/ppermute | solution.py:46
  23.7 1.8 %project.3 = (bf16[1,1,128,512]{3,2,1,0:T(8,128)(2,1)S(1)}, bf16[1,128,192]{2,1,0:T(8,128)(2,1)S(1)}, bf16[128,768]{1,0:T(8,128)(2,1)S(1)}) custom-call(s32[6]{0:T(128)S(1)} %stack.24.refs_0_, bf16[1,144,768]{2,1,0:T(8,128)(2,1)S(1)} %collective-permute-done.4.refs_1_, f32[1,768]{1,0:T(1,128)S(1)} %broadcast_in_dim.24.refs_4_.refs_2_.refs_6_, ...), custom_call_target="tpu_custom_call" | custom-call | flops 3449999872 | bytes 1024 | tf_op jit(solution)/shard_map/project/pallas_call | solution.py:123
  27.0 9.9 %attention_forward.1 = (bf16[128,192]{1,0:T(8,128)(2,1)S(1)}, bf16[128,192]{1,0:T(8,128)(2,1)S(1)}, bf16[128,192]{1,0:T(8,128)(2,1)S(1)}, bf16[128,192]{1,0:T(8,...) custom-call(s32[6]{0:T(128)S(1)} %stack.24.refs_0_, ...), custom_call_target="tpu_custom_call" | custom-call | flops 11500000256 | bytes 1024 | tf_op jit(solution)/shard_map/attention_forward/pallas_call | solution.py:123
  38.9 2.8 %collective-permute-start.9 = (bf16[128,192]{1,0:T(8,128)(2,1)S(1)}, bf16[128,192]{1,0:T(8,128)(2,1)S(1)}, u32[]{:S(2)}, u32[]{:S(2)}) collective-permute-start(bf16[128,192]{1,0:T(8,128)(2,1)S(1)} %get-tuple-element.128), channel_id=1, source_target_pairs={{0,4},{1,12},{2,6},{3,14},{4,0},{5,8},{6,2},{7,10},{8,5},{9,13},{1... | collective-permute-start | bytes 147464 | tf_op jit(solution)/shard_map/ppermute | solution.py:46
  42.2 2.6 %collective-permute-done.9.refs_3_.refs_9_ = bf16[128,192]{1,0:T(8,128)(2,1)S(1)} collective-permute-done((bf16[128,192]{1,0:T(8,128)(2,1)S(1)}, bf16[128,192]{1,0:T(8,128)(2,1)S(1)}, u32[]{:S(2)}, u32[]{:S(2)}) %collective-permute-start.9) | collective-permute-done | bytes 49184 | tf_op jit(solution)/shard_map/ppermute | solution.py:46
  44.7 3.0 %collective-permute-done.10.refs_4_.refs_10_ = bf16[128,192]{1,0:T(8,128)(2,1)S(1)} collective-permute-done((bf16[128,192]{1,0:T(8,128)(2,1)S(1)}, bf16[128,192]{1,0:T(8,128)(2,1)S(1)}, u32[]{:S(2)}, u32[]{:S(2)}) %collective-permute-start.10) | collective-permute-done | bytes 49184 | tf_op jit(solution)/shard_map/ppermute | solution.py:46
  47.8 3.1 %ffn_forward.1 = (f32[128,768]{1,0:T(8,128)S(1)}, bf16[128,768]{1,0:T(8,128)(2,1)S(1)}, bf16[128,2048]{1,0:T(8,128)(2,1)S(1)}, f32[128,2048]{1,0:T(8,128)S(1)}, f32[128,2048]{1,0:T(8,128)S(1)}) custom-call(s32[6]{0:T(128)S(1)} %stack.24.refs_0_, bf16[128,192]{1,0:T(8,128)(2,1)S(1)} %collective-permute-done.7.refs_1_.refs_7_, ...), custom_call_target="tpu_custom_call" | custom-call | flops 16099999744 | bytes 1024 | tf_op jit(solution)/shard_map/ffn_forward/pallas_call | solution.py:123
  51.6 5.5 %ffn_backward.1 = (bf16[128,768]{1,0:T(8,128)(2,1)}, f32[128,768]{1,0:T(8,128)S(1)}, f32[1,768]{1,0:T(1,128)S(1)}, bf16[128,192]{1,0:T(8,128)(2,1)S(1)}, bf16[12...) custom-call(s32[6]{0:T(128)S(1)} %stack.24.refs_0_, ...), custom_call_target="tpu_custom_call" | custom-call | flops 6899999744 | bytes 1024 | tf_op jit(solution)/shard_map/ffn_backward/pallas_call | solution.py:123
  57.1 2.8 %collective-permute-start.18 = (bf16[128,768]{1,0:T(8,128)(2,1)S(1)}, bf16[128,768]{1,0:T(8,128)(2,1)S(1)}, u32[]{:S(2)}, u32[]{:S(2)}) collective-permute-start(bf16[128,768]{1,0:T(8,128)(2,1)S(1)} %get-tuple-element.144.refs_1_), channel_id=1, source_target_pairs={{0,8},{1,9},{2,10},{3,11},{4,12},{5,13},{6,14},{7,15},{8,0},{9,1},... | collective-permute-start | bytes 589832 | tf_op jit(solution)/shard_map/ppermute | solution.py:46
  61.7 3.3 %collective-permute-start.16 = (bf16[128,192]{1,0:T(8,128)(2,1)S(1)}, bf16[128,192]{1,0:T(8,128)(2,1)S(1)}, u32[]{:S(2)}, u32[]{:S(2)}) collective-permute-start(bf16[128,192]{1,0:T(8,128)(2,1)S(1)} %get-tuple-element.142), channel_id=1, source_target_pairs={{0,6},{1,14},{2,4},{3,12},{4,2},{5,10},{6,0},{7,8},{8,7},{9,15},{1... | collective-permute-start | bytes 147464 | tf_op jit(solution)/shard_map/ppermute | solution.py:46
  65.0 2.8 %down_grad.1 = (f32[4,256,192]{2,1,0:T(8,128)S(1)}, bf16[4,256,192]{2,1,0:T(8,128)(2,1)S(1)}, bf16[512,512]{1,0:T(8,128)(2,1)S(1)}, bf16[512,512]{1,0:T(8,128)(2,1)S(1)}, bf16[512,768]{1,0:T(8,128)(2,1)S(1)}) custom-call(s32[6]{0:T(128)S(1)} %stack.24.refs_0_, bf16[128,768]{1,0:T(8,128)(2,1)S(1)} %get-tuple-element.144.refs_1_, ...), custom_call_target="tpu_custom_call" | custom-call | flops 1150000000 | bytes 1024 | tf_op jit(solution)/shard_map/down_grad/pallas_call | solution.py:123
  67.8 4.7 %collective-permute-start.20 = (bf16[4,256,192]{2,1,0:T(8,128)(2,1)S(1)}, bf16[4,256,192]{2,1,0:T(8,128)(2,1)S(1)}, u32[]{:S(2)}, u32[]{:S(2)}) collective-permute-start(bf16[4,256,192]{2,1,0:T(8,128)(2,1)S(1)} %get-tuple-element.147), channel_id=1, source_target_pairs={{0,1},{1,0},{2,3},{3,2},{4,5},{5,4},{6,7},{7,6},{8,9},{9,8},{10,11... | collective-permute-start | bytes 1179656 | tf_op jit(solution)/shard_map/ppermute | solution.py:46
  72.5 8.2 %attention_backward.1 = (bf16[128,192]{1,0:T(8,128)(2,1)S(1)}, bf16[128,192]{1,0:T(8,128)(2,1)S(1)}, bf16[128,192]{1,0:T(8,128)(2,1)S(1)}, bf16[128,192]{1,0:T(8...) custom-call(s32[6]{0:T(128)S(1)} %stack.24.refs_0_, ...), custom_call_target="tpu_custom_call" | custom-call | flops 8049999872 | bytes 1024 | tf_op jit(solution)/shard_map/attention_backward/pallas_call | solution.py:123
  86.9 3.3 %collective-permute-done.24.refs_5_ = bf16[128,1152]{1,0:T(8,128)(2,1)S(1)} collective-permute-done((bf16[128,1152]{1,0:T(8,128)(2,1)S(1)}, bf16[128,1152]{1,0:T(8,128)(2,1)S(1)}, u32[]{:S(2)}, u32[]{:S(2)}) %collective-permute-start.24) | collective-permute-done | bytes 294944 | tf_op jit(solution)/shard_map/ppermute | solution.py:46
  90.2 2.6 %qkv_grad.1 = (f32[2,192,576]{2,1,0:T(8,128)S(1)}, bf16[416,576]{1,0:T(8,128)(2,1)S(1)}, f32[24,128]{1,0:T(8,128)S(1)}) custom-call(s32[6]{0:T(128)S(1)} %stack.24.refs_0_, bf16[128,576]{1,0:T(8,128)(2,1)S(1)} %get-tuple-element.191.refs_1_, bf16[128,576]{1,0:T(8,128)(2,1)S(1)} %get-tuple-element.192.refs_2_, ...), custom_call_target="tpu_custom_call" | custom-call | flops 575000000 | bytes 1024 | tf_op jit(solution)/shard_map/qkv_grad/pallas_call | solution.py:123
  97.8 4.7 %collective-permute-done.30.refs_2_ = bf16[2,256,192]{2,1,0:T(8,128)(2,1)S(1)} collective-permute-done((bf16[2,256,192]{2,1,0:T(8,128)(2,1)S(1)}, bf16[2,256,192]{2,1,0:T(8,128)(2,1)S(1)}, u32[]{:S(2)}, u32[]{:S(2)}) %collective-permute-start.30) | collective-permute-done | bytes 196640 | tf_op jit(solution)/shard_map/ppermute | solution.py:46
  106.6 2.1 %collective-permute-start.27 = (bf16[128,576]{1,0:T(8,128)(2,1)S(1)}, bf16[128,576]{1,0:T(8,128)(2,1)S(1)}, u32[]{:S(2)}, u32[]{:S(2)}) collective-permute-start(bf16[128,576]{1,0:T(8,128)(2,1)S(1)} %get-tuple-element.192.refs_2_), channel_id=1, source_target_pairs={{0,2},{1,10},{2,0},{3,8},{4,6},{5,14},{6,4},{7,12},{8,3},{9,11},{1... | collective-permute-start | bytes 442376 | tf_op jit(solution)/shard_map/ppermute | solution.py:46
  109.3 3.4 %collective-permute-done.33.refs_2_ = bf16[1,256,192]{2,1,0:T(8,128)(2,1)S(1)} collective-permute-done((bf16[1,256,192]{2,1,0:T(8,128)(2,1)S(1)}, bf16[1,256,192]{2,1,0:T(8,128)(2,1)S(1)}, u32[]{:S(2)}, u32[]{:S(2)}) %collective-permute-start.33) | collective-permute-done | bytes 98336 | tf_op jit(solution)/shard_map/ppermute | solution.py:46
  113.3 2.0 %collective-permute-start.29 = (bf16[128,576]{1,0:T(8,128)(2,1)S(1)}, bf16[128,576]{1,0:T(8,128)(2,1)S(1)}, u32[]{:S(2)}, u32[]{:S(2)}) collective-permute-start(bf16[128,576]{1,0:T(8,128)(2,1)S(1)} %get-tuple-element.194.refs_4_), channel_id=1, source_target_pairs={{0,6},{1,14},{2,4},{3,12},{4,2},{5,10},{6,0},{7,8},{8,7},{9,15},{1... | collective-permute-start | bytes 442376 | tf_op jit(solution)/shard_map/ppermute | solution.py:46
  116.7 1.6 %collective-permute-start.38 = (bf16[2,96,704]{2,1,0:T(8,128)(2,1)S(1)}, bf16[2,96,704]{2,1,0:T(8,128)(2,1)S(1)}, u32[]{:S(2)}, u32[]{:S(2)}) collective-permute-start(bf16[2,96,704]{2,1,0:T(8,128)(2,1)S(1)} %get-tuple-element.217), channel_id=1, source_target_pairs={{0,2},{1,3},{2,0},{3,1},{4,6},{5,7},{6,4},{7,5},{8,10},{9,11},{10,... | collective-permute-start | bytes 811016 | tf_op jit(solution)/shard_map/ppermute | solution.py:46
  119.2 3.0 %collective-permute-start.37 = (bf16[128,576]{1,0:T(8,128)(2,1)S(1)}, bf16[128,576]{1,0:T(8,128)(2,1)S(1)}, u32[]{:S(2)}, u32[]{:S(2)}) collective-permute-start(bf16[128,576]{1,0:T(8,128)(2,1)S(1)} %get-tuple-element.213), channel_id=1, source_target_pairs={{0,1},{1,0},{2,3},{3,2},{4,5},{5,4},{6,7},{7,6},{8,9},{9,8},{10,11... | collective-permute-start | bytes 442376 | tf_op jit(solution)/shard_map/ppermute | solution.py:46
  122.2 4.8 %collective-permute-done.28.refs_3_ = bf16[128,576]{1,0:T(8,128)(2,1)S(1)} collective-permute-done((bf16[128,576]{1,0:T(8,128)(2,1)S(1)}, bf16[128,576]{1,0:T(8,128)(2,1)S(1)}, u32[]{:S(2)}, u32[]{:S(2)}) %collective-permute-start.28) | collective-permute-done | bytes 147488 | tf_op jit(solution)/shard_map/ppermute | solution.py:46
  126.9 1.9 %collective-permute-start.43 = (bf16[256,192]{1,0:T(8,128)(2,1)S(1)}, bf16[256,192]{1,0:T(8,128)(2,1)S(1)}, u32[]{:S(2)}, u32[]{:S(2)}) collective-permute-start(bf16[256,192]{1,0:T(8,128)(2,1)S(1)} %down_sum.5), channel_id=1, source_target_pairs={{0,0},{1,1},{2,8},{3,9},{4,16},{5,17},{6,24},{7,25},{8,2},{9,3},{1... | collective-permute-start | bytes 294920 | tf_op jit(solution)/shard_map/ppermute | solution.py:46
  128.8 4.6 %input_grad.1 = f32[128,768]{1,0:T(8,128)} custom-call(s32[6]{0:T(128)S(1)} %stack.24.refs_0_, bf16[128,576]{1,0:T(8,128)(2,1)S(1)} %collective-permute-done.26.refs_1_, bf16[128,576]{1,0:T(8,128)(2,1)S(1)} %collective-permute-done.27.refs_2_, bf16[128,576]{1,0:T(8,128)(2,1)S(1)} %collective-permute-done.28.refs_3_, ...), custom_call_target="tpu_custom_call" | custom-call | flops 575000000 | bytes 1024 | tf_op jit(solution)/shard_map/input_grad/pallas_call | solution.py:123
  136.4 6.2 %collective-permute-start.41 = (bf16[96,576]{1,0:T(8,128)(2,1)S(1)}, bf16[96,576]{1,0:T(8,128)(2,1)S(1)}, u32[]{:S(2)}, u32[]{:S(2)}) collective-permute-start(bf16[96,576]{1,0:T(8,128)(2,1)S(1)} %bitcast.34), channel_id=1, source_target_pairs={{0,0},{1,1},{2,8},{3,9},{4,16},{5,17},{6,24},{7,25},{8,2},{9,3},{1... | collective-permute-start | bytes 331784 | tf_op jit(solution)/shard_map/ppermute | solution.py:46
  144.1 2.9 %collective-permute-done.39 = f32[24,128]{1,0:T(8,128)S(1)} collective-permute-done((f32[24,128]{1,0:T(8,128)S(1)}, f32[24,128]{1,0:T(8,128)S(1)}, u32[]{:S(2)}, u32[]{:S(2)}) %collective-permute-start.39) | collective-permute-done | bytes 12320 | tf_op jit(solution)/shard_map/ppermute | solution.py:46
  147.5 1.9 %collective-permute-done.41 = bf16[96,576]{1,0:T(8,128)(2,1)S(1)} collective-permute-done((bf16[96,576]{1,0:T(8,128)(2,1)S(1)}, bf16[96,576]{1,0:T(8,128)(2,1)S(1)}, u32[]{:S(2)}, u32[]{:S(2)}) %collective-permute-start.41) | collective-permute-done | bytes 110624 | tf_op jit(solution)/shard_map/ppermute | solution.py:46
  153.0 4.7 %collective-permute-done.42.refs_2_ = bf16[1,96,704]{2,1,0:T(8,128)(2,1)S(1)} collective-permute-done((bf16[1,96,704]{2,1,0:T(8,128)(2,1)S(1)}, bf16[1,96,704]{2,1,0:T(8,128)(2,1)S(1)}, u32[]{:S(2)}, u32[]{:S(2)}) %collective-permute-start.42) | collective-permute-done | bytes 135200 | tf_op jit(solution)/shard_map/ppermute | solution.py:46
  (116 shorter events, 40.8 us)
Async XLA Ops:
  2.4 14.0 %collective-permute-start.2 = (bf16[144,768]{1,0:T(8,128)(2,1)}, bf16[144,768]{1,0:T(8,128)(2,1)S(1)}, u32[]{:S(2)}, u32[]{:S(2)}) collective-permute-start(bf16[144,768]{1,0:T(8,128)(2,1)} %pack.1), channel_id=1, source_target_pairs={{0,4},{1,12},{2,6},{3,14},{4,0},{5,8},{6,2},{7,10},{8,5},{9,13},{1... | collective-permute-start | bytes 663560 | tf_op jit(solution)/shard_map/ppermute | solution.py:46
  5.0 12.3 %collective-permute-start.1 = (bf16[144,768]{1,0:T(8,128)(2,1)}, bf16[144,768]{1,0:T(8,128)(2,1)S(1)}, u32[]{:S(2)}, u32[]{:S(2)}) collective-permute-start(bf16[144,768]{1,0:T(8,128)(2,1)} %pack.1), channel_id=1, source_target_pairs={{0,2},{1,10},{2,0},{3,8},{4,6},{5,14},{6,4},{7,12},{8,3},{9,11},{1... | collective-permute-start | bytes 663560 | tf_op jit(solution)/shard_map/ppermute | solution.py:46
  6.6 10.7 %collective-permute-start = (bf16[144,768]{1,0:T(8,128)(2,1)}, bf16[144,768]{1,0:T(8,128)(2,1)S(1)}, u32[]{:S(2)}, u32[]{:S(2)}) collective-permute-start(bf16[144,768]{1,0:T(8,128)(2,1)} %pack.1), channel_id=1, source_target_pairs={{0,0},{1,8},{2,2},{3,10},{4,4},{5,12},{6,6},{7,14},{8,1},{9,9},{10... | collective-permute-start | bytes 663560 | tf_op jit(solution)/shard_map/ppermute | solution.py:46
  8.2 11.4 %collective-permute-start.3 = (bf16[128,768]{1,0:T(8,128)(2,1)S(1)}, bf16[128,768]{1,0:T(8,128)(2,1)S(1)}, u32[]{:S(2)}, u32[]{:S(2)}) collective-permute-start(bf16[128,768]{1,0:T(8,128)(2,1)S(1)} %bitcast.25), channel_id=1, source_target_pairs={{0,16},{1,17},{2,18},{3,19},{4,20},{5,21},{6,22},{7,23},{8,24},{9,... | collective-permute-start | bytes 589832 | tf_op jit(solution)/shard_map/ppermute | solution.py:46
  16.4 7.3 %collective-permute-start.4 = (bf16[1,144,768]{2,1,0:T(8,128)(2,1)S(1)}, bf16[1,144,768]{2,1,0:T(8,128)(2,1)S(1)}, u32[]{:S(2)}, u32[]{:S(2)}) collective-permute-start(bf16[1,144,768]{2,1,0:T(8,128)(2,1)S(1)} %bitcast.30), channel_id=1, source_target_pairs={{0,2},{1,3},{2,0},{3,1},{4,6},{5,7},{6,4},{7,5},{8,10},{9,11},{10,... | collective-permute-start | bytes 663560 | tf_op jit(solution)/shard_map/ppermute | solution.py:46
  19.6 7.4 %collective-permute-start.5 = (bf16[3,1,128,512]{3,2,1,0:T(8,128)(2,1)S(1)}, bf16[3,1,128,512]{3,2,1,0:T(8,128)(2,1)S(1)}, u32[]{:S(2)}, u32[]{:S(2)}) collective-permute-start(bf16[3,1,128,512]{3,2,1,0:T(8,128)(2,1)S(1)} %get-tuple-element.122.refs_1_), channel_id=1, source_target_pairs={{0,8},{1,9},{2,10},{3,11},{4,12},{5,13},{6,14},{7,15},{8,0},{9,1},... | collective-permute-start | bytes 1179656 | tf_op jit(solution)/shard_map/ppermute | solution.py:46
  25.6 16.1 %collective-permute-start.11 = (bf16[128,768]{1,0:T(8,128)(2,1)S(1)}, bf16[128,768]{1,0:T(8,128)(2,1)S(1)}, u32[]{:S(2)}, u32[]{:S(2)}) collective-permute-start(bf16[128,768]{1,0:T(8,128)(2,1)S(1)} %bitcast.26), channel_id=1, source_target_pairs={{0,8},{1,9},{2,10},{3,11},{4,12},{5,13},{6,14},{7,15},{8,0},{9,1},... | collective-permute-start | bytes 589832 | tf_op jit(solution)/shard_map/ppermute | solution.py:46
  26.1 16.1 %collective-permute-start.12 = (bf16[128,768]{1,0:T(8,128)(2,1)S(1)}, bf16[128,768]{1,0:T(8,128)(2,1)S(1)}, u32[]{:S(2)}, u32[]{:S(2)}) collective-permute-start(bf16[128,768]{1,0:T(8,128)(2,1)S(1)} %collective-permute-done.3.refs_7_), channel_id=1, source_target_pairs={{0,8},{1,9},{2,10},{3,11},{4,12},{5,13},{6,14},{7,15},{8,0},{9,1},... | collective-permute-start | bytes 589832 | tf_op jit(solution)/shard_map/ppermute | solution.py:46
  59.8 12.6 %collective-permute-start.13 = (bf16[128,192]{1,0:T(8,128)(2,1)S(1)}, bf16[128,192]{1,0:T(8,128)(2,1)S(1)}, u32[]{:S(2)}, u32[]{:S(2)}) collective-permute-start(bf16[128,192]{1,0:T(8,128)(2,1)S(1)} %get-tuple-element.139), channel_id=1, source_target_pairs={{0,0},{1,8},{2,2},{3,10},{4,4},{5,12},{6,6},{7,14},{8,1},{9,9},{10... | collective-permute-start | bytes 147464 | tf_op jit(solution)/shard_map/ppermute | solution.py:46
  60.5 12.0 %collective-permute-start.14 = (bf16[128,192]{1,0:T(8,128)(2,1)S(1)}, bf16[128,192]{1,0:T(8,128)(2,1)S(1)}, u32[]{:S(2)}, u32[]{:S(2)}) collective-permute-start(bf16[128,192]{1,0:T(8,128)(2,1)S(1)} %get-tuple-element.140), channel_id=1, source_target_pairs={{0,2},{1,10},{2,0},{3,8},{4,6},{5,14},{6,4},{7,12},{8,3},{9,11},{1... | collective-permute-start | bytes 147464 | tf_op jit(solution)/shard_map/ppermute | solution.py:46
  60.6 11.9 %collective-permute-start.15 = (bf16[128,192]{1,0:T(8,128)(2,1)S(1)}, bf16[128,192]{1,0:T(8,128)(2,1)S(1)}, u32[]{:S(2)}, u32[]{:S(2)}) collective-permute-start(bf16[128,192]{1,0:T(8,128)(2,1)S(1)} %get-tuple-element.141), channel_id=1, source_target_pairs={{0,4},{1,12},{2,6},{3,14},{4,0},{5,8},{6,2},{7,10},{8,5},{9,13},{1... | collective-permute-start | bytes 147464 | tf_op jit(solution)/shard_map/ppermute | solution.py:46
  61.7 10.8 %collective-permute-start.16 = (bf16[128,192]{1,0:T(8,128)(2,1)S(1)}, bf16[128,192]{1,0:T(8,128)(2,1)S(1)}, u32[]{:S(2)}, u32[]{:S(2)}) collective-permute-start(bf16[128,192]{1,0:T(8,128)(2,1)S(1)} %get-tuple-element.142), channel_id=1, source_target_pairs={{0,6},{1,14},{2,4},{3,12},{4,2},{5,10},{6,0},{7,8},{8,7},{9,15},{1... | collective-permute-start | bytes 147464 | tf_op jit(solution)/shard_map/ppermute | solution.py:46
  67.8 17.4 %collective-permute-start.20 = (bf16[4,256,192]{2,1,0:T(8,128)(2,1)S(1)}, bf16[4,256,192]{2,1,0:T(8,128)(2,1)S(1)}, u32[]{:S(2)}, u32[]{:S(2)}) collective-permute-start(bf16[4,256,192]{2,1,0:T(8,128)(2,1)S(1)} %get-tuple-element.147), channel_id=1, source_target_pairs={{0,1},{1,0},{2,3},{3,2},{4,5},{5,4},{6,7},{7,6},{8,9},{9,8},{10,11... | collective-permute-start | bytes 1179656 | tf_op jit(solution)/shard_map/ppermute | solution.py:46
  80.8 9.4 %collective-permute-start.24 = (bf16[128,1152]{1,0:T(8,128)(2,1)S(1)}, bf16[128,1152]{1,0:T(8,128)(2,1)S(1)}, u32[]{:S(2)}, u32[]{:S(2)}) collective-permute-start(bf16[128,1152]{1,0:T(8,128)(2,1)S(1)} %get-tuple-element.188), channel_id=1, source_target_pairs={{0,16},{1,17},{2,18},{3,19},{4,20},{5,21},{6,22},{7,23},{8,24},{9,... | collective-permute-start | bytes 884744 | tf_op jit(solution)/shard_map/ppermute | solution.py:46
  83.5 11.2 %collective-permute-start.22 = (bf16[4,96,512]{2,1,0:T(8,128)(2,1)S(1)}, bf16[4,96,512]{2,1,0:T(8,128)(2,1)S(1)}, u32[]{:S(2)}, u32[]{:S(2)}) collective-permute-start(bf16[4,96,512]{2,1,0:T(8,128)(2,1)S(1)} %get-tuple-element.169), channel_id=1, source_target_pairs={{0,1},{1,0},{2,3},{3,2},{4,5},{5,4},{6,7},{7,6},{8,9},{9,8},{10,11... | collective-permute-start | bytes 1179656 | tf_op jit(solution)/shard_map/ppermute | solution.py:46
  84.1 11.4 %collective-permute-start.23 = (bf16[128,1152]{1,0:T(8,128)(2,1)S(1)}, bf16[128,1152]{1,0:T(8,128)(2,1)S(1)}, u32[]{:S(2)}, u32[]{:S(2)}) collective-permute-start(bf16[128,1152]{1,0:T(8,128)(2,1)S(1)} %get-tuple-element.187.refs_3_), channel_id=1, source_target_pairs={{0,8},{1,9},{2,10},{3,11},{4,12},{5,13},{6,14},{7,15},{8,0},{9,1},... | collective-permute-start | bytes 884744 | tf_op jit(solution)/shard_map/ppermute | solution.py:46
  92.8 10.3 %collective-permute-start.31 = (bf16[416,576]{1,0:T(8,128)(2,1)S(1)}, bf16[416,576]{1,0:T(8,128)(2,1)S(1)}, u32[]{:S(2)}, u32[]{:S(2)}) collective-permute-start(bf16[416,576]{1,0:T(8,128)(2,1)S(1)} %get-tuple-element.182), channel_id=1, source_target_pairs={{0,8},{1,9},{2,10},{3,11},{4,12},{5,13},{6,14},{7,15},{8,0},{9,1},... | collective-permute-start | bytes 1437704 | tf_op jit(solution)/shard_map/ppermute | solution.py:46
  93.4 9.2 %collective-permute-start.30 = (bf16[2,256,192]{2,1,0:T(8,128)(2,1)S(1)}, bf16[2,256,192]{2,1,0:T(8,128)(2,1)S(1)}, u32[]{:S(2)}, u32[]{:S(2)}) collective-permute-start(bf16[2,256,192]{2,1,0:T(8,128)(2,1)S(1)} %get-tuple-element.172), channel_id=1, source_target_pairs={{0,2},{1,3},{2,0},{3,1},{4,6},{5,7},{6,4},{7,5},{8,10},{9,11},{10,... | collective-permute-start | bytes 589832 | tf_op jit(solution)/shard_map/ppermute | solution.py:46
  97.0 19.0 %collective-permute-start.35 = (bf16[4,96,704]{2,1,0:T(8,128)(2,1)S(1)}, bf16[4,96,704]{2,1,0:T(8,128)(2,1)S(1)}, u32[]{:S(2)}, u32[]{:S(2)}) collective-permute-start(bf16[4,96,704]{2,1,0:T(8,128)(2,1)S(1)} %get-tuple-element.190), channel_id=1, source_target_pairs={{0,1},{1,0},{2,3},{3,2},{4,5},{5,4},{6,7},{7,6},{8,9},{9,8},{10,11... | collective-permute-start | bytes 1622024 | tf_op jit(solution)/shard_map/ppermute | solution.py:46
  97.3 9.2 %collective-permute-start.32 = (bf16[2,96,512]{2,1,0:T(8,128)(2,1)S(1)}, bf16[2,96,512]{2,1,0:T(8,128)(2,1)S(1)}, u32[]{:S(2)}, u32[]{:S(2)}) collective-permute-start(bf16[2,96,512]{2,1,0:T(8,128)(2,1)S(1)} %get-tuple-element.207), channel_id=1, source_target_pairs={{0,2},{1,3},{2,0},{3,1},{4,6},{5,7},{6,4},{7,5},{8,10},{9,11},{10,... | collective-permute-start | bytes 589832 | tf_op jit(solution)/shard_map/ppermute | solution.py:46
  103.9 9.4 %collective-permute-start.34 = (bf16[224,576]{1,0:T(8,128)(2,1)S(1)}, bf16[224,576]{1,0:T(8,128)(2,1)S(1)}, u32[]{:S(2)}, u32[]{:S(2)}) collective-permute-start(bf16[224,576]{1,0:T(8,128)(2,1)S(1)} %get-tuple-element.204), channel_id=1, source_target_pairs={{0,16},{1,17},{2,18},{3,19},{4,20},{5,21},{6,22},{7,23},{8,24},{9,... | collective-permute-start | bytes 774152 | tf_op jit(solution)/shard_map/ppermute | solution.py:46
  105.4 7.3 %collective-permute-start.33 = (bf16[1,256,192]{2,1,0:T(8,128)(2,1)S(1)}, bf16[1,256,192]{2,1,0:T(8,128)(2,1)S(1)}, u32[]{:S(2)}, u32[]{:S(2)}) collective-permute-start(bf16[1,256,192]{2,1,0:T(8,128)(2,1)S(1)} %get-tuple-element.200), channel_id=1, source_target_pairs={{0,4},{1,5},{2,6},{3,7},{4,0},{5,1},{6,2},{7,3},{8,12},{9,13},{10,... | collective-permute-start | bytes 294920 | tf_op jit(solution)/shard_map/ppermute | solution.py:46
  105.9 12.4 %collective-permute-start.26 = (bf16[128,576]{1,0:T(8,128)(2,1)S(1)}, bf16[128,576]{1,0:T(8,128)(2,1)S(1)}, u32[]{:S(2)}, u32[]{:S(2)}) collective-permute-start(bf16[128,576]{1,0:T(8,128)(2,1)S(1)} %get-tuple-element.191.refs_1_), channel_id=1, source_target_pairs={{0,0},{1,8},{2,2},{3,10},{4,4},{5,12},{6,6},{7,14},{8,1},{9,9},{10... | collective-permute-start | bytes 442376 | tf_op jit(solution)/shard_map/ppermute | solution.py:46
  106.6 12.6 %collective-permute-start.27 = (bf16[128,576]{1,0:T(8,128)(2,1)S(1)}, bf16[128,576]{1,0:T(8,128)(2,1)S(1)}, u32[]{:S(2)}, u32[]{:S(2)}) collective-permute-start(bf16[128,576]{1,0:T(8,128)(2,1)S(1)} %get-tuple-element.192.refs_2_), channel_id=1, source_target_pairs={{0,2},{1,10},{2,0},{3,8},{4,6},{5,14},{6,4},{7,12},{8,3},{9,11},{1... | collective-permute-start | bytes 442376 | tf_op jit(solution)/shard_map/ppermute | solution.py:46
  112.7 14.2 %collective-permute-start.28 = (bf16[128,576]{1,0:T(8,128)(2,1)S(1)}, bf16[128,576]{1,0:T(8,128)(2,1)S(1)}, u32[]{:S(2)}, u32[]{:S(2)}) collective-permute-start(bf16[128,576]{1,0:T(8,128)(2,1)S(1)} %get-tuple-element.193.refs_3_), channel_id=1, source_target_pairs={{0,4},{1,12},{2,6},{3,14},{4,0},{5,8},{6,2},{7,10},{8,5},{9,13},{1... | collective-permute-start | bytes 442376 | tf_op jit(solution)/shard_map/ppermute | solution.py:46
  113.3 15.5 %collective-permute-start.29 = (bf16[128,576]{1,0:T(8,128)(2,1)S(1)}, bf16[128,576]{1,0:T(8,128)(2,1)S(1)}, u32[]{:S(2)}, u32[]{:S(2)}) collective-permute-start(bf16[128,576]{1,0:T(8,128)(2,1)S(1)} %get-tuple-element.194.refs_4_), channel_id=1, source_target_pairs={{0,6},{1,14},{2,4},{3,12},{4,2},{5,10},{6,0},{7,8},{8,7},{9,15},{1... | collective-permute-start | bytes 442376 | tf_op jit(solution)/shard_map/ppermute | solution.py:46
  116.7 26.0 %collective-permute-start.38 = (bf16[2,96,704]{2,1,0:T(8,128)(2,1)S(1)}, bf16[2,96,704]{2,1,0:T(8,128)(2,1)S(1)}, u32[]{:S(2)}, u32[]{:S(2)}) collective-permute-start(bf16[2,96,704]{2,1,0:T(8,128)(2,1)S(1)} %get-tuple-element.217), channel_id=1, source_target_pairs={{0,2},{1,3},{2,0},{3,1},{4,6},{5,7},{6,4},{7,5},{8,10},{9,11},{10,... | collective-permute-start | bytes 811016 | tf_op jit(solution)/shard_map/ppermute | solution.py:46
  118.3 16.3 %collective-permute-start.36 = (bf16[1,96,512]{2,1,0:T(8,128)(2,1)S(1)}, bf16[1,96,512]{2,1,0:T(8,128)(2,1)S(1)}, u32[]{:S(2)}, u32[]{:S(2)}) collective-permute-start(bf16[1,96,512]{2,1,0:T(8,128)(2,1)S(1)} %get-tuple-element.209), channel_id=1, source_target_pairs={{0,4},{1,5},{2,6},{3,7},{4,0},{5,1},{6,2},{7,3},{8,12},{9,13},{10,... | collective-permute-start | bytes 294920 | tf_op jit(solution)/shard_map/ppermute | solution.py:46
  119.2 16.7 %collective-permute-start.37 = (bf16[128,576]{1,0:T(8,128)(2,1)S(1)}, bf16[128,576]{1,0:T(8,128)(2,1)S(1)}, u32[]{:S(2)}, u32[]{:S(2)}) collective-permute-start(bf16[128,576]{1,0:T(8,128)(2,1)S(1)} %get-tuple-element.213), channel_id=1, source_target_pairs={{0,1},{1,0},{2,3},{3,2},{4,5},{5,4},{6,7},{7,6},{8,9},{9,8},{10,11... | collective-permute-start | bytes 442376 | tf_op jit(solution)/shard_map/ppermute | solution.py:46
  126.9 16.4 %collective-permute-start.43 = (bf16[256,192]{1,0:T(8,128)(2,1)S(1)}, bf16[256,192]{1,0:T(8,128)(2,1)S(1)}, u32[]{:S(2)}, u32[]{:S(2)}) collective-permute-start(bf16[256,192]{1,0:T(8,128)(2,1)S(1)} %down_sum.5), channel_id=1, source_target_pairs={{0,0},{1,1},{2,8},{3,9},{4,16},{5,17},{6,24},{7,25},{8,2},{9,3},{1... | collective-permute-start | bytes 294920 | tf_op jit(solution)/shard_map/ppermute | solution.py:46
  136.4 12.9 %collective-permute-start.41 = (bf16[96,576]{1,0:T(8,128)(2,1)S(1)}, bf16[96,576]{1,0:T(8,128)(2,1)S(1)}, u32[]{:S(2)}, u32[]{:S(2)}) collective-permute-start(bf16[96,576]{1,0:T(8,128)(2,1)S(1)} %bitcast.34), channel_id=1, source_target_pairs={{0,0},{1,1},{2,8},{3,9},{4,16},{5,17},{6,24},{7,25},{8,2},{9,3},{1... | collective-permute-start | bytes 331784 | tf_op jit(solution)/shard_map/ppermute | solution.py:46
  150.1 7.6 %collective-permute-start.42 = (bf16[1,96,704]{2,1,0:T(8,128)(2,1)S(1)}, bf16[1,96,704]{2,1,0:T(8,128)(2,1)S(1)}, u32[]{:S(2)}, u32[]{:S(2)}) collective-permute-start(bf16[1,96,704]{2,1,0:T(8,128)(2,1)S(1)} %get-tuple-element.227), channel_id=1, source_target_pairs={{0,4},{1,5},{2,6},{3,7},{4,0},{5,1},{6,2},{7,3},{8,12},{9,13},{10,... | collective-permute-start | bytes 405512 | tf_op jit(solution)/shard_map/ppermute | solution.py:46
  (24 other events, 215.0 us)

commit v2 on v1

--- a/solution.py
+++ b/solution.py
@@ -54,9 +54,18 @@
     def across(self, block):
         return self.send(block, lambda x, c, g, s, y: (x ^ 1, c, g, s, y))
 
+    def far_group(self, block):
+        return self.wide_mask(block, self.wide // 2)
+
+    def near_group(self, block):
+        return self.wide_mask(block, self.wide // 4)
+
     def wide_bit(self, block, bit):
+        return self.wide_mask(block, 1 << bit)
+
+    def wide_mask(self, block, mask):
         def target(x, c, g, s, y):
-            w = ((g * self.s_count + s) * 2 + y) ^ (1 << bit)
+            w = ((g * self.s_count + s) * 2 + y) ^ mask
             return (x, c, w // (2 * self.s_count), (w // 2) % self.s_count, w % 2)
 
         return self.send(block, target)
@@ -553,7 +562,7 @@
         in_hbm=(8,),
         staged=tuple(("out", i) for i in range(6)) if s_count == 1 else (),
         mebibytes=13 if s_count == 1 else 60,
-        us=7,
+        us=0.01,
     )
 
 
@@ -617,10 +626,9 @@
     (place,) = smem
     out_ref, grad_ref, gain_grad_ref = outs[0:3]
     dctx = outs[3:7]
-    mine_ref, far_ref = outs[7:9]
-    w_down, w_gate, w_up, w_out = get(10), get(11), get(12), get(13)
+    w_down, w_gate, w_up, w_out = get(6), get(7), get(8), get(9)
     count = 4
-    group, across = place[0], place[4]
+    group = place[0]
     tok, width = grad_ref.shape
     ff = w_gate.shape[1]
     local = width // groups
@@ -648,9 +656,9 @@
     for d in range(4):
         start = pl.multiple_of((group ^ d) * local, local)
         dctx[d][...] = dot(attn, w_out[pl.ds(start, local), :], 1, 1).astype(bf16)
-    for ref, which in ((mine_ref, across), (far_ref, 1 - across)):
+    for ref, which in ((outs[7], place[4]), (outs[8], 1 - place[4])):
         for d in range(4):
-            ref[:, d * local : (d + 1) * local] = get(6 + d)[...]
+            ref[:, d * local : (d + 1) * local] = get(10 + d)[...]
         start = pl.multiple_of(which * (width // 2), width // 2)
         ref[:, width:] = attn_scr[:, pl.ds(start, width // 2)]
     out_ref[...] = (middle + dot(get(2)[...], w_down[...], 1, 0)).astype(bf16)
@@ -663,7 +671,7 @@
         ffn_backward_body,
         "ffn_backward",
         [place],
-        [cot, middle, hidden, act, slope, gain, *ctx, w_down, w_gate, w_up, w_out],
+        [cot, middle, hidden, act, slope, gain, w_down, w_gate, w_up, w_out, *ctx],
         [shaped(bf16, tok, width), shaped(f32, tok, width), shaped(f32, 1, width)]
         + [shaped(bf16, tok, local)] * 4
         + [shaped(bf16, tok, width + width // 2)] * 2,
@@ -673,145 +681,267 @@
     )
 
 
-def split_rows(total, wide, odd, kept_ref, sent_ref, cols):
-    block = total.shape[0] // wide
-    for i in range(wide // 2):
-        even_rows = total[2 * i * block : (2 * i + 1) * block, :]
-        odd_rows = total[(2 * i + 1) * block : (2 * i + 2) * block, :]
-        kept_ref[i, :, cols] = jnp.where(odd, odd_rows, even_rows)
-        sent_ref[i, :, cols] = jnp.where(odd, even_rows, odd_rows).astype(bf16)
-
-
-def down_grad_body(smem, get, outs, cot_scr, hidden_scr, total_scr, *, wide):
+def ffn_grad_body(
+    smem, get, outs, normed_scr, cot_scr, hidden_scr, gate_scr, up_scr, both_scr, down_scr, *, s_count
+):
     (place,) = smem
-    kept_ref, sent_ref, gate_ref, up_ref, normed_scr = outs
-    odd = place[3] == 1
-    rows, quarter = hidden_scr.shape
-    tok = rows // 4
+    kept_ref, sent_ref = outs
+    group, core, far = place[0], place[1], place[4] == 1
+    rows, eighth = hidden_scr.shape
+    tok = rows // 8
     width = normed_scr.shape[1]
     local = width // groups
-    for i in range(4):
+    for i in range(8):
         normed_scr[i * tok : (i + 1) * tok, :] = get(i)[...]
-        cot_scr[i * tok : (i + 1) * tok, :] = get(4 + i)[...]
-    start = pl.multiple_of((place[4] * 2 + place[1]) * quarter, quarter)
-    half = quarter // 2
+        cot_scr[i * tok : (i + 1) * tok, :] = get(8 + i)[...]
+    start = ((group % 2) * 2 + core) * 2 * eighth + (group // 2) * eighth
+    part = pl.ds(pl.multiple_of(start, eighth), eighth)
+    w_gate, w_up, w_down = get(16)[:, part], get(17)[:, part], get(18)[part, :]
+    half = rows // 2
     for i in range(2):
-        cols = slice(i * half, (i + 1) * half)
-        part = pl.ds(pl.multiple_of(start + i * half, half), half)
-        up = dot(normed_scr[...], get(9)[:, part], 1, 0)
-        act, slope = gated(dot(normed_scr[...], get(8)[:, part], 1, 0), up)
-        hidden_scr[:, cols] = (act * up).astype(bf16)
-        hidden_grad = dot(cot_scr[...], get(10)[part, :], 1, 1)
-        gate_ref[:, cols] = (hidden_grad * slope).astype(bf16)
-        up_ref[:, cols] = (hidden_grad * act).astype(bf16)
-    total_scr[...] = dot(hidden_scr[...], cot_scr[...], 0, 0)
-    blocks = wide // groups
-    block = quarter // blocks
-    for i in range(wide // 2):
-        g, j = 2 * i // blocks, 2 * i % blocks
-        cols = slice(g * local, (g + 1) * local)
-        even_rows = total_scr[j * block : (j + 1) * block, cols]
-        odd_rows = total_scr[(j + 1) * block : (j + 2) * block, cols]
-        kept_ref[i] = jnp.where(odd, odd_rows, even_rows)
-        sent_ref[i] = jnp.where(odd, even_rows, odd_rows).astype(bf16)
-
-
-def down_grad(place, normed, cot, w_gate, w_up, w_down, wide):
+        span = slice(i * half, (i + 1) * half)
+        up = dot(normed_scr[span, :], w_up, 1, 0)
+        act, slope = gated(dot(normed_scr[span, :], w_gate, 1, 0), up)
+        hidden_scr[span, :] = (act * up).astype(bf16)
+        hidden_grad = dot(cot_scr[span, :], w_down, 1, 1)
+        gate_scr[span, :] = (hidden_grad * slope).astype(bf16)
+        up_scr[span, :] = (hidden_grad * act).astype(bf16)
+    both_scr[:, :eighth] = dot(normed_scr[...], gate_scr[...], 0, 0)
+    both_scr[:, eighth:] = dot(normed_scr[...], up_scr[...], 0, 0)
+    down_scr[...] = dot(hidden_scr[...], cot_scr[...], 0, 0)
+    unit = kept_ref.shape[1]
+    block = 3 * unit // 2
+
+    def pieces(x, s, y):
+        found = []
+        for k in range(3):
+            parts = []
+            for j in range(2):
+                at = (((x + 2 * j) * s_count + s) * 2 + y) * block
+                low, high = max(k * unit - j * block, 0), min((k + 1) * unit - j * block, block)
+                if low < high:
+                    parts.append(both_scr[at + low : at + high, :])
+            found.append(parts[0] if len(parts) == 1 else jnp.concatenate(parts, axis=0))
+        for k in range(4):
+            at = (s * 4 + k) * unit
+            cols = slice((x * 2 + y) * local, (x * 2 + y + 1) * local)
+            found.append(down_scr[at : at + unit, cols])
+        return found
+
+    for s in range(s_count):
+        for y in range(2):
+            lane = 0
+            for near, other in zip(pieces(0, s, y), pieces(1, s, y)):
+                cols = slice(lane, lane + near.shape[1])
+                kept_ref[s * 2 + y, :, cols] = jnp.where(far, other, near)
+                sent_ref[s * 2 + y, :, cols] = jnp.where(far, near, other).astype(bf16)
+                lane += near.shape[1]
+
+
+def ffn_grad(place, normed, cot, w_gate, w_up, w_down, s_count):
     tok, width = normed[0].shape
     ff = w_gate.shape[1]
-    shape = (wide // 2, ff // wide, width // groups)
-    return kernel_call(
-        functools.partial(down_grad_body, wide=wide),
-        "down_grad",
+    eighth = ff // 8
+    unit = eighth // (4 * s_count)
+    shape = (2 * s_count, unit, 3 * 2 * eighth + 4 * width // groups)
+    return kernel_call(
+        functools.partial(ffn_grad_body, s_count=s_count),
+        "ffn_grad",
         [place],
         [*normed, *cot, w_gate, w_up, w_down],
-        [shaped(f32, *shape), shaped(bf16, *shape)]
-        + [shaped(bf16, 4 * tok, ff // 4)] * 2
-        + [shaped(bf16, 4 * tok, width)],
+        [shaped(f32, *shape), shaped(bf16, *shape)],
         scratch=[
-            pltpu.VMEM((4 * tok, width), bf16),
-            pltpu.VMEM((4 * tok, ff // 4), bf16),
-            pltpu.VMEM((ff // 4, width), f32),
+            pltpu.VMEM((8 * tok, width), bf16),
+            pltpu.VMEM((8 * tok, width), bf16),
+            pltpu.VMEM((8 * tok, eighth), bf16),
+            pltpu.VMEM((8 * tok, eighth), bf16),
+            pltpu.VMEM((8 * tok, eighth), bf16),
+            pltpu.VMEM((width, 2 * eighth), f32),
+            pltpu.VMEM((eighth, width), f32),
         ],
-        mebibytes=10,
-        us=1,
-    )
-
-
-def up_grad_body(smem, get, outs, total_scr, *, wide):
+        mebibytes=16,
+        us=0.01,
+    )
+
+
+def out_grad_body(smem, get, outs, ctx_scr, attn_scr, out_scr):
     (place,) = smem
-    total_scr[...] = dot(get(0)[...], get(1)[...], 0, 0)
-    split_rows(total_scr, wide, place[3] == 1, *outs, slice(None))
-
-
-def up_grad(place, normed, grad, wide):
-    width = normed.shape[1]
-    quarter = grad.shape[1]
-    shape = (wide // 2, width // wide, quarter)
-    return kernel_call(
-        functools.partial(up_grad_body, wide=wide),
-        "up_grad",
-        [place],
-        [normed, grad],
-        [shaped(f32, *shape), shaped(bf16, *shape)],
-        scratch=[pltpu.VMEM((width, quarter), f32)],
-        mebibytes=5,
-        us=0.5,
-    )
-
-
-def gate_grad_body(
-    smem, get, outs, ctx_scr, attn_scr, total_scr, out_scr, *, wide
-):
-    (place,) = smem
+    kept_ref, sent_ref = outs
     group, core, odd = place[0], place[1], place[3] == 1
-    rows, width = get(0).shape
-    tok = rows // 4
+    tok = ctx_scr.shape[0] // 4
+    width = ctx_scr.shape[1]
     local = width // groups
-    quarter = total_scr.shape[1]
     for i in range(4):
         rows = slice(i * tok, (i + 1) * tok)
-        ctx_scr[rows, :] = get(2 + i)[:, :width]
-        both = get(2 + i)[:, width:]
+        ctx_scr[rows, :] = get(i)[:, :width]
+        both = get(i)[:, width:]
         attn_scr[rows, :] = jnp.where(core == 0, both[:, :local], both[:, local:])
-    total_scr[...] = dot(get(0)[...], get(1)[...], 0, 0)
-    split_rows(total_scr, wide, odd, *outs, slice(0, quarter))
     turned = dot(ctx_scr[...], attn_scr[...], 0, 0)
     for d in range(4):
         start = pl.multiple_of((group ^ d) * local, local)
         out_scr[pl.ds(start, local), :] = turned[d * local : (d + 1) * local]
-    split_rows(out_scr, wide, odd, *outs, slice(quarter, quarter + local))
-
-
-def gate_grad(place, normed, grad, attn, wide):
-    rows, width = normed.shape
-    quarter = grad.shape[1]
+    pieces, block, unused = kept_ref.shape
+    for i in range(pieces):
+        even = out_scr[2 * i * block : (2 * i + 1) * block, :]
+        other = out_scr[(2 * i + 1) * block : (2 * i + 2) * block, :]
+        kept_ref[i] = jnp.where(odd, other, even)
+        sent_ref[i * block : (i + 1) * block, :] = jnp.where(odd, even, other).astype(bf16)
+
+
+def out_weight_grad(place, parts, wide):
+    tok, span = parts[0].shape
+    width = span * 2 // 3
     local = width // groups
-    shape = (wide // 2, width // wide, quarter + local)
-    return kernel_call(
-        functools.partial(gate_grad_body, wide=wide),
-        "gate_grad",
+    shape = (wide // 2, width // wide, local)
+    return kernel_call(
+        out_grad_body,
+        "out_grad",
         [place],
-        [normed, grad, *attn],
-        [shaped(f32, *shape), shaped(bf16, *shape)],
+        parts,
+        [shaped(f32, *shape), shaped(bf16, width // 2, local)],
         scratch=[
-            pltpu.VMEM((rows, width), bf16),
-            pltpu.VMEM((rows, local), bf16),
-            pltpu.VMEM((width, quarter), f32),
+            pltpu.VMEM((4 * tok, width), bf16),
+            pltpu.VMEM((4 * tok, local), bf16),
             pltpu.VMEM((width, local), f32),
         ],
-        mebibytes=8,
-        us=0.5,
+        mebibytes=5,
+        us=0.01,
+    )
+
+
+def out_sum_body(smem, get, outs, *, bit, riding):
+    (place,) = smem
+    kept, received = get(0), get(1)
+    remaining, block, unused = kept.shape
+    totals = [
+        kept[i] + received[i * block : (i + 1) * block, :].astype(f32) for i in range(remaining)
+    ]
+    if riding:
+        small = get(2)[...]
+        if "in" in riding:
+            small = attached(received, remaining * block, small)
+            outs[-1][...] = small
+    if remaining == 1:
+        outs[0][...] = totals[0]
+        return
+    odd = ((place[5] >> bit) & 1) == 1
+    for i in range(remaining // 2):
+        outs[0][i] = jnp.where(odd, totals[2 * i + 1], totals[2 * i])
+        theirs = jnp.where(odd, totals[2 * i], totals[2 * i + 1])
+        outs[1][i * block : (i + 1) * block, :] = theirs.astype(bf16)
+    if riding:
+        filled = remaining // 2 * block
+        rest = outs[1].shape[0] - filled
+        outs[1][filled:, :] = jnp.zeros((rest, outs[1].shape[1]), bf16)
+        attach_rows(outs[1], filled, small)
+
+
+def out_sum(layout, place, kept, sent, bit, small=None, riding=()):
+    remaining, block, local = kept.shape
+    extra = 2 * room(small.shape[0]) if riding else 0
+    if remaining == 1:
+        outputs = [shaped(f32, block, local)]
+    else:
+        outputs = [
+            shaped(f32, remaining // 2, block, local),
+            shaped(bf16, remaining // 2 * block + extra, local),
+        ]
+    if "in" in riding:
+        outputs.append(shaped(f32, *small.shape))
+    return kernel_call(
+        functools.partial(out_sum_body, bit=bit + 1, riding=riding),
+        "out_sum",
+        [place],
+        [kept, layout.wide_bit(sent, bit)] + ([small] if riding else []),
+        outputs,
+        us=0.01,
+    )
+
+
+def ffn_sum_body(smem, get, outs):
+    (place,) = smem
+    odd = place[3] == 1
+    for i in range(outs[0].shape[0]):
+        even = get(0)[2 * i] + get(1)[2 * i].astype(f32)
+        other = get(0)[2 * i + 1] + get(1)[2 * i + 1].astype(f32)
+        outs[0][i] = jnp.where(odd, other, even)
+        outs[1][i] = jnp.where(odd, even, other).astype(bf16)
+
+
+def ffn_sum(place, kept, received):
+    pieces, unit, span = kept.shape
+    return kernel_call(
+        ffn_sum_body,
+        "ffn_sum",
+        [place],
+        [kept, received],
+        [shaped(f32, pieces // 2, unit, span), shaped(bf16, pieces // 2, unit, span)],
+        us=0.01,
+    )
+
+
+def ffn_last_body(smem, get, outs, both_scr):
+    (place,) = smem
+    total = get(0)[0].astype(f32) + get(1)[0].astype(f32)
+    unit = total.shape[0]
+    block, span = outs[0].shape
+    local = outs[2].shape[1]
+    for k in range(3):
+        both_scr[k * unit : (k + 1) * unit, :] = total[:, k * span : (k + 1) * span]
+    for k in range(4):
+        at = 3 * span + k * local
+        outs[2][k * unit : (k + 1) * unit, :] = total[:, at : at + local].astype(bf16)
+    low = place[0] // 2 == 0
+    first, second = both_scr[:block, :], both_scr[block:, :]
+    outs[0][...] = jnp.where(low, first, second).astype(bf16)
+    outs[1][...] = jnp.where(low, second, first).astype(bf16)
+
+
+def ffn_last(place, kept, received, local):
+    unused, unit, span = kept.shape
+    both = (span - 4 * local) // 3
+    return kernel_call(
+        ffn_last_body,
+        "ffn_last",
+        [place],
+        [kept, received],
+        [shaped(bf16, 3 * unit // 2, both)] * 2 + [shaped(bf16, 4 * unit, local)],
+        scratch=[pltpu.VMEM((3 * unit, both), f32)],
+        us=0.01,
+    )
+
+
+def ffn_owned_body(smem, get, outs):
+    (place,) = smem
+    low = place[0] // 2 == 0
+    eighth = get(0).shape[1] // 2
+    own, other = get(0)[...].astype(f32), get(1)[...].astype(f32)
+    first, second = jnp.where(low, own, other), jnp.where(low, other, own)
+    for i in range(2):
+        cols = slice(i * eighth, (i + 1) * eighth)
+        outs[i][:, :eighth] = first[:, cols]
+        outs[i][:, eighth:] = second[:, cols]
+    outs[2][...] = jnp.transpose(get(2)[...].astype(f32))
+
+
+def ffn_owned(place, own, other, down):
+    return kernel_call(
+        ffn_owned_body,
+        "ffn_owned",
+        [place],
+        [own, other, down],
+        [shaped(f32, *own.shape)] * 2 + [shaped(f32, *down.shape[::-1])],
+        us=1,
     )
 
 
 def collect_body(smem, get, outs):
-    local = outs[0].shape[1] // 3
+    local = outs[0].shape[2] // 3
     for d in range(4):
-        outs[d][:, :local] = get(d)[...]
+        outs[d // 2][d % 2, :, :local] = get(d)[...]
     for d in range(4):
         total = get(4)[d].astype(f32) + get(5)[d].astype(f32)
-        outs[d][:, local:] = total.astype(bf16)
+        outs[d // 2][d % 2, :, local:] = total.astype(bf16)
 
 
 def collect(dq, kept, received):
@@ -821,9 +951,9 @@
         "collect",
         [],
         [*dq, kept, received],
-        [shaped(bf16, tok, 3 * local)] * 4,
+        [shaped(bf16, 2, tok, 3 * local)] * 2,
         staged=tuple(range(6)),
-        us=0.5,
+        us=0.01,
     )
 
 
@@ -838,11 +968,23 @@
     ref[rows : rows + small.shape[0], small.shape[1] : 2 * small.shape[1]] = low
 
 
+def attach_rows(ref, rows, small):
+    high, low = exact(small)
+    count, lanes = small.shape
+    ref[rows : rows + count, :lanes] = high
+    below = rows + room(count)
+    ref[below : below + count, :lanes] = low
+
+
 def attached(ref, rows, small):
     count, lanes = small.shape
     high, low = exact(small)
     theirs = ref[rows : rows + count, :lanes].astype(f32)
-    theirs = theirs + ref[rows : rows + count, lanes : 2 * lanes].astype(f32)
+    if ref.shape[1] >= 2 * lanes:
+        theirs = theirs + ref[rows : rows + count, lanes : 2 * lanes].astype(f32)
+    else:
+        below = rows + room(count)
+        theirs = theirs + ref[below : below + count, :lanes].astype(f32)
     return high.astype(f32) + low.astype(f32) + theirs
 
 
@@ -854,9 +996,9 @@
     local = span // 3
     tok = grad_scr.shape[0] // 4
     for d in range(4):
-        grad_scr[d * tok : (d + 1) * tok, :] = get(d)[...]
-    total_scr[...] = dot(get(4)[...], grad_scr[: 3 * tok, :], 0, 0)
-    total_scr[...] += dot(get(11)[...], grad_scr[3 * tok :, :], 0, 0)
+        grad_scr[d * tok : (d + 1) * tok, :] = get(d // 2)[d % 2]
+    total_scr[...] = dot(get(2)[...], grad_scr[: 3 * tok, :], 0, 0)
+    total_scr[...] += dot(get(9)[...], grad_scr[3 * tok :, :], 0, 0)
     quarter = width // 4
     for i in range(2):
         start = pl.multiple_of((2 * i + core) * quarter, quarter)
@@ -867,20 +1009,20 @@
     ones = jnp.ones((8, local), bf16)
     gain_grad = jnp.zeros((8, width), f32)
     for i in range(3):
-        both = get(8 + i)[:, pl.ds(window, -(-local // 128) * 128)]
+        both = get(6 + i)[:, pl.ds(window, -(-local // 128) * 128)]
         weight = jnp.where(late, both[:, both.shape[1] - local :], both[:, :local])
         product = total_scr[:, i * local : (i + 1) * local] * weight.astype(f32)
         high, rest = exact(product)
         gain_grad = gain_grad + dot(ones, high, 1, 1) + dot(ones, rest, 1, 1)
-    gain_grad = gain_grad[0:1] / get(5)[...]
-    ffn_gain = get(6)[...]
+    gain_grad = gain_grad[0:1] / get(3)[...]
+    ffn_gain = get(4)[...]
     lanes = 128
     rows = width // lanes
     for i in range(rows):
         small_ref[i : i + 1, :] = gain_grad[:, i * lanes : (i + 1) * lanes]
         small_ref[rows + i : rows + i + 1, :] = ffn_gain[:, i * lanes : (i + 1) * lanes]
     heads = (small_ref.shape[0] - 2 * rows) // groups
-    table = get(7)[:heads, :]
+    table = get(5)[:heads, :]
     for i in range(groups):
         at = 2 * rows + i * heads
         small_ref[at : at + heads, :] = jnp.where(group == i, table, 0.0)
@@ -893,24 +1035,47 @@
 
 
 def qkv_grad(
-    place, grads, normed_first, normed_last, gain, gain_grad, table, head_count, w_query, w_key, w_value
+    place,
+    grads,
+    normed_first,
+    normed_last,
+    gain,
+    gain_grad,
+    table,
+    head_count,
+    w_query,
+    w_key,
+    w_value,
 ):
-    rows, width = 4 * grads[0].shape[0], normed_first.shape[1]
-    span = grads[0].shape[1]
+    rows, width = 4 * grads[0].shape[1], normed_first.shape[1]
+    local = width // groups
     count = 2 * width // 128 + head_count
     return kernel_call(
         qkv_grad_body,
         "qkv_grad",
         [place],
-        [*grads, normed_first, gain, gain_grad, table, w_query, w_key, w_value, normed_last],
         [
-            shaped(f32, 2, width // 4, span),
-            shaped(bf16, width // 2 + room(count), span),
+            *grads,
+            normed_first,
+            gain,
+            gain_grad,
+            table,
+            w_query,
+            w_key,
+            w_value,
+            normed_last,
+        ],
+        [
+            shaped(f32, 2, width // 4, 3 * local),
+            shaped(bf16, width // 2 + room(count), 3 * local),
             shaped(f32, count, 128),
         ],
-        scratch=[pltpu.VMEM((rows, span), bf16), pltpu.VMEM((width, span), f32)],
-        mebibytes=7,
-        us=0.5,
+        scratch=[
+            pltpu.VMEM((rows, 3 * local), bf16),
+            pltpu.VMEM((width, 3 * local), f32),
+        ],
+        mebibytes=10,
+        us=0.01,
     )
 
 
@@ -923,9 +1088,9 @@
     ]
     summed = attached(received, parts * rows, small[...])
     if axis == "y":
+        outs[-1][...] = summed
         for i in range(parts):
             outs[0][i] = totals[i].astype(outs[0].dtype)
-        outs[1][...] = summed
         return
     kept_ref, sent_ref, small_ref = outs
     small_ref[...] = summed
@@ -964,22 +1129,22 @@
         [place],
         [kept, small, received],
         outputs + [shaped(f32, count, 128)],
-        us=0.5,
+        us=0.01,
     )
 
 
 def input_grad_body(smem, get, outs, all_scr):
     (place,) = smem
     group = place[0]
-    weights = [get(7 + i) for i in range(3)]
-    local = get(0).shape[1] // 3
+    weights = [get(6 + i) for i in range(3)]
+    local = get(0).shape[2] // 3
     window = -(-local // 128) * 128
-    tok = get(0).shape[0]
+    tok = get(0).shape[1]
     spare = jnp.zeros((tok, window - local), bf16)
     all_scr[...] = jnp.zeros_like(all_scr)
     for d in range(4):
         start, late = group_window(group ^ d, local)
-        grads = get(d)[...]
+        grads = get((0, 2, 1, 2)[d])[d // 3]
         for i in range(3):
             part = grads[:, i * local : (i + 1) * local]
             part = jnp.where(
@@ -991,11 +1156,11 @@
     normed_grad = dot(all_scr[0], weights[0][...], 1, 1)
     for i in range(1, 3):
         normed_grad = normed_grad + dot(all_scr[i], weights[i][...], 1, 1)
-    values = get(4)[...].astype(f32)
+    values = get(3)[...].astype(f32)
     scale = rms_scale(values)
     unit = values * scale
-    scaled = normed_grad * get(5)[...]
-    outs[0][...] = get(6)[...] + scale * (
+    scaled = normed_grad * get(4)[...]
+    outs[0][...] = get(5)[...] + scale * (
         scaled - unit * jnp.mean(unit * scaled, axis=1, keepdims=True)
     )
 
@@ -1008,56 +1173,33 @@
         [*grads, tokens, gain, middle_grad, w_query, w_key, w_value],
         [shaped(f32, *tokens.shape)],
         scratch=[pltpu.VMEM((3, *tokens.shape), bf16)],
-        staged=(0, 1, 2, 3, 4, 6),
+        staged=(0, 1, 2, 3, 5),
         mebibytes=6,
-        us=0.5,
+        us=0.01,
     )[0]
 
 
-def add_split_body(smem, get, outs, *, bit, splits):
-    (place,) = smem
-    kept, received = get(0), get(1)
-    if kept.shape[0] == 1:
-        total = kept[0].astype(f32) + received[0].astype(f32)
-        at = 0
-        for i, span in enumerate(splits):
-            outs[i][...] = total[:, at : at + span].astype(outs[i].dtype)
-            at += span
-        return
-    odd = ((place[5] >> bit) & 1) == 1
-    for i in range(kept.shape[0] // 2):
-        even_rows = kept[2 * i].astype(f32) + received[2 * i].astype(f32)
-        odd_rows = kept[2 * i + 1].astype(f32) + received[2 * i + 1].astype(f32)
-        outs[1][i] = jnp.where(odd, even_rows, odd_rows).astype(bf16)
-        outs[0][i] = jnp.where(odd, odd_rows, even_rows)
-
-
-def wide_sum(layout, place, kept, sent, bit, splits, name, us, first=(), last=f32):
-    received = layout.wide_bit(sent, bit)
-    kept = after(kept, first)
-    remaining, block, columns = kept.shape
-    if remaining == 1:
-        outputs = [shaped(last, block, span) for span in splits]
-    else:
-        shape = (remaining // 2, block, columns)
-        outputs = [shaped(f32, *shape), shaped(bf16, *shape)]
-    return kernel_call(
-        functools.partial(add_split_body, bit=bit + 1, splits=splits),
-        f"{name}_sum",
-        [place],
-        [kept, received],
-        outputs,
-        us=us,
-    )
-
-
-def turned_down_body(smem, get, outs):
-    outs[0][...] = jnp.transpose(get(0)[...].astype(f32))
-
-
-def turned_down(block):
-    return kernel_call(
-        turned_down_body, "down_out", [], [block], [shaped(f32, *block.shape[::-1])], us=1
+def stacked_body(smem, get, outs):
+    rows = get(0).shape[0]
+    outs[0][:rows, :] = get(0)[...]
+    outs[0][rows:, :] = get(1)[...]
+
+
+def stacked(first, second):
+    rows, width = first.shape
+    return kernel_call(
+        stacked_body, "stacked", [], [first, second], [shaped(bf16, 2 * rows, width)], us=0.01
+    )[0]
+
+
+def forwarded_body(smem, get, outs):
+    outs[0][0] = get(0)[1]
+    outs[0][1] = get(1)[1]
+
+
+def forwarded(near, far):
+    return kernel_call(
+        forwarded_body, "forwarded", [], [near, far], [shaped(bf16, *near.shape)], us=0.01
     )[0]
 
 
@@ -1114,37 +1256,44 @@
         while size < s_count:
             own[d] = jnp.concatenate([own[d], layout.wide_bit(own[d], size.bit_length())], axis=0)
             size *= 2
-    cot_across = layout.across(out_grad)
     bias = bias_rows(place, bias_table, 4 * tok)
     kv_first, q_first, normed_first = project(place, own[:3], gain_attn, w_query, w_key, w_value)
-    kv_first = after(kv_first, (bias, cot_across))
+    kv_first = after(kv_first, bias)
+    cot = after(out_grad, kv_first)
+    cot = [out_grad, layout.near_group(cot), layout.far_group(cot)]
     kv_last, q_last, normed_last = project(place, own[3:], gain_attn, w_query, w_key, w_value)
     kv = [kv_first, kv_last, layout.core(kv_first), layout.core(kv_last)]
     outs = attention_forward(place, kv, [q_first, q_last], bias)
     ctx_parts = outs[:4]
     q_own, k_all, v_all, o_own, probs = outs[4:]
+    ctx_parts = after(ctx_parts, cot)
     ctx = [layout.turned(ctx_parts[d], d) for d in range(4)]
-    cot = [out_grad, layout.core(out_grad), cot_across, layout.core(cot_across)]
-    ctx = after(ctx, cot)
+    cot.append(layout.near_group(after(cot[2], ctx)))
 
     middle, normed_ffn, hidden, act, slope = ffn_forward(
         place, ctx, tokens, gain_ffn, w_out, w_gate, w_up
     )
-    normed_across = layout.across(normed_ffn)
+    bits = layout.wide.bit_length() - 1
+    normed_far = layout.far_group(normed_ffn)
     back = ffn_backward(
         place, out_grad, middle, hidden, act, slope, gain_ffn, ctx, w_down, w_gate, w_up, w_out
     )
     output, middle_grad, grad_gain_ffn = back[0:3]
     dctx = [layout.turned(back[3 + d], d) for d in range(4)]
     mine, far = back[7:9]
-    normed_near, normed_across = after((normed_ffn, normed_across), back[3:7])
-    normed_core = layout.core(normed_near)
-    normed = [normed_ffn, normed_core, normed_across, layout.core(normed_across)]
-    *down, gate, up, normed = down_grad(place, normed, cot, w_gate, w_up, w_down, layout.wide)
-
-    dctx = after(dctx, down)
+    far = layout.across(after(far, dctx[0]))
+    normed_near, normed_far = after((normed_ffn, normed_far), dctx[1])
+    normed = [
+        normed_ffn,
+        layout.near_group(normed_near),
+        normed_far,
+        layout.near_group(normed_far),
+    ]
+
+    dctx = after(dctx, cot[3])
     back = attention_backward(place, dctx, q_own, k_all, v_all, o_own, probs)
     dq, kept, sent, table_rows = back[:4], back[4], back[5], back[6]
+
     received = layout.core(sent)
     size = s_count
     while size > 1:
@@ -1152,16 +1301,15 @@
         total = kept.astype(f32) + received.astype(f32)
         kept = total[:size]
         received = layout.wide_bit(total[size:].astype(bf16), size.bit_length())
-
-    far, mine, up = after((far, mine, up), sent)
-    far = layout.across(far)
-    mine_core = layout.core(mine)
-    up = up_grad(place, normed, up, layout.wide)
-    quarter_ff = ff // layout.narrow
-    bits = layout.wide.bit_length() - 1
-    width_sum = functools.partial(wide_sum, layout, place)
-    down = width_sum(*down, 0, (local,), "down", 0.5, up, last=bf16)
-    low_grads = collect(dq, after(kept[0], down), received[0])
+    normed, cot, mine, far = after((normed, cot, mine, far), sent)
+    normed = normed + [layout.core(block) for block in normed]
+    cot = cot + [layout.core(block) for block in cot]
+    out_parts = [mine, layout.core(mine), far, layout.core(far)]
+    low_grads = collect(dq, kept[0], received[0])
+    ffn_kept, ffn_sent = ffn_grad(
+        place, after(normed, low_grads), cot, w_gate, w_up, w_down, s_count
+    )
+    normed_first = after(normed_first, ffn_sent)
     qkv_kept, qkv_sent, small = qkv_grad(
         place,
         low_grads,
@@ -1175,37 +1323,37 @@
         w_key,
         w_value,
     )
-    up = width_sum(*up, 0, (quarter_ff,), "up", 0.5, qkv_sent)
-    far = after(far, low_grads)
-    outs_parts = [mine, mine_core, far, layout.core(far)]
-    normed = after(normed, up[0])
-    gate = gate_grad(place, normed, gate, outs_parts, layout.wide)
-    low_grads = after(low_grads, gate[1])
-    returned = [layout.turned(low_grads[d], d) for d in range(4)]
-    down = width_sum(*down, 1, (local,), "down", 0.5, gate, last=bf16)
+    out = out_weight_grad(place, after(out_parts, qkv_sent), layout.wide)
+
+    returned = [layout.turned(low_grads[0], 0), layout.turned(low_grads[1], 2)]
+    qkv_kept = after(qkv_kept, out)
+    step = qkv_sum(place, qkv_kept, small, layout.core(qkv_sent), "core", s_count, layout.wide)
+    ffn_kept, ffn_sent = ffn_sum(place, after(ffn_kept, step), layout.across(ffn_sent))
+    out_kept, out_sent = after(out, ffn_sent)
     step = qkv_sum(
-        place, after(qkv_kept, down), small, layout.core(qkv_sent), "core", s_count, layout.wide
-    )
-    up = width_sum(*up, 1, (quarter_ff,), "up", 0.5, step)
-    for bit in range(2, bits):
-        down = width_sum(*down, bit, (local,), "down", 0.5, up, last=bf16)
-    step = qkv_sum(
-        place, after(step[0], down), step[2], layout.across(step[1]), "x", s_count, layout.wide
-    )
-    gate = width_sum(*gate, 0, (quarter_ff, local), "gate", 0.5, step)
-    middle_grad = after(middle_grad, gate)
-    input_grad = final_input_grad(
-        place, returned, tokens, gain_attn, middle_grad, w_query, w_key, w_value
-    )
-    for bit in range(2, bits):
-        up = width_sum(*up, bit, (quarter_ff,), "up", 0.5, input_grad)
+        place, after(step[0], ffn_kept), step[2], layout.across(step[1]), "x", s_count, layout.wide
+    )
+    received = layout.wide_bit(ffn_sent, 0)
+    size = s_count
+    bit = 1
+    while size > 1:
+        size //= 2
+        total = (ffn_kept + received.astype(f32)).reshape(size, 2, *ffn_kept.shape[1:])
+        ffn_kept, ffn_sent = halved(total, 1, (s_own >> (bit - 1)) & 1)
+        received = layout.wide_bit(ffn_sent.astype(bf16), bit)
+        bit += 1
+    onward = forwarded(returned[0], after(returned[1], step))
+    returned.append(layout.wide_bit(onward, bits - 2))
+    ffn_parts = ffn_last(place, after(ffn_kept, onward), received, local)
     part, small = qkv_sum(
-        place, after(step[0], up), step[2], layout.wide_bit(step[1], 0), "y", s_count, layout.wide
-    )
-    gate = width_sum(*gate, 1, (quarter_ff, local), "gate", 0.5, part)
-    small = after(small, gate[0])
-    for bit in range(2, bits):
-        gate = width_sum(*gate, bit, (quarter_ff, local), "gate", 0.5, part)
+        place,
+        after(step[0], ffn_parts),
+        step[2],
+        layout.wide_bit(step[1], 0),
+        "y",
+        s_count,
+        layout.wide,
+    )
     rows = width // layout.wide
     size = s_count
     bit = 1
@@ -1214,18 +1362,48 @@
         part = part.reshape(size, 2, rows, 3 * local)
         kept, sent = halved(part, 1, (s_own >> (bit - 1)) & 1)
         part = kept + layout.wide_bit(sent.astype(bf16), bit).astype(f32)
+        small = small + layout.wide_bit(small, bit)
         bit += 1
     part = part.reshape(rows, 3 * local).astype(bf16)
 
-    def to_owner(x, c, g, s, y):
-        return (g // 2, g % 2, x * 2 + c, s, y)
-
-    final_qkv = layout.send(part, to_owner).astype(f32)
-    final_down = turned_down(layout.send(down[0], to_owner)).T
-    (final_up,), (final_gate, final_out) = up, gate
-
-    for bit in range(1, bits):
-        small = small + layout.wide_bit(small, bit)
+    for bit in range(bits - 1):
+        riding = ("in",) * (bit > bits - 3) + ("out",) * (bit > bits - 4)
+        first = small if riding else part
+        if bit == bits - 2:
+            middle_grad = after(middle_grad, out_sent)
+            input_grad = final_input_grad(
+                place, returned, tokens, gain_attn, middle_grad, w_query, w_key, w_value
+            )
+            first = input_grad
+        outs = out_sum(layout, place, after(out_kept, first), out_sent, bit, small, riding)
+        out_kept, out_sent = outs[:2]
+        if "in" in riding:
+            small = outs[2]
+
+    def half_owner(flip):
+        return lambda x, c, g, s, y: (g % 2, c, x + 2 * (g // 2 ^ flip), s, y)
+
+    def down_owner(x, c, g, s, y):
+        at = g // 2 * s_count + s
+        return (x, y, g % 2 * 2 + c, at // 2, at % 2)
+
+    final_gate, final_up, final_down = ffn_owned(
+        place,
+        layout.send(ffn_parts[0], half_owner(0)),
+        layout.send(ffn_parts[1], half_owner(1)),
+        layout.send(ffn_parts[2], down_owner),
+    )
+    part = layout.send(part, lambda x, c, g, s, y: (g // 2, g % 2, x * 2 + c, s, y)).astype(f32)
+    final_query, final_key, final_value = (
+        part[:, :local],
+        part[:, local : 2 * local],
+        part[:, 2 * local :],
+    )
+
+    out_kept = after(out_kept, final_gate)
+    final_out, small = out_sum(
+        layout, place, out_kept, out_sent, bits - 1, small, ("in",)
+    )
     gain_rows = width // 128
     sum_gain_attn = small[:gain_rows].reshape(width)
     sum_gain_ffn = small[gain_rows : 2 * gain_rows].reshape(width)
@@ -1234,14 +1412,14 @@
         output[None],
         input_grad[None],
         sum_gain_attn,
-        final_qkv[:, :local],
-        final_qkv[:, local : 2 * local],
-        final_qkv[:, 2 * local :],
+        final_query,
+        final_key,
+        final_value,
         final_out,
         sum_gain_ffn,
         final_gate,
         final_up,
-        final_down,
+        final_down.T,
         sum_table,
     )
 

time: 162 us -> 155 us (0.957)
  Pallas kernels: 56.6 us -> 52.6 us
    pallas_call x27 -> x23, Pallas kernels: 56.6 us -> 52.6 us  [kernel_call(): pl.pallas_call(kernel, out_shape=outputs, in_specs=[pl.BlockSpec(memory_s...]
    ppermute x44 -> x47, waiting for transfers between devices: 47.3 us -> 45.9 us  [send(): return lax.ppermute(block, axes, route)]
    ppermute x44 -> x47, starting transfers between devices: 51.8 us -> 51.7 us  [send(): return lax.ppermute(block, axes, route)]
  transfers between devices with their start and end apart: 44 -> 47, of which waited for: 16 -> 16; matrix products, arithmetic and copies ran while one was open for 1% -> 1% of each run, Pallas kernels for 32% -> 28%
where the time goes in v2:
time: 155 us; the launch traced here: 153 us
  Pallas kernels  52.6 us (34%)
  starting transfers between devices  51.7 us (33%)
  waiting for transfers between devices  45.9 us (30%)
  local copies, waits for them, and re-layouts  2.19 us (1%)
    pallas_call x23, Pallas kernels, kernel_call(): pl.pallas_call(kernel, out_shape=outputs, in_specs=[pl.BlockSpec(memory_s...  52.6 us
    ppermute x47, starting transfers between devices, send(): return lax.ppermute(block, axes, route)  51.7 us
    ppermute x47, waiting for transfers between devices, send(): return lax.ppermute(block, axes, route)  45.9 us
  transfers between devices with their start and end apart: 47, of which 16 were waited for; matrix products, arithmetic and copies ran while one was open for 1% of the time, Pallas kernels for 28%

profile of v2, /device:TPU:2, one launch (start us, length us, event | category | flops | bytes accessed | tf_op | source)
XLA Modules:
  0.0 153.5 jit_solution(6338185942732377092)
XLA Ops:
  0.7 1.7 %pack.1 = bf16[144,768]{1,0:T(8,128)(2,1)} custom-call(bf16[128,768]{1,0:T(8,128)(2,1)} %bitcast.24, s32[1,128]{1,0:T(1,128)} %refs_1_.2), custom_call_target="tpu_custom_call" | custom-call | flops 1150000000 | bytes 1024 | tf_op jit(solution)/shard_map/pack/pallas_call | solution.py:132
  2.3 2.7 %collective-permute-start.2 = (bf16[144,768]{1,0:T(8,128)(2,1)}, bf16[144,768]{1,0:T(8,128)(2,1)S(1)}, u32[]{:S(2)}, u32[]{:S(2)}) collective-permute-start(bf16[144,768]{1,0:T(8,128)(2,1)} %pack.1), channel_id=1, source_target_pairs={{0,4},{1,12},{2,6},{3,14},{4,0},{5,8},{6,2},{7,10},{8,5},{9,13},{1... | collective-permute-start | bytes 663560 | tf_op jit(solution)/shard_map/ppermute | solution.py:46
  9.2 7.1 %collective-permute-done.2 = bf16[144,768]{1,0:T(8,128)(2,1)S(1)} collective-permute-done((bf16[144,768]{1,0:T(8,128)(2,1)}, bf16[144,768]{1,0:T(8,128)(2,1)S(1)}, u32[]{:S(2)}, u32[]{:S(2)}) %collective-permute-start.2) | collective-permute-done | bytes 221216 | tf_op jit(solution)/shard_map/ppermute | solution.py:46
  17.4 2.2 %project.2 = (bf16[3,1,128,512]{3,2,1,0:T(8,128)(2,1)S(1)}, bf16[3,128,192]{2,1,0:T(8,128)(2,1)S(1)}, bf16[384,768]{1,0:T(8,128)(2,1)S(1)}) custom-call(s32[6]{0:T(128)S(1)} %stack.24.refs_0_, bf16[1,144,768]{2,1,0:T(8,128)(2,1)S(1)} %bitcast.34, bf16[1,144,768]{2,1,0:T(8,128)(2,1)S(1)} %bitcast.35, bf16[1,144,768]{2,1,0:T(8,128)(2,1)S(1)} %bitcast.33, ...), custom_call_target="tpu_custom_call" | custom-call | flops 3449999872 | bytes 1024 | tf_op jit(solution)/shard_map/project/pallas_call | solution.py:132
  20.4 3.3 %collective-permute-done.3.refs_1_ = bf16[1,144,768]{2,1,0:T(8,128)(2,1)S(1)} collective-permute-done((bf16[1,144,768]{2,1,0:T(8,128)(2,1)S(1)}, bf16[1,144,768]{2,1,0:T(8,128)(2,1)S(1)}, u32[]{:S(2)}, u32[]{:S(2)}) %collective-permute-start.3) | collective-permute-done | bytes 221216 | tf_op jit(solution)/shard_map/ppermute | solution.py:46
  23.6 1.8 %project.3 = (bf16[1,1,128,512]{3,2,1,0:T(8,128)(2,1)S(1)}, bf16[1,128,192]{2,1,0:T(8,128)(2,1)S(1)}, bf16[128,768]{1,0:T(8,128)(2,1)S(1)}) custom-call(s32[6]{0:T(128)S(1)} %stack.24.refs_0_, bf16[1,144,768]{2,1,0:T(8,128)(2,1)S(1)} %collective-permute-done.3.refs_1_, f32[1,768]{1,0:T(1,128)S(1)} %broadcast_in_dim.24.refs_4_.refs_2_.refs_5_, ...), custom_call_target="tpu_custom_call" | custom-call | flops 3449999872 | bytes 1024 | tf_op jit(solution)/shard_map/project/pallas_call | solution.py:132
  26.8 2.7 %collective-permute-start.7 = (bf16[128,768]{1,0:T(8,128)(2,1)S(1)}, bf16[128,768]{1,0:T(8,128)(2,1)S(1)}, u32[]{:S(2)}, u32[]{:S(2)}) collective-permute-start(bf16[128,768]{1,0:T(8,128)(2,1)S(1)} %bitcast.28), channel_id=1, source_target_pairs={{0,4},{1,5},{2,6},{3,7},{4,0},{5,1},{6,2},{7,3},{8,12},{9,13},{10,... | collective-permute-start | bytes 589832 | tf_op jit(solution)/shard_map/ppermute | solution.py:46
  29.6 9.8 %attention_forward.1 = (bf16[128,192]{1,0:T(8,128)(2,1)S(1)}, bf16[128,192]{1,0:T(8,128)(2,1)S(1)}, bf16[128,192]{1,0:T(8,128)(2,1)S(1)}, bf16[128,192]{1,0:T(8,...) custom-call(s32[6]{0:T(128)S(1)} %stack.24.refs_0_, ...), custom_call_target="tpu_custom_call" | custom-call | flops 11500000256 | bytes 1024 | tf_op jit(solution)/shard_map/attention_forward/pallas_call | solution.py:132
  39.7 2.5 %collective-permute-start.11 = (bf16[128,192]{1,0:T(8,128)(2,1)S(1)}, bf16[128,192]{1,0:T(8,128)(2,1)S(1)}, u32[]{:S(2)}, u32[]{:S(2)}) collective-permute-start(bf16[128,192]{1,0:T(8,128)(2,1)S(1)} %get-tuple-element.142), channel_id=1, source_target_pairs={{0,6},{1,14},{2,4},{3,12},{4,2},{5,10},{6,0},{7,8},{8,7},{9,15},{1... | collective-permute-start | bytes 147464 | tf_op jit(solution)/shard_map/ppermute | solution.py:46
  43.9 3.8 %collective-permute-done.10.refs_3_.refs_13_ = bf16[128,192]{1,0:T(8,128)(2,1)S(1)} collective-permute-done((bf16[128,192]{1,0:T(8,128)(2,1)S(1)}, bf16[128,192]{1,0:T(8,128)(2,1)S(1)}, u32[]{:S(2)}, u32[]{:S(2)}) %collective-permute-start.10) | collective-permute-done | bytes 49184 | tf_op jit(solution)/shard_map/ppermute | solution.py:46
  48.3 3.1 %ffn_forward.1 = (f32[128,768]{1,0:T(8,128)S(1)}, bf16[128,768]{1,0:T(8,128)(2,1)S(1)}, bf16[128,2048]{1,0:T(8,128)(2,1)S(1)}, f32[128,2048]{1,0:T(8,128)S(1)}, f32[128,2048]{1,0:T(8,128)S(1)}) custom-call(s32[6]{0:T(128)S(1)} %stack.24.refs_0_, bf16[128,192]{1,0:T(8,128)(2,1)S(1)} %collective-permute-done.8.refs_1_.refs_11_, ...), custom_call_target="tpu_custom_call" | custom-call | flops 16099999744 | bytes 1024 | tf_op jit(solution)/shard_map/ffn_forward/pallas_call | solution.py:132
  53.3 5.5 %ffn_backward.1 = (bf16[128,768]{1,0:T(8,128)(2,1)}, f32[128,768]{1,0:T(8,128)S(1)}, f32[1,768]{1,0:T(1,128)S(1)}, bf16[128,192]{1,0:T(8,128)(2,1)S(1)}, bf16[12...) custom-call(s32[6]{0:T(128)S(1)} %stack.24.refs_0_, ...), custom_call_target="tpu_custom_call" | custom-call | flops 6899999744 | bytes 1024 | tf_op jit(solution)/shard_map/ffn_backward/pallas_call | solution.py:132
  61.3 1.9 %collective-permute-start.14 = (bf16[128,192]{1,0:T(8,128)(2,1)S(1)}, bf16[128,192]{1,0:T(8,128)(2,1)S(1)}, u32[]{:S(2)}, u32[]{:S(2)}) collective-permute-start(bf16[128,192]{1,0:T(8,128)(2,1)S(1)} %get-tuple-element.150), channel_id=1, source_target_pairs={{0,4},{1,12},{2,6},{3,14},{4,0},{5,8},{6,2},{7,10},{8,5},{9,13},{1... | collective-permute-start | bytes 147464 | tf_op jit(solution)/shard_map/ppermute | solution.py:46
  63.2 1.9 %collective-permute-done.13.refs_2_ = bf16[128,192]{1,0:T(8,128)(2,1)S(1)} collective-permute-done((bf16[128,192]{1,0:T(8,128)(2,1)S(1)}, bf16[128,192]{1,0:T(8,128)(2,1)S(1)}, u32[]{:S(2)}, u32[]{:S(2)}) %collective-permute-start.13) | collective-permute-done | bytes 49184 | tf_op jit(solution)/shard_map/ppermute | solution.py:46
  65.1 1.9 %collective-permute-start.15 = (bf16[128,192]{1,0:T(8,128)(2,1)S(1)}, bf16[128,192]{1,0:T(8,128)(2,1)S(1)}, u32[]{:S(2)}, u32[]{:S(2)}) collective-permute-start(bf16[128,192]{1,0:T(8,128)(2,1)S(1)} %get-tuple-element.151), channel_id=1, source_target_pairs={{0,6},{1,14},{2,4},{3,12},{4,2},{5,10},{6,0},{7,8},{8,7},{9,15},{1... | collective-permute-start | bytes 147464 | tf_op jit(solution)/shard_map/ppermute | solution.py:46
  67.3 1.8 %collective-permute-start.22 = (bf16[128,768]{1,0:T(8,128)(2,1)S(1)}, bf16[128,768]{1,0:T(8,128)(2,1)S(1)}, u32[]{:S(2)}, u32[]{:S(2)}) collective-permute-start(bf16[128,768]{1,0:T(8,128)(2,1)S(1)} %collective-permute-done.20.refs_3_), channel_id=1, source_target_pairs={{0,2},{1,3},{2,0},{3,1},{4,6},{5,7},{6,4},{7,5},{8,10},{9,11},{10,... | collective-permute-start | bytes 589832 | tf_op jit(solution)/shard_map/ppermute | solution.py:46
  69.1 2.2 %collective-permute-done.15.refs_4_ = bf16[128,192]{1,0:T(8,128)(2,1)S(1)} collective-permute-done((bf16[128,192]{1,0:T(8,128)(2,1)S(1)}, bf16[128,192]{1,0:T(8,128)(2,1)S(1)}, u32[]{:S(2)}, u32[]{:S(2)}) %collective-permute-start.15) | collective-permute-done | bytes 49184 | tf_op jit(solution)/shard_map/ppermute | solution.py:46
  71.2 8.0 %attention_backward.1 = (bf16[128,192]{1,0:T(8,128)(2,1)S(1)}, bf16[128,192]{1,0:T(8,128)(2,1)S(1)}, bf16[128,192]{1,0:T(8,128)(2,1)S(1)}, bf16[128,192]{1,0:T(8...) custom-call(s32[6]{0:T(128)S(1)} %stack.24.refs_0_, ...), custom_call_target="tpu_custom_call" | custom-call | flops 11500000 | bytes 1024 | tf_op jit(solution)/shard_map/attention_backward/pallas_call | solution.py:132
  79.3 5.1 %collective-permute-start.17 = (bf16[1,4,128,384]{3,2,1,0:T(8,128)(2,1)S(1)}, bf16[1,4,128,384]{3,2,1,0:T(8,128)(2,1)S(1)}, u32[]{:S(2)}, u32[]{:S(2)}) collective-permute-start(bf16[1,4,128,384]{3,2,1,0:T(8,128)(2,1)S(1)} %get-tuple-element.167), channel_id=1, source_target_pairs={{0,8},{1,9},{2,10},{3,11},{4,12},{5,13},{6,14},{7,15},{8,0},{9,1},... | collective-permute-start | bytes 1179656 | tf_op jit(solution)/shard_map/ppermute | solution.py:46
  88.4 3.6 %ffn_grad.1 = (f32[2,64,2304]{2,1,0:T(8,128)S(1)}, bf16[2,64,2304]{2,1,0:T(8,128)(2,1)S(1)}) custom-call(s32[6]{0:T(128)S(1)} %stack.24.refs_0_, bf16[128,768]{1,0:T(8,128)(2,1)S(1)} %get-tuple-element.181.refs_1_, bf16[128,768]{1,0:T(8,128)(2,1)S(1)} %collective-permute-done.21.refs_2_, bf16[128,768]{1,0:T(8,128)(2,1)S(1)} %collective-permute-done.20.refs_3_, ...), custom_call_target="tpu_custom_call" | custom-call | flops 11500000 | bytes 1024 | tf_op jit(solution)/shard_map/ffn_grad/pallas_call | solution.py:132
  92.9 2.6 %qkv_grad.1 = (f32[2,192,576]{2,1,0:T(8,128)S(1)}, bf16[416,576]{1,0:T(8,128)(2,1)S(1)}, f32[24,128]{1,0:T(8,128)S(1)}) custom-call(s32[6]{0:T(128)S(1)} %stack.24.refs_0_, bf16[2,128,576]{2,1,0:T(8,128)(2,1)S(1)} %get-tuple-element.168.refs_1_, bf16[2,128,576]{2,1,0:T(8,128)(2,1)S(1)} %get-tuple-element.169.refs_2_, ...), custom_call_target="tpu_custom_call" | custom-call | flops 11500000 | bytes 1024 | tf_op jit(solution)/shard_map/qkv_grad/pallas_call | solution.py:132
  96.1 1.8 %collective-permute-done.32.refs_2_ = bf16[128,1152]{1,0:T(8,128)(2,1)S(1)} collective-permute-done((bf16[128,1152]{1,0:T(8,128)(2,1)S(1)}, bf16[128,1152]{1,0:T(8,128)(2,1)S(1)}, u32[]{:S(2)}, u32[]{:S(2)}) %collective-permute-start.32) | collective-permute-done | bytes 294944 | tf_op jit(solution)/shard_map/ppermute | solution.py:46
  102.2 6.0 %collective-permute-done.35.refs_2_ = bf16[2,64,2304]{2,1,0:T(8,128)(2,1)S(1)} collective-permute-done((bf16[2,64,2304]{2,1,0:T(8,128)(2,1)S(1)}, bf16[2,64,2304]{2,1,0:T(8,128)(2,1)S(1)}, u32[]{:S(2)}, u32[]{:S(2)}) %collective-permute-start.35) | collective-permute-done | bytes 589856 | tf_op jit(solution)/shard_map/ppermute | solution.py:46
  109.8 4.0 %collective-permute-done.36.refs_3_ = bf16[224,576]{1,0:T(8,128)(2,1)S(1)} collective-permute-done((bf16[224,576]{1,0:T(8,128)(2,1)S(1)}, bf16[224,576]{1,0:T(8,128)(2,1)S(1)}, u32[]{:S(2)}, u32[]{:S(2)}) %collective-permute-start.36) | collective-permute-done | bytes 258080 | tf_op jit(solution)/shard_map/ppermute | solution.py:46
  115.2 3.2 %collective-permute-done.19.refs_1_.refs_2_ = bf16[2,128,576]{2,1,0:T(8,128)(2,1)S(1)} collective-permute-done((bf16[2,128,576]{2,1,0:T(8,128)(2,1)S(1)}, bf16[2,128,576]{2,1,0:T(8,128)(2,1)S(1)}, u32[]{:S(2)}, u32[]{:S(2)}) %collective-permute-start.19) | collective-permute-done | bytes 294944 | tf_op jit(solution)/shard_map/ppermute | solution.py:46
  120.0 2.0 %collective-permute-done.38.refs_2_ = bf16[1,64,2304]{2,1,0:T(8,128)(2,1)S(1)} collective-permute-done((bf16[1,64,2304]{2,1,0:T(8,128)(2,1)S(1)}, bf16[1,64,2304]{2,1,0:T(8,128)(2,1)S(1)}, u32[]{:S(2)}, u32[]{:S(2)}) %collective-permute-start.38) | collective-permute-done | bytes 294944 | tf_op jit(solution)/shard_map/ppermute | solution.py:46
  123.3 5.8 %collective-permute-start.42 = (bf16[96,512]{1,0:T(8,128)(2,1)S(1)}, bf16[96,512]{1,0:T(8,128)(2,1)S(1)}, u32[]{:S(2)}, u32[]{:S(2)}) collective-permute-start(bf16[96,512]{1,0:T(8,128)(2,1)S(1)} %get-tuple-element.225), channel_id=1, source_target_pairs={{0,0},{1,1},{2,16},{3,17},{4,4},{5,5},{6,20},{7,21},{8,8},{9,9},{1... | collective-permute-start | bytes 294920 | tf_op jit(solution)/shard_map/ppermute | solution.py:46
  129.1 3.1 %collective-permute-start.43 = (bf16[96,512]{1,0:T(8,128)(2,1)S(1)}, bf16[96,512]{1,0:T(8,128)(2,1)S(1)}, u32[]{:S(2)}, u32[]{:S(2)}) collective-permute-start(bf16[96,512]{1,0:T(8,128)(2,1)S(1)} %get-tuple-element.226), channel_id=1, source_target_pairs={{0,4},{1,5},{2,20},{3,21},{4,0},{5,1},{6,16},{7,17},{8,12},{9,13},... | collective-permute-start | bytes 294920 | tf_op jit(solution)/shard_map/ppermute | solution.py:46
  133.4 1.9 %collective-permute-start.46 = (bf16[96,576]{1,0:T(8,128)(2,1)S(1)}, bf16[96,576]{1,0:T(8,128)(2,1)S(1)}, u32[]{:S(2)}, u32[]{:S(2)}) collective-permute-start(bf16[96,576]{1,0:T(8,128)(2,1)S(1)} %bitcast.36), channel_id=1, source_target_pairs={{0,0},{1,1},{2,8},{3,9},{4,16},{5,17},{6,24},{7,25},{8,2},{9,3},{1... | collective-permute-start | bytes 331784 | tf_op jit(solution)/shard_map/ppermute | solution.py:46
  135.4 2.5 %collective-permute-done.42.refs_1_ = bf16[96,512]{1,0:T(8,128)(2,1)S(1)} collective-permute-done((bf16[96,512]{1,0:T(8,128)(2,1)S(1)}, bf16[96,512]{1,0:T(8,128)(2,1)S(1)}, u32[]{:S(2)}, u32[]{:S(2)}) %collective-permute-start.42) | collective-permute-done | bytes 98336 | tf_op jit(solution)/shard_map/ppermute | solution.py:46
  139.3 4.0 %input_grad.1 = f32[128,768]{1,0:T(8,128)} custom-call(s32[6]{0:T(128)S(1)} %stack.24.refs_0_, bf16[2,128,576]{2,1,0:T(8,128)(2,1)S(1)} %collective-permute-done.18.refs_0_.refs_1_, bf16[2,128,576]{2,1,0:T(8,128)(2,1)S(1)} %collective-permute-done.19.refs_1_.refs_2_, bf16[2,128,576]{2,1,0:T(8,128)(2,1)S(1)} %collective-permute-done.37.refs_3_, ...), custom_call_target="tpu_custom_call" | custom-call | flops 11500000 | bytes 1024 | tf_op jit(solution)/shard_map/input_grad/pallas_call | solution.py:132
  144.8 6.3 %collective-permute-done.45.refs_2_ = bf16[160,192]{1,0:T(8,128)(2,1)S(1)} collective-permute-done((bf16[160,192]{1,0:T(8,128)(2,1)S(1)}, bf16[160,192]{1,0:T(8,128)(2,1)S(1)}, u32[]{:S(2)}, u32[]{:S(2)}) %collective-permute-start.45) | collective-permute-done | bytes 61472 | tf_op jit(solution)/shard_map/ppermute | solution.py:46
  (116 shorter events, 36.7 us)
Async XLA Ops:
  2.3 14.0 %collective-permute-start.2 = (bf16[144,768]{1,0:T(8,128)(2,1)}, bf16[144,768]{1,0:T(8,128)(2,1)S(1)}, u32[]{:S(2)}, u32[]{:S(2)}) collective-permute-start(bf16[144,768]{1,0:T(8,128)(2,1)} %pack.1), channel_id=1, source_target_pairs={{0,4},{1,12},{2,6},{3,14},{4,0},{5,8},{6,2},{7,10},{8,5},{9,13},{1... | collective-permute-start | bytes 663560 | tf_op jit(solution)/shard_map/ppermute | solution.py:46
  5.0 12.4 %collective-permute-start = (bf16[144,768]{1,0:T(8,128)(2,1)}, bf16[144,768]{1,0:T(8,128)(2,1)S(1)}, u32[]{:S(2)}, u32[]{:S(2)}) collective-permute-start(bf16[144,768]{1,0:T(8,128)(2,1)} %pack.1), channel_id=1, source_target_pairs={{0,0},{1,8},{2,2},{3,10},{4,4},{5,12},{6,6},{7,14},{8,1},{9,9},{10... | collective-permute-start | bytes 663560 | tf_op jit(solution)/shard_map/ppermute | solution.py:46
  6.6 10.8 %collective-permute-start.1 = (bf16[144,768]{1,0:T(8,128)(2,1)}, bf16[144,768]{1,0:T(8,128)(2,1)S(1)}, u32[]{:S(2)}, u32[]{:S(2)}) collective-permute-start(bf16[144,768]{1,0:T(8,128)(2,1)} %pack.1), channel_id=1, source_target_pairs={{0,2},{1,10},{2,0},{3,8},{4,6},{5,14},{6,4},{7,12},{8,3},{9,11},{1... | collective-permute-start | bytes 663560 | tf_op jit(solution)/shard_map/ppermute | solution.py:46
  16.4 7.3 %collective-permute-start.3 = (bf16[1,144,768]{2,1,0:T(8,128)(2,1)S(1)}, bf16[1,144,768]{2,1,0:T(8,128)(2,1)S(1)}, u32[]{:S(2)}, u32[]{:S(2)}) collective-permute-start(bf16[1,144,768]{2,1,0:T(8,128)(2,1)S(1)} %bitcast.32), channel_id=1, source_target_pairs={{0,2},{1,3},{2,0},{3,1},{4,6},{5,7},{6,4},{7,5},{8,10},{9,11},{10,... | collective-permute-start | bytes 663560 | tf_op jit(solution)/shard_map/ppermute | solution.py:46
  19.6 9.9 %collective-permute-start.4 = (bf16[3,1,128,512]{3,2,1,0:T(8,128)(2,1)S(1)}, bf16[3,1,128,512]{3,2,1,0:T(8,128)(2,1)S(1)}, u32[]{:S(2)}, u32[]{:S(2)}) collective-permute-start(bf16[3,1,128,512]{3,2,1,0:T(8,128)(2,1)S(1)} %get-tuple-element.130.refs_1_), channel_id=1, source_target_pairs={{0,8},{1,9},{2,10},{3,11},{4,12},{5,13},{6,14},{7,15},{8,0},{9,1},... | collective-permute-start | bytes 1179656 | tf_op jit(solution)/shard_map/ppermute | solution.py:46
  25.5 13.9 %collective-permute-start.6 = (bf16[128,768]{1,0:T(8,128)(2,1)S(1)}, bf16[128,768]{1,0:T(8,128)(2,1)S(1)}, u32[]{:S(2)}, u32[]{:S(2)}) collective-permute-start(bf16[128,768]{1,0:T(8,128)(2,1)S(1)} %bitcast.27), channel_id=1, source_target_pairs={{0,2},{1,3},{2,0},{3,1},{4,6},{5,7},{6,4},{7,5},{8,10},{9,11},{10,... | collective-permute-start | bytes 589832 | tf_op jit(solution)/shard_map/ppermute | solution.py:46
  26.8 12.6 %collective-permute-start.7 = (bf16[128,768]{1,0:T(8,128)(2,1)S(1)}, bf16[128,768]{1,0:T(8,128)(2,1)S(1)}, u32[]{:S(2)}, u32[]{:S(2)}) collective-permute-start(bf16[128,768]{1,0:T(8,128)(2,1)S(1)} %bitcast.28), channel_id=1, source_target_pairs={{0,4},{1,5},{2,6},{3,7},{4,0},{5,1},{6,2},{7,3},{8,12},{9,13},{10,... | collective-permute-start | bytes 589832 | tf_op jit(solution)/shard_map/ppermute | solution.py:46
  39.4 8.2 %collective-permute-start.10 = (bf16[128,192]{1,0:T(8,128)(2,1)S(1)}, bf16[128,192]{1,0:T(8,128)(2,1)S(1)}, u32[]{:S(2)}, u32[]{:S(2)}) collective-permute-start(bf16[128,192]{1,0:T(8,128)(2,1)S(1)} %get-tuple-element.141), channel_id=1, source_target_pairs={{0,4},{1,12},{2,6},{3,14},{4,0},{5,8},{6,2},{7,10},{8,5},{9,13},{1... | collective-permute-start | bytes 147464 | tf_op jit(solution)/shard_map/ppermute | solution.py:46
  39.7 8.0 %collective-permute-start.11 = (bf16[128,192]{1,0:T(8,128)(2,1)S(1)}, bf16[128,192]{1,0:T(8,128)(2,1)S(1)}, u32[]{:S(2)}, u32[]{:S(2)}) collective-permute-start(bf16[128,192]{1,0:T(8,128)(2,1)S(1)} %get-tuple-element.142), channel_id=1, source_target_pairs={{0,6},{1,14},{2,4},{3,12},{4,2},{5,10},{6,0},{7,8},{8,7},{9,15},{1... | collective-permute-start | bytes 147464 | tf_op jit(solution)/shard_map/ppermute | solution.py:46
  51.5 15.6 %collective-permute-start.20 = (bf16[128,768]{1,0:T(8,128)(2,1)S(1)}, bf16[128,768]{1,0:T(8,128)(2,1)S(1)}, u32[]{:S(2)}, u32[]{:S(2)}) collective-permute-start(bf16[128,768]{1,0:T(8,128)(2,1)S(1)} %get-tuple-element.181.refs_1_), channel_id=1, source_target_pairs={{0,4},{1,5},{2,6},{3,7},{4,0},{5,1},{6,2},{7,3},{8,12},{9,13},{10,... | collective-permute-start | bytes 589832 | tf_op jit(solution)/shard_map/ppermute | solution.py:46
  52.5 18.7 %collective-permute-start.16 = (bf16[128,768]{1,0:T(8,128)(2,1)S(1)}, bf16[128,768]{1,0:T(8,128)(2,1)S(1)}, u32[]{:S(2)}, u32[]{:S(2)}) collective-permute-start(bf16[128,768]{1,0:T(8,128)(2,1)S(1)} %collective-permute-done.7.refs_11_), channel_id=1, source_target_pairs={{0,2},{1,3},{2,0},{3,1},{4,6},{5,7},{6,4},{7,5},{8,10},{9,11},{10,... | collective-permute-start | bytes 589832 | tf_op jit(solution)/shard_map/ppermute | solution.py:46
  59.4 5.7 %collective-permute-start.13 = (bf16[128,192]{1,0:T(8,128)(2,1)S(1)}, bf16[128,192]{1,0:T(8,128)(2,1)S(1)}, u32[]{:S(2)}, u32[]{:S(2)}) collective-permute-start(bf16[128,192]{1,0:T(8,128)(2,1)S(1)} %get-tuple-element.149), channel_id=1, source_target_pairs={{0,2},{1,10},{2,0},{3,8},{4,6},{5,14},{6,4},{7,12},{8,3},{9,11},{1... | collective-permute-start | bytes 147464 | tf_op jit(solution)/shard_map/ppermute | solution.py:46
  60.8 23.5 %collective-permute-start.23 = (bf16[128,1152]{1,0:T(8,128)(2,1)S(1)}, bf16[128,1152]{1,0:T(8,128)(2,1)S(1)}, u32[]{:S(2)}, u32[]{:S(2)}) collective-permute-start(bf16[128,1152]{1,0:T(8,128)(2,1)S(1)} %get-tuple-element.176), channel_id=1, source_target_pairs={{0,16},{1,17},{2,18},{3,19},{4,20},{5,21},{6,22},{7,23},{8,24},{9,... | collective-permute-start | bytes 884744 | tf_op jit(solution)/shard_map/ppermute | solution.py:46
  61.3 6.0 %collective-permute-start.14 = (bf16[128,192]{1,0:T(8,128)(2,1)S(1)}, bf16[128,192]{1,0:T(8,128)(2,1)S(1)}, u32[]{:S(2)}, u32[]{:S(2)}) collective-permute-start(bf16[128,192]{1,0:T(8,128)(2,1)S(1)} %get-tuple-element.150), channel_id=1, source_target_pairs={{0,4},{1,12},{2,6},{3,14},{4,0},{5,8},{6,2},{7,10},{8,5},{9,13},{1... | collective-permute-start | bytes 147464 | tf_op jit(solution)/shard_map/ppermute | solution.py:46
  65.1 6.1 %collective-permute-start.15 = (bf16[128,192]{1,0:T(8,128)(2,1)S(1)}, bf16[128,192]{1,0:T(8,128)(2,1)S(1)}, u32[]{:S(2)}, u32[]{:S(2)}) collective-permute-start(bf16[128,192]{1,0:T(8,128)(2,1)S(1)} %get-tuple-element.151), channel_id=1, source_target_pairs={{0,6},{1,14},{2,4},{3,12},{4,2},{5,10},{6,0},{7,8},{8,7},{9,15},{1... | collective-permute-start | bytes 147464 | tf_op jit(solution)/shard_map/ppermute | solution.py:46
  67.1 17.3 %collective-permute-start.21 = (bf16[128,768]{1,0:T(8,128)(2,1)S(1)}, bf16[128,768]{1,0:T(8,128)(2,1)S(1)}, u32[]{:S(2)}, u32[]{:S(2)}) collective-permute-start(bf16[128,768]{1,0:T(8,128)(2,1)S(1)} %get-tuple-element.181.refs_1_), channel_id=1, source_target_pairs={{0,2},{1,3},{2,0},{3,1},{4,6},{5,7},{6,4},{7,5},{8,10},{9,11},{10,... | collective-permute-start | bytes 589832 | tf_op jit(solution)/shard_map/ppermute | solution.py:46
  67.3 17.0 %collective-permute-start.22 = (bf16[128,768]{1,0:T(8,128)(2,1)S(1)}, bf16[128,768]{1,0:T(8,128)(2,1)S(1)}, u32[]{:S(2)}, u32[]{:S(2)}) collective-permute-start(bf16[128,768]{1,0:T(8,128)(2,1)S(1)} %collective-permute-done.20.refs_3_), channel_id=1, source_target_pairs={{0,2},{1,3},{2,0},{3,1},{4,6},{5,7},{6,4},{7,5},{8,10},{9,11},{10,... | collective-permute-start | bytes 589832 | tf_op jit(solution)/shard_map/ppermute | solution.py:46
  79.3 7.6 %collective-permute-start.17 = (bf16[1,4,128,384]{3,2,1,0:T(8,128)(2,1)S(1)}, bf16[1,4,128,384]{3,2,1,0:T(8,128)(2,1)S(1)}, u32[]{:S(2)}, u32[]{:S(2)}) collective-permute-start(bf16[1,4,128,384]{3,2,1,0:T(8,128)(2,1)S(1)} %get-tuple-element.167), channel_id=1, source_target_pairs={{0,8},{1,9},{2,10},{3,11},{4,12},{5,13},{6,14},{7,15},{8,0},{9,1},... | collective-permute-start | bytes 1179656 | tf_op jit(solution)/shard_map/ppermute | solution.py:46
  92.0 16.2 %collective-permute-start.35 = (bf16[2,64,2304]{2,1,0:T(8,128)(2,1)S(1)}, bf16[2,64,2304]{2,1,0:T(8,128)(2,1)S(1)}, u32[]{:S(2)}, u32[]{:S(2)}) collective-permute-start(bf16[2,64,2304]{2,1,0:T(8,128)(2,1)S(1)} %get-tuple-element.193), channel_id=1, source_target_pairs={{0,16},{1,17},{2,18},{3,19},{4,20},{5,21},{6,22},{7,23},{8,24},{9,... | collective-permute-start | bytes 1769480 | tf_op jit(solution)/shard_map/ppermute | solution.py:46
  100.2 13.5 %collective-permute-start.36 = (bf16[224,576]{1,0:T(8,128)(2,1)S(1)}, bf16[224,576]{1,0:T(8,128)(2,1)S(1)}, u32[]{:S(2)}, u32[]{:S(2)}) collective-permute-start(bf16[224,576]{1,0:T(8,128)(2,1)S(1)} %get-tuple-element.212), channel_id=1, source_target_pairs={{0,16},{1,17},{2,18},{3,19},{4,20},{5,21},{6,22},{7,23},{8,24},{9,... | collective-permute-start | bytes 774152 | tf_op jit(solution)/shard_map/ppermute | solution.py:46
  101.5 16.9 %collective-permute-start.19 = (bf16[2,128,576]{2,1,0:T(8,128)(2,1)S(1)}, bf16[2,128,576]{2,1,0:T(8,128)(2,1)S(1)}, u32[]{:S(2)}, u32[]{:S(2)}) collective-permute-start(bf16[2,128,576]{2,1,0:T(8,128)(2,1)S(1)} %get-tuple-element.169.refs_2_), channel_id=1, source_target_pairs={{0,4},{1,12},{2,6},{3,14},{4,0},{5,8},{6,2},{7,10},{8,5},{9,13},{1... | collective-permute-start | bytes 884744 | tf_op jit(solution)/shard_map/ppermute | solution.py:46
  101.5 16.9 %collective-permute-start.18 = (bf16[2,128,576]{2,1,0:T(8,128)(2,1)S(1)}, bf16[2,128,576]{2,1,0:T(8,128)(2,1)S(1)}, u32[]{:S(2)}, u32[]{:S(2)}) collective-permute-start(bf16[2,128,576]{2,1,0:T(8,128)(2,1)S(1)} %get-tuple-element.168.refs_1_), channel_id=1, source_target_pairs={{0,0},{1,8},{2,2},{3,10},{4,4},{5,12},{6,6},{7,14},{8,1},{9,9},{10... | collective-permute-start | bytes 884744 | tf_op jit(solution)/shard_map/ppermute | solution.py:46
  108.9 13.1 %collective-permute-start.38 = (bf16[1,64,2304]{2,1,0:T(8,128)(2,1)S(1)}, bf16[1,64,2304]{2,1,0:T(8,128)(2,1)S(1)}, u32[]{:S(2)}, u32[]{:S(2)}) collective-permute-start(bf16[1,64,2304]{2,1,0:T(8,128)(2,1)S(1)} %get-tuple-element.222), channel_id=1, source_target_pairs={{0,1},{1,0},{2,3},{3,2},{4,5},{5,4},{6,7},{7,6},{8,9},{9,8},{10,11... | collective-permute-start | bytes 884744 | tf_op jit(solution)/shard_map/ppermute | solution.py:46
  114.4 14.7 %collective-permute-start.39 = (bf16[128,576]{1,0:T(8,128)(2,1)S(1)}, bf16[128,576]{1,0:T(8,128)(2,1)S(1)}, u32[]{:S(2)}, u32[]{:S(2)}) collective-permute-start(bf16[128,576]{1,0:T(8,128)(2,1)S(1)} %get-tuple-element.218), channel_id=1, source_target_pairs={{0,1},{1,0},{2,3},{3,2},{4,5},{5,4},{6,7},{7,6},{8,9},{9,8},{10,11... | collective-permute-start | bytes 442376 | tf_op jit(solution)/shard_map/ppermute | solution.py:46
  118.4 20.9 %collective-permute-start.37 = (bf16[2,128,576]{2,1,0:T(8,128)(2,1)S(1)}, bf16[2,128,576]{2,1,0:T(8,128)(2,1)S(1)}, u32[]{:S(2)}, u32[]{:S(2)}) collective-permute-start(bf16[2,128,576]{2,1,0:T(8,128)(2,1)S(1)} %forwarded.1), channel_id=1, source_target_pairs={{0,2},{1,3},{2,0},{3,1},{4,6},{5,7},{6,4},{7,5},{8,10},{9,11},{10,... | collective-permute-start | bytes 884744 | tf_op jit(solution)/shard_map/ppermute | solution.py:46
  118.5 14.3 %collective-permute-start.40 = (bf16[384,192]{1,0:T(8,128)(2,1)S(1)}, bf16[384,192]{1,0:T(8,128)(2,1)S(1)}, u32[]{:S(2)}, u32[]{:S(2)}) collective-permute-start(bf16[384,192]{1,0:T(8,128)(2,1)S(1)} %get-tuple-element.231), channel_id=1, source_target_pairs={{0,1},{1,0},{2,3},{3,2},{4,5},{5,4},{6,7},{7,6},{8,9},{9,8},{10,11... | collective-permute-start | bytes 442376 | tf_op jit(solution)/shard_map/ppermute | solution.py:46
  122.6 12.7 %collective-permute-start.44 = (bf16[256,192]{1,0:T(8,128)(2,1)S(1)}, bf16[256,192]{1,0:T(8,128)(2,1)S(1)}, u32[]{:S(2)}, u32[]{:S(2)}) collective-permute-start(bf16[256,192]{1,0:T(8,128)(2,1)S(1)} %get-tuple-element.227), channel_id=1, source_target_pairs={{0,0},{1,8},{2,4},{3,12},{4,1},{5,9},{6,5},{7,13},{8,2},{9,10},{10... | collective-permute-start | bytes 294920 | tf_op jit(solution)/shard_map/ppermute | solution.py:46
  123.3 14.6 %collective-permute-start.42 = (bf16[96,512]{1,0:T(8,128)(2,1)S(1)}, bf16[96,512]{1,0:T(8,128)(2,1)S(1)}, u32[]{:S(2)}, u32[]{:S(2)}) collective-permute-start(bf16[96,512]{1,0:T(8,128)(2,1)S(1)} %get-tuple-element.225), channel_id=1, source_target_pairs={{0,0},{1,1},{2,16},{3,17},{4,4},{5,5},{6,20},{7,21},{8,8},{9,9},{1... | collective-permute-start | bytes 294920 | tf_op jit(solution)/shard_map/ppermute | solution.py:46
  129.1 8.8 %collective-permute-start.43 = (bf16[96,512]{1,0:T(8,128)(2,1)S(1)}, bf16[96,512]{1,0:T(8,128)(2,1)S(1)}, u32[]{:S(2)}, u32[]{:S(2)}) collective-permute-start(bf16[96,512]{1,0:T(8,128)(2,1)S(1)} %get-tuple-element.226), channel_id=1, source_target_pairs={{0,4},{1,5},{2,20},{3,21},{4,0},{5,1},{6,16},{7,17},{8,12},{9,13},... | collective-permute-start | bytes 294920 | tf_op jit(solution)/shard_map/ppermute | solution.py:46
  133.4 10.6 %collective-permute-start.46 = (bf16[96,576]{1,0:T(8,128)(2,1)S(1)}, bf16[96,576]{1,0:T(8,128)(2,1)S(1)}, u32[]{:S(2)}, u32[]{:S(2)}) collective-permute-start(bf16[96,576]{1,0:T(8,128)(2,1)S(1)} %bitcast.36), channel_id=1, source_target_pairs={{0,0},{1,1},{2,8},{3,9},{4,16},{5,17},{6,24},{7,25},{8,2},{9,3},{1... | collective-permute-start | bytes 331784 | tf_op jit(solution)/shard_map/ppermute | solution.py:46
  135.4 8.0 %collective-permute-start.41 = (bf16[256,192]{1,0:T(8,128)(2,1)S(1)}, bf16[256,192]{1,0:T(8,128)(2,1)S(1)}, u32[]{:S(2)}, u32[]{:S(2)}) collective-permute-start(bf16[256,192]{1,0:T(8,128)(2,1)S(1)} %get-tuple-element.232), channel_id=1, source_target_pairs={{0,2},{1,3},{2,0},{3,1},{4,6},{5,7},{6,4},{7,5},{8,10},{9,11},{10,... | collective-permute-start | bytes 294920 | tf_op jit(solution)/shard_map/ppermute | solution.py:46
  143.9 7.2 %collective-permute-start.45 = (bf16[160,192]{1,0:T(8,128)(2,1)S(1)}, bf16[160,192]{1,0:T(8,128)(2,1)S(1)}, u32[]{:S(2)}, u32[]{:S(2)}) collective-permute-start(bf16[160,192]{1,0:T(8,128)(2,1)S(1)} %get-tuple-element.239), channel_id=1, source_target_pairs={{0,4},{1,5},{2,6},{3,7},{4,0},{5,1},{6,2},{7,3},{8,12},{9,13},{10,... | collective-permute-start | bytes 184328 | tf_op jit(solution)/shard_map/ppermute | solution.py:46
  (27 other events, 188.5 us)

commit v3 on v2

--- a/solution.py
+++ b/solution.py
@@ -268,7 +268,7 @@
 def forward_body(smem, get, outs, segk, strip, s_scr, p_scr, sems, *, blocks, chunk):
     (place,) = smem
     ctx = outs[0:4]
-    q_ref, k_ref, v_ref, o_ref, p_hbm = outs[4:9]
+    q_ref, k_ref, v_ref, o_ref, p_ref = outs[4:9]
     group, core, s_own = place[0], place[1], place[2]
     tok = 128
     head_size = 64
@@ -301,7 +301,7 @@
 
     def p_copy(slot, h, d):
         return pltpu.make_async_copy(
-            p_scr.at[slot], p_hbm.at[h, :, pl.ds(d * tok, tok), :], sems.at[slot]
+            p_scr.at[slot], p_ref.at[h, :, pl.ds(d * tok, tok), :], sems.at[slot]
         )
 
     heads = local // head_size
@@ -320,6 +320,8 @@
         strip[:, tok * (blocks + 1) :] = jnp.broadcast_to(
             bias_row[:, span - 1 :], (tok, tok * (blocks - 2))
         )
+        if chunks == 1:
+            s_scr[...] = dot(q_ref[:, cols], k_ref[:, cols], 1, 1)
         for d in range(4):
             query_block = block_of(d, 0, 0)
             strip_base = tok * (blocks - 1) - query_block * tok
@@ -330,19 +332,23 @@
                 pending.pop(slot).wait()
             queries = q_ref[d * tok : (d + 1) * tok, cols]
             if chunks == 1:
-                s_scr[slot] = dot(queries, k_ref[:, cols], 1, 1)
                 for r in range(0, tok, rows_at_once):
                     rows = slice(r, r + rows_at_once)
                     bias = strip[rows, pl.ds(pl.multiple_of(strip_base, tok), seq)]
-                    scores = s_scr[slot, rows, :] + bias
+                    scores = s_scr[d * tok + r : d * tok + r + rows_at_once, :] + bias
                     scores = jnp.where(seg_col[rows] == segk[0:1, :], scores, masked_score)
                     top = jnp.max(scores, axis=1, keepdims=True)
                     exps = jnp.exp(scores - top)
                     total = jnp.sum(exps, axis=1, keepdims=True)
-                    p_scr[slot, 0, rows, :] = (exps * (1.0 / total)).astype(bf16)
-                weighted = jnp.dot(
-                    p_scr[slot, 0], v_ref[:, cols], preferred_element_type=f32
-                )
+                    at = d * tok + r
+                    p_ref[h, 0, at : at + rows_at_once, :] = (exps * (1.0 / total)).astype(bf16)
+                if d < 3:
+                    continue
+                all_weighted = dot(p_ref[h, 0], v_ref[:, cols], 1, 0)
+                o_ref[:, cols] = all_weighted
+                for k in range(4):
+                    ctx[k][:, cols] = all_weighted[k * tok : (k + 1) * tok].astype(bf16)
+                continue
             else:
                 def score_chunk(i, top):
                     start = pl.multiple_of(i * chunk, chunk)
@@ -378,9 +384,10 @@
                 weighted = lax.fori_loop(
                     0, chunks, weigh_chunk, jnp.zeros((tok, head_size), f32)
                 )
-            copy = p_copy(slot, h, d)
-            copy.start()
-            pending[slot] = copy
+            if chunks > 1:
+                copy = p_copy(slot, h, d)
+                copy.start()
+                pending[slot] = copy
             o_ref[d * tok : (d + 1) * tok, cols] = weighted
             ctx[d][:, cols] = weighted.astype(bf16)
     for copy in pending.values():
@@ -409,21 +416,21 @@
         scratch=[
             pltpu.VMEM((8, seq), f32),
             pltpu.VMEM((tok, (2 * blocks - 1) * tok), f32),
-            pltpu.VMEM((2 if seq == chunk else 1, tok, seq), f32),
-            pltpu.VMEM((2, seq // chunk, tok, chunk), bf16),
+            pltpu.VMEM((4 * tok, seq) if seq == chunk else (1, tok, seq), f32),
+            pltpu.VMEM((2, seq // chunk, tok, chunk) if s_count > 1 else (2, 1, 16, 128), bf16),
             pltpu.SemaphoreType.DMA((2,)),
         ],
-        in_hbm=(("out", 8),),
-        mebibytes=8 if s_count == 1 else 60,
+        in_hbm=(("out", 8),) if s_count > 1 else (),
+        mebibytes=9 if s_count == 1 else 60,
         us=10,
     )
 
 
 def backward_body(
-    smem, get, outs, p_scr, ds_scr, dctx_scr, strip, dq_scr, kv_scr, rows_scr, sems, *, blocks, chunk
+    smem, get, outs, p_scr, ds_scr, dctx_scr, strip, dq_scr, kv_scr, rows_scr, dp_scr, sems, *, blocks, chunk
 ):
     (place,) = smem
-    p_hbm = get(8)
+    p_ref = get(8)
     dq = outs[0:4]
     keep_ref, send_ref, table_ref = outs[4:7]
     group, core, s_own = place[0], place[1], place[2]
@@ -434,9 +441,10 @@
     s_count = blocks // 8
 
     def p_copy(h, i, slot):
-        return pltpu.make_async_copy(p_hbm.at[h, i], p_scr.at[slot], sems.at[slot])
-
-    p_copy(0, 0, 0).start()
+        return pltpu.make_async_copy(p_ref.at[h, i], p_scr.at[slot], sems.at[slot])
+
+    if chunks > 1:
+        p_copy(0, 0, 0).start()
     for d in range(4):
         dctx_scr[d * tok : (d + 1) * tok, :] = get(d)[...]
     q_ref, k_ref, v_ref, o_ref = get(4), get(5), get(6), get(7)
@@ -452,23 +460,27 @@
         def run_chunk(i, h=h, cols=cols, out_grad=out_grad, delta=delta):
             start = pl.multiple_of(i * chunk, chunk)
             slot = (h * chunks + i) % 2
-            following = h * chunks + i + 1
-
-            @pl.when(following < heads * chunks)
-            def _():
-                p_copy(following // chunks, following % chunks, 1 - slot).start()
-
-            p_copy(h, i, slot).wait()
+            if chunks > 1:
+                following = h * chunks + i + 1
+
+                @pl.when(following < heads * chunks)
+                def _():
+                    p_copy(following // chunks, following % chunks, 1 - slot).start()
+
+                p_copy(h, i, slot).wait()
+                probs = p_scr.at[slot]
+            else:
+                probs = p_ref.at[h, 0]
             keys = k_ref[pl.ds(start, chunk), cols]
             values = v_ref[pl.ds(start, chunk), cols]
+            dp_scr[...] = dot(out_grad, values, 1, 1)
             for d in range(4):
                 query_block = ((group ^ d) * s_count + s_own) * 2 + core
                 base = pl.multiple_of(tok * (blocks - 1) - query_block * tok + start, tok)
-                prob_grad = dot(out_grad[d * tok : (d + 1) * tok], values, 1, 1)
                 for r in range(0, tok, rows_at_once):
                     rows = slice(d * tok + r, d * tok + r + rows_at_once)
-                    here = prob_grad[r : r + rows_at_once] - delta[rows]
-                    low = (p_scr[slot, rows, :].astype(f32) * here).astype(bf16)
+                    here = dp_scr[rows, :] - delta[rows]
+                    low = (probs[rows, :].astype(f32) * here).astype(bf16)
                     ds_scr[rows, :] = low
                     strip[r : r + rows_at_once, pl.ds(base, chunk)] += low.astype(f32)
             scores_grad = ds_scr[...]
@@ -478,8 +490,8 @@
             else:
                 dq_scr[:, cols] += part
             queries = q_ref[:, cols]
-            kv_scr[0, pl.ds(start, chunk), :] = dot(scores_grad, queries, 0, 0).astype(bf16)
-            kv_scr[1, pl.ds(start, chunk), :] = dot(p_scr[slot], out_grad, 0, 0).astype(bf16)
+            kv_scr[0, pl.ds(start, chunk), :] = jnp.transpose(dot(jnp.transpose(queries), scores_grad, 1, 0).astype(bf16))
+            kv_scr[1, pl.ds(start, chunk), :] = jnp.transpose(dot(jnp.transpose(out_grad), probs[...], 1, 0).astype(bf16))
 
         if chunks == 1:
             run_chunk(0)
@@ -550,18 +562,19 @@
         [*dctx, q, k, v, o, p],
         shapes,
         scratch=[
-            pltpu.VMEM((2, 4 * tok, chunk), bf16),
+            pltpu.VMEM((2, 4 * tok, chunk) if s_count > 1 else (2, 16, 128), bf16),
             pltpu.VMEM((4 * tok, chunk), bf16),
             pltpu.VMEM((4 * tok, local), bf16),
             pltpu.VMEM((tok, (2 * blocks - 1) * tok), f32),
             pltpu.VMEM((4 * tok, local), f32),
             pltpu.VMEM((2, seq, 64), bf16),
             pltpu.VMEM((8, 4 * tok), f32),
+            pltpu.VMEM((4 * tok, chunk), f32),
             pltpu.SemaphoreType.DMA((2,)),
         ],
-        in_hbm=(8,),
+        in_hbm=(8,) if s_count > 1 else (),
         staged=tuple(("out", i) for i in range(6)) if s_count == 1 else (),
-        mebibytes=13 if s_count == 1 else 60,
+        mebibytes=15 if s_count == 1 else 60,
         us=0.01,
     )
 
@@ -764,10 +777,10 @@
     )
 
 
-def out_grad_body(smem, get, outs, ctx_scr, attn_scr, out_scr):
+def out_grad_body(smem, get, outs, ctx_scr, attn_scr, out_scr, *, order):
     (place,) = smem
     kept_ref, sent_ref = outs
-    group, core, odd = place[0], place[1], place[3] == 1
+    group, core, odd = place[0], place[1], ((place[5] >> order[0]) & 1) == 1
     tok = ctx_scr.shape[0] // 4
     width = ctx_scr.shape[1]
     local = width // groups
@@ -782,23 +795,26 @@
         out_scr[pl.ds(start, local), :] = turned[d * local : (d + 1) * local]
     pieces, block, unused = kept_ref.shape
     for i in range(pieces):
-        even = out_scr[2 * i * block : (2 * i + 1) * block, :]
-        other = out_scr[(2 * i + 1) * block : (2 * i + 2) * block, :]
+        first, second = (
+            sum(((n >> k) & 1) << bit for k, bit in enumerate(order)) for n in (2 * i, 2 * i + 1)
+        )
+        even = out_scr[first * block : (first + 1) * block, :]
+        other = out_scr[second * block : (second + 1) * block, :]
         kept_ref[i] = jnp.where(odd, other, even)
-        sent_ref[i * block : (i + 1) * block, :] = jnp.where(odd, even, other).astype(bf16)
-
-
-def out_weight_grad(place, parts, wide):
+        sent_ref[i] = jnp.where(odd, even, other).astype(bf16)
+
+
+def out_weight_grad(place, parts, wide, order):
     tok, span = parts[0].shape
     width = span * 2 // 3
     local = width // groups
     shape = (wide // 2, width // wide, local)
     return kernel_call(
-        out_grad_body,
+        functools.partial(out_grad_body, order=order),
         "out_grad",
         [place],
         parts,
-        [shaped(f32, *shape), shaped(bf16, width // 2, local)],
+        [shaped(f32, *shape), shaped(bf16, *shape)],
         scratch=[
             pltpu.VMEM((4 * tok, width), bf16),
             pltpu.VMEM((4 * tok, local), bf16),
@@ -809,50 +825,34 @@
     )
 
 
-def out_sum_body(smem, get, outs, *, bit, riding):
+def out_sum_body(smem, get, outs, *, following):
     (place,) = smem
     kept, received = get(0), get(1)
-    remaining, block, unused = kept.shape
-    totals = [
-        kept[i] + received[i * block : (i + 1) * block, :].astype(f32) for i in range(remaining)
-    ]
-    if riding:
-        small = get(2)[...]
-        if "in" in riding:
-            small = attached(received, remaining * block, small)
-            outs[-1][...] = small
+    remaining = kept.shape[0]
     if remaining == 1:
-        outs[0][...] = totals[0]
+        outs[0][...] = kept[0] + received[0].astype(f32)
         return
-    odd = ((place[5] >> bit) & 1) == 1
+    odd = ((place[5] >> following) & 1) == 1
     for i in range(remaining // 2):
-        outs[0][i] = jnp.where(odd, totals[2 * i + 1], totals[2 * i])
-        theirs = jnp.where(odd, totals[2 * i], totals[2 * i + 1])
-        outs[1][i * block : (i + 1) * block, :] = theirs.astype(bf16)
-    if riding:
-        filled = remaining // 2 * block
-        rest = outs[1].shape[0] - filled
-        outs[1][filled:, :] = jnp.zeros((rest, outs[1].shape[1]), bf16)
-        attach_rows(outs[1], filled, small)
-
-
-def out_sum(layout, place, kept, sent, bit, small=None, riding=()):
+        even = kept[2 * i] + received[2 * i].astype(f32)
+        other = kept[2 * i + 1] + received[2 * i + 1].astype(f32)
+        outs[0][i] = jnp.where(odd, other, even)
+        outs[1][i] = jnp.where(odd, even, other).astype(bf16)
+
+
+def out_sum(layout, place, kept, sent, order, step):
     remaining, block, local = kept.shape
-    extra = 2 * room(small.shape[0]) if riding else 0
     if remaining == 1:
         outputs = [shaped(f32, block, local)]
     else:
-        outputs = [
-            shaped(f32, remaining // 2, block, local),
-            shaped(bf16, remaining // 2 * block + extra, local),
-        ]
-    if "in" in riding:
-        outputs.append(shaped(f32, *small.shape))
-    return kernel_call(
-        functools.partial(out_sum_body, bit=bit + 1, riding=riding),
+        shape = (remaining // 2, block, local)
+        outputs = [shaped(f32, *shape), shaped(bf16, *shape)]
+    following = order[step + 1] if step + 1 < len(order) else 0
+    return kernel_call(
+        functools.partial(out_sum_body, following=following),
         "out_sum",
         [place],
-        [kept, layout.wide_bit(sent, bit)] + ([small] if riding else []),
+        [kept, layout.wide_bit(sent, order[step])],
         outputs,
         us=0.01,
     )
@@ -1079,7 +1079,7 @@
     )
 
 
-def qkv_sum_body(smem, get, outs, *, axis):
+def qkv_sum_body(smem, get, outs, *, axis, s_count):
     (place,) = smem
     kept, small, received = get(0), get(1), get(2)
     parts, rows, span = kept.shape
@@ -1087,44 +1087,46 @@
         kept[i] + received[i * rows : (i + 1) * rows, :].astype(f32) for i in range(parts)
     ]
     summed = attached(received, parts * rows, small[...])
-    if axis == "y":
-        outs[-1][...] = summed
+    outs[-1][...] = summed
+    if axis == "x":
         for i in range(parts):
             outs[0][i] = totals[i].astype(outs[0].dtype)
         return
-    kept_ref, sent_ref, small_ref = outs
-    small_ref[...] = summed
+    kept_ref, sent_ref = outs[:2]
+    blocks, block = kept_ref.shape[0], kept_ref.shape[1]
     if axis == "core":
-        far = place[4] == 1
-        mine, theirs = jnp.where(far, totals[1], totals[0]), jnp.where(far, totals[0], totals[1])
-        blocks, block = kept_ref.shape[0], kept_ref.shape[1]
+        other = place[3] == 1
+        pairs = []
         for i in range(blocks):
-            kept_ref[i] = mine[i * block : (i + 1) * block]
-        sent_ref[:rows, :] = theirs.astype(bf16)
+            source, at = totals[i // s_count], 2 * (i % s_count) * block
+            pairs.append((source[at : at + block], source[at + block : at + 2 * block]))
     else:
-        odd = place[3] == 1
-        for i in range(parts // 2):
-            kept_ref[i] = jnp.where(odd, totals[2 * i + 1], totals[2 * i])
-            theirs = jnp.where(odd, totals[2 * i], totals[2 * i + 1])
-            sent_ref[i * rows : (i + 1) * rows, :] = theirs.astype(bf16)
-    filled = sent_ref.shape[0] - room(small.shape[0])
-    sent_ref[filled:, :] = jnp.zeros((room(small.shape[0]), span), bf16)
+        other = place[4] == 1
+        pairs = [(totals[i], totals[blocks + i]) for i in range(blocks)]
+    for i, (first, second) in enumerate(pairs):
+        kept_ref[i] = jnp.where(other, second, first)
+        theirs = jnp.where(other, first, second)
+        sent_ref[i * block : (i + 1) * block, :] = theirs.astype(bf16)
+    filled = blocks * block
+    sent_ref[filled:, :] = jnp.zeros((sent_ref.shape[0] - filled, span), bf16)
     attach(sent_ref, filled, summed)
 
 
-def qkv_sum(place, kept, small, received, axis, s_count, wide):
+def qkv_sum(place, kept, small, received, axis, s_count):
     parts, rows, span = kept.shape
     count = small.shape[0]
-    if axis == "core":
-        shape, sent = (2 * s_count, rows // (2 * s_count), span), rows
-    else:
-        shape, sent = (parts // 2, rows, span), parts // 2 * rows
-    if axis == "y":
+    if axis == "x":
         outputs = [shaped(bf16 if s_count == 1 else f32, *kept.shape)]
     else:
-        outputs = [shaped(f32, *shape), shaped(bf16, sent + room(count), span)]
-    return kernel_call(
-        functools.partial(qkv_sum_body, axis=axis),
+        shape = (parts * s_count, rows // (2 * s_count), span)
+        if axis == "y":
+            shape = (parts // 2, rows, span)
+        outputs = [
+            shaped(f32, *shape),
+            shaped(bf16, shape[0] * shape[1] + room(count), span),
+        ]
+    return kernel_call(
+        functools.partial(qkv_sum_body, axis=axis, s_count=s_count),
         f"qkv_sum_{axis}",
         [place],
         [kept, small, received],
@@ -1323,37 +1325,23 @@
         w_key,
         w_value,
     )
-    out = out_weight_grad(place, after(out_parts, qkv_sent), layout.wide)
+    order = (bits - 2, bits - 1, *range(bits - 2))
+    out = out_weight_grad(place, after(out_parts, qkv_sent), layout.wide, order)
 
     returned = [layout.turned(low_grads[0], 0), layout.turned(low_grads[1], 2)]
     qkv_kept = after(qkv_kept, out)
-    step = qkv_sum(place, qkv_kept, small, layout.core(qkv_sent), "core", s_count, layout.wide)
-    ffn_kept, ffn_sent = ffn_sum(place, after(ffn_kept, step), layout.across(ffn_sent))
-    out_kept, out_sent = after(out, ffn_sent)
+    step = qkv_sum(place, qkv_kept, small, layout.core(qkv_sent), "core", s_count)
+    out = out_sum(layout, place, after(out[0], step), out[1], order, 0)
+    ffn_kept, ffn_sent = ffn_sum(place, after(ffn_kept, out), layout.across(ffn_sent))
     step = qkv_sum(
-        place, after(step[0], ffn_kept), step[2], layout.across(step[1]), "x", s_count, layout.wide
-    )
-    received = layout.wide_bit(ffn_sent, 0)
-    size = s_count
-    bit = 1
-    while size > 1:
-        size //= 2
-        total = (ffn_kept + received.astype(f32)).reshape(size, 2, *ffn_kept.shape[1:])
-        ffn_kept, ffn_sent = halved(total, 1, (s_own >> (bit - 1)) & 1)
-        received = layout.wide_bit(ffn_sent.astype(bf16), bit)
-        bit += 1
+        place, after(step[0], ffn_kept), step[2], layout.wide_bit(step[1], 0), "y", s_count
+    )
     onward = forwarded(returned[0], after(returned[1], step))
     returned.append(layout.wide_bit(onward, bits - 2))
-    ffn_parts = ffn_last(place, after(ffn_kept, onward), received, local)
     part, small = qkv_sum(
-        place,
-        after(step[0], ffn_parts),
-        step[2],
-        layout.wide_bit(step[1], 0),
-        "y",
-        s_count,
-        layout.wide,
-    )
+        place, after(step[0], onward), step[2], layout.across(step[1]), "x", s_count
+    )
+    out = out_sum(layout, place, after(out[0], part), out[1], order, 1)
     rows = width // layout.wide
     size = s_count
     bit = 1
@@ -1365,20 +1353,18 @@
         small = small + layout.wide_bit(small, bit)
         bit += 1
     part = part.reshape(rows, 3 * local).astype(bf16)
-
-    for bit in range(bits - 1):
-        riding = ("in",) * (bit > bits - 3) + ("out",) * (bit > bits - 4)
-        first = small if riding else part
-        if bit == bits - 2:
-            middle_grad = after(middle_grad, out_sent)
-            input_grad = final_input_grad(
-                place, returned, tokens, gain_attn, middle_grad, w_query, w_key, w_value
-            )
-            first = input_grad
-        outs = out_sum(layout, place, after(out_kept, first), out_sent, bit, small, riding)
-        out_kept, out_sent = outs[:2]
-        if "in" in riding:
-            small = outs[2]
+    received = layout.wide_bit(ffn_sent, 0)
+    size = s_count
+    bit = 1
+    while size > 1:
+        size //= 2
+        total = (ffn_kept + received.astype(f32)).reshape(size, 2, *ffn_kept.shape[1:])
+        ffn_kept, ffn_sent = halved(total, 1, (s_own >> (bit - 1)) & 1)
+        received = layout.wide_bit(ffn_sent.astype(bf16), bit)
+        bit += 1
+    ffn_parts = ffn_last(place, after(ffn_kept, out), received, local)
+    small = small + layout.wide_bit(small, bits - 2)
+    small = small + layout.wide_bit(small, bits - 1)
 
     def half_owner(flip):
         return lambda x, c, g, s, y: (g % 2, c, x + 2 * (g // 2 ^ flip), s, y)
@@ -1399,11 +1385,14 @@
         part[:, local : 2 * local],
         part[:, 2 * local :],
     )
-
-    out_kept = after(out_kept, final_gate)
-    final_out, small = out_sum(
-        layout, place, out_kept, out_sent, bits - 1, small, ("in",)
-    )
+    middle_grad = after(middle_grad, ffn_parts)
+    input_grad = final_input_grad(
+        place, returned, tokens, gain_attn, middle_grad, w_query, w_key, w_value
+    )
+    for step in range(2, bits):
+        out = out_sum(layout, place, after(out[0], input_grad), out[1], order, step)
+    (final_out,) = out
+
     gain_rows = width // 128
     sum_gain_attn = small[:gain_rows].reshape(width)
     sum_gain_ffn = small[gain_rows : 2 * gain_rows].reshape(width)

time: 155 us -> 152 us (0.981)
  Pallas kernels: 52.6 us -> 46.6 us
  starting transfers between devices: 51.7 us -> 57.1 us
  waiting for transfers between devices: 45.9 us -> 44.3 us
    pallas_call x23, Pallas kernels: 52.6 us -> 46.6 us  [kernel_call(): pl.pallas_call(kernel, out_shape=outputs, in_specs=[pl.BlockSpec(memory_s...]
    ppermute x47 -> x49, starting transfers between devices: 51.7 us -> 57.1 us  [send(): return lax.ppermute(block, axes, route)]
    ppermute x47 -> x49, waiting for transfers between devices: 45.9 us -> 44.3 us  [send(): return lax.ppermute(block, axes, route)]
  transfers between devices with their start and end apart: 47 -> 49, of which waited for: 16 -> 19; matrix products, arithmetic and copies ran while one was open for 1% -> 1% of each run, Pallas kernels for 28% -> 23%
where the time goes in v3:
time: 152 us; the launch traced here: 151 us
  starting transfers between devices  57.1 us (38%)
  Pallas kernels  46.6 us (31%)
  waiting for transfers between devices  44.3 us (29%)
  local copies, waits for them, and re-layouts  2.19 us (1%)
    ppermute x49, starting transfers between devices, send(): return lax.ppermute(block, axes, route)  57.1 us
    pallas_call x23, Pallas kernels, kernel_call(): pl.pallas_call(kernel, out_shape=outputs, in_specs=[pl.BlockSpec(memory_s...  46.6 us
    ppermute x49, waiting for transfers between devices, send(): return lax.ppermute(block, axes, route)  44.3 us
  transfers between devices with their start and end apart: 49, of which 19 were waited for; matrix products, arithmetic and copies ran while one was open for 1% of the time, Pallas kernels for 23%

profile of v3, /device:TPU:2, one launch (start us, length us, event | category | flops | bytes accessed | tf_op | source)
XLA Modules:
  0.0 151.3 jit_solution(15913284648522355246)
XLA Ops:
  2.3 2.7 %collective-permute-start.2 = (bf16[144,768]{1,0:T(8,128)(2,1)}, bf16[144,768]{1,0:T(8,128)(2,1)S(1)}, u32[]{:S(2)}, u32[]{:S(2)}) collective-permute-start(bf16[144,768]{1,0:T(8,128)(2,1)} %pack.1), channel_id=1, source_target_pairs={{0,4},{1,12},{2,6},{3,14},{4,0},{5,8},{6,2},{7,10},{8,5},{9,13},{1... | collective-permute-start | bytes 663560 | tf_op jit(solution)/shard_map/ppermute | solution.py:46
  9.2 7.1 %collective-permute-done.2 = bf16[144,768]{1,0:T(8,128)(2,1)S(1)} collective-permute-done((bf16[144,768]{1,0:T(8,128)(2,1)}, bf16[144,768]{1,0:T(8,128)(2,1)S(1)}, u32[]{:S(2)}, u32[]{:S(2)}) %collective-permute-start.2) | collective-permute-done | bytes 221216 | tf_op jit(solution)/shard_map/ppermute | solution.py:46
  17.4 2.2 %project.2 = (bf16[3,1,128,512]{3,2,1,0:T(8,128)(2,1)S(1)}, bf16[3,128,192]{2,1,0:T(8,128)(2,1)S(1)}, bf16[384,768]{1,0:T(8,128)(2,1)S(1)}) custom-call(s32[6]{0:T(128)S(1)} %stack.24.refs_0_, bf16[1,144,768]{2,1,0:T(8,128)(2,1)S(1)} %bitcast.34, bf16[1,144,768]{2,1,0:T(8,128)(2,1)S(1)} %bitcast.35, bf16[1,144,768]{2,1,0:T(8,128)(2,1)S(1)} %bitcast.33, ...), custom_call_target="tpu_custom_call" | custom-call | flops 3449999872 | bytes 1024 | tf_op jit(solution)/shard_map/project/pallas_call | solution.py:132
  20.4 3.3 %collective-permute-done.3.refs_1_ = bf16[1,144,768]{2,1,0:T(8,128)(2,1)S(1)} collective-permute-done((bf16[1,144,768]{2,1,0:T(8,128)(2,1)S(1)}, bf16[1,144,768]{2,1,0:T(8,128)(2,1)S(1)}, u32[]{:S(2)}, u32[]{:S(2)}) %collective-permute-start.3) | collective-permute-done | bytes 221216 | tf_op jit(solution)/shard_map/ppermute | solution.py:46
  26.8 2.7 %collective-permute-start.7 = (bf16[128,768]{1,0:T(8,128)(2,1)S(1)}, bf16[128,768]{1,0:T(8,128)(2,1)S(1)}, u32[]{:S(2)}, u32[]{:S(2)}) collective-permute-start(bf16[128,768]{1,0:T(8,128)(2,1)S(1)} %bitcast.28), channel_id=1, source_target_pairs={{0,4},{1,5},{2,6},{3,7},{4,0},{5,1},{6,2},{7,3},{8,12},{9,13},{10,... | collective-permute-start | bytes 589832 | tf_op jit(solution)/shard_map/ppermute | solution.py:46
  29.6 5.9 %attention_forward.1 = (bf16[128,192]{1,0:T(8,128)(2,1)S(1)}, bf16[128,192]{1,0:T(8,128)(2,1)S(1)}, bf16[128,192]{1,0:T(8,128)(2,1)S(1)}, bf16[128,192]{1,0:T(8,...) custom-call(s32[6]{0:T(128)S(1)} %stack.24.refs_0_, ...), custom_call_target="tpu_custom_call" | custom-call | flops 11500000256 | bytes 1024 | tf_op jit(solution)/shard_map/attention_forward/pallas_call | solution.py:132
  36.8 2.2 %collective-permute-done.7.refs_11_ = bf16[128,768]{1,0:T(8,128)(2,1)S(1)} collective-permute-done((bf16[128,768]{1,0:T(8,128)(2,1)S(1)}, bf16[128,768]{1,0:T(8,128)(2,1)S(1)}, u32[]{:S(2)}, u32[]{:S(2)}) %collective-permute-start.7) | collective-permute-done | bytes 196640 | tf_op jit(solution)/shard_map/ppermute | solution.py:46
  39.2 2.4 %collective-permute-start.11 = (bf16[128,192]{1,0:T(8,128)(2,1)S(1)}, bf16[128,192]{1,0:T(8,128)(2,1)S(1)}, u32[]{:S(2)}, u32[]{:S(2)}) collective-permute-start(bf16[128,192]{1,0:T(8,128)(2,1)S(1)} %get-tuple-element.137), channel_id=1, source_target_pairs={{0,6},{1,14},{2,4},{3,12},{4,2},{5,10},{6,0},{7,8},{8,7},{9,15},{1... | collective-permute-start | bytes 147464 | tf_op jit(solution)/shard_map/ppermute | solution.py:46
  43.4 3.8 %collective-permute-done.10.refs_3_.refs_13_ = bf16[128,192]{1,0:T(8,128)(2,1)S(1)} collective-permute-done((bf16[128,192]{1,0:T(8,128)(2,1)S(1)}, bf16[128,192]{1,0:T(8,128)(2,1)S(1)}, u32[]{:S(2)}, u32[]{:S(2)}) %collective-permute-start.10) | collective-permute-done | bytes 49184 | tf_op jit(solution)/shard_map/ppermute | solution.py:46
  47.8 3.1 %ffn_forward.1 = (f32[128,768]{1,0:T(8,128)S(1)}, bf16[128,768]{1,0:T(8,128)(2,1)S(1)}, bf16[128,2048]{1,0:T(8,128)(2,1)S(1)}, f32[128,2048]{1,0:T(8,128)S(1)}, f32[128,2048]{1,0:T(8,128)S(1)}) custom-call(s32[6]{0:T(128)S(1)} %stack.24.refs_0_, bf16[128,192]{1,0:T(8,128)(2,1)S(1)} %collective-permute-done.8.refs_1_.refs_11_, ...), custom_call_target="tpu_custom_call" | custom-call | flops 16099999744 | bytes 1024 | tf_op jit(solution)/shard_map/ffn_forward/pallas_call | solution.py:132
  52.9 5.4 %ffn_backward.1 = (bf16[128,768]{1,0:T(8,128)(2,1)}, f32[128,768]{1,0:T(8,128)S(1)}, f32[1,768]{1,0:T(1,128)S(1)}, bf16[128,192]{1,0:T(8,128)(2,1)S(1)}, bf16[12...) custom-call(s32[6]{0:T(128)S(1)} %stack.24.refs_0_, ...), custom_call_target="tpu_custom_call" | custom-call | flops 6899999744 | bytes 1024 | tf_op jit(solution)/shard_map/ffn_backward/pallas_call | solution.py:132
  61.0 1.9 %collective-permute-start.14 = (bf16[128,192]{1,0:T(8,128)(2,1)S(1)}, bf16[128,192]{1,0:T(8,128)(2,1)S(1)}, u32[]{:S(2)}, u32[]{:S(2)}) collective-permute-start(bf16[128,192]{1,0:T(8,128)(2,1)S(1)} %get-tuple-element.145), channel_id=1, source_target_pairs={{0,4},{1,12},{2,6},{3,14},{4,0},{5,8},{6,2},{7,10},{8,5},{9,13},{1... | collective-permute-start | bytes 147464 | tf_op jit(solution)/shard_map/ppermute | solution.py:46
  64.7 2.0 %collective-permute-start.15 = (bf16[128,192]{1,0:T(8,128)(2,1)S(1)}, bf16[128,192]{1,0:T(8,128)(2,1)S(1)}, u32[]{:S(2)}, u32[]{:S(2)}) collective-permute-start(bf16[128,192]{1,0:T(8,128)(2,1)S(1)} %get-tuple-element.146), channel_id=1, source_target_pairs={{0,6},{1,14},{2,4},{3,12},{4,2},{5,10},{6,0},{7,8},{8,7},{9,15},{1... | collective-permute-start | bytes 147464 | tf_op jit(solution)/shard_map/ppermute | solution.py:46
  68.7 2.1 %collective-permute-done.15.refs_4_ = bf16[128,192]{1,0:T(8,128)(2,1)S(1)} collective-permute-done((bf16[128,192]{1,0:T(8,128)(2,1)S(1)}, bf16[128,192]{1,0:T(8,128)(2,1)S(1)}, u32[]{:S(2)}, u32[]{:S(2)}) %collective-permute-start.15) | collective-permute-done | bytes 49184 | tf_op jit(solution)/shard_map/ppermute | solution.py:46
  70.8 6.2 %attention_backward.1 = (bf16[128,192]{1,0:T(8,128)(2,1)S(1)}, bf16[128,192]{1,0:T(8,128)(2,1)S(1)}, bf16[128,192]{1,0:T(8,128)(2,1)S(1)}, bf16[128,192]{1,0:T(8...) custom-call(s32[6]{0:T(128)S(1)} %stack.24.refs_0_, ...), custom_call_target="tpu_custom_call" | custom-call | flops 11500000 | bytes 1024 | tf_op jit(solution)/shard_map/attention_backward/pallas_call | solution.py:132
  77.0 4.5 %collective-permute-start.17 = (bf16[1,4,128,384]{3,2,1,0:T(8,128)(2,1)S(1)}, bf16[1,4,128,384]{3,2,1,0:T(8,128)(2,1)S(1)}, u32[]{:S(2)}, u32[]{:S(2)}) collective-permute-start(bf16[1,4,128,384]{3,2,1,0:T(8,128)(2,1)S(1)} %get-tuple-element.162), channel_id=1, source_target_pairs={{0,8},{1,9},{2,10},{3,11},{4,12},{5,13},{6,14},{7,15},{8,0},{9,1},... | collective-permute-start | bytes 1179656 | tf_op jit(solution)/shard_map/ppermute | solution.py:46
  85.6 3.6 %ffn_grad.1 = (f32[2,64,2304]{2,1,0:T(8,128)S(1)}, bf16[2,64,2304]{2,1,0:T(8,128)(2,1)S(1)}) custom-call(s32[6]{0:T(128)S(1)} %stack.24.refs_0_, bf16[128,768]{1,0:T(8,128)(2,1)S(1)} %get-tuple-element.176.refs_1_, bf16[128,768]{1,0:T(8,128)(2,1)S(1)} %collective-permute-done.21.refs_2_, bf16[128,768]{1,0:T(8,128)(2,1)S(1)} %collective-permute-done.20.refs_3_, ...), custom_call_target="tpu_custom_call" | custom-call | flops 11500000 | bytes 1024 | tf_op jit(solution)/shard_map/ffn_grad/pallas_call | solution.py:132
  89.2 2.6 %qkv_grad.1 = (f32[2,192,576]{2,1,0:T(8,128)S(1)}, bf16[416,576]{1,0:T(8,128)(2,1)S(1)}, f32[24,128]{1,0:T(8,128)S(1)}) custom-call(s32[6]{0:T(128)S(1)} %stack.24.refs_0_, bf16[2,128,576]{2,1,0:T(8,128)(2,1)S(1)} %get-tuple-element.163.refs_1_, bf16[2,128,576]{2,1,0:T(8,128)(2,1)S(1)} %get-tuple-element.164.refs_2_, ...), custom_call_target="tpu_custom_call" | custom-call | flops 11500000 | bytes 1024 | tf_op jit(solution)/shard_map/qkv_grad/pallas_call | solution.py:132
  96.9 1.9 %collective-permute-start.37 = (bf16[224,576]{1,0:T(8,128)(2,1)S(1)}, bf16[224,576]{1,0:T(8,128)(2,1)S(1)}, u32[]{:S(2)}, u32[]{:S(2)}) collective-permute-start(bf16[224,576]{1,0:T(8,128)(2,1)S(1)} %get-tuple-element.207), channel_id=1, source_target_pairs={{0,1},{1,0},{2,3},{3,2},{4,5},{5,4},{6,7},{7,6},{8,9},{9,8},{10,11... | collective-permute-start | bytes 774152 | tf_op jit(solution)/shard_map/ppermute | solution.py:46
  98.8 2.9 %collective-permute-start.19 = (bf16[2,128,576]{2,1,0:T(8,128)(2,1)S(1)}, bf16[2,128,576]{2,1,0:T(8,128)(2,1)S(1)}, u32[]{:S(2)}, u32[]{:S(2)}) collective-permute-start(bf16[2,128,576]{2,1,0:T(8,128)(2,1)S(1)} %get-tuple-element.164.refs_2_), channel_id=1, source_target_pairs={{0,4},{1,12},{2,6},{3,14},{4,0},{5,8},{6,2},{7,10},{8,5},{9,13},{1... | collective-permute-start | bytes 884744 | tf_op jit(solution)/shard_map/ppermute | solution.py:46
  102.6 2.0 %collective-permute-done.35.refs_2_ = bf16[4,96,192]{2,1,0:T(8,128)(2,1)S(1)} collective-permute-done((bf16[4,96,192]{2,1,0:T(8,128)(2,1)S(1)}, bf16[4,96,192]{2,1,0:T(8,128)(2,1)S(1)}, u32[]{:S(2)}, u32[]{:S(2)}) %collective-permute-start.35) | collective-permute-done | bytes 147488 | tf_op jit(solution)/shard_map/ppermute | solution.py:46
  105.3 2.3 %collective-permute-done.36.refs_2_ = bf16[2,64,2304]{2,1,0:T(8,128)(2,1)S(1)} collective-permute-done((bf16[2,64,2304]{2,1,0:T(8,128)(2,1)S(1)}, bf16[2,64,2304]{2,1,0:T(8,128)(2,1)S(1)}, u32[]{:S(2)}, u32[]{:S(2)}) %collective-permute-start.36) | collective-permute-done | bytes 589856 | tf_op jit(solution)/shard_map/ppermute | solution.py:46
  111.7 1.9 %collective-permute-start.40 = (bf16[2,96,192]{2,1,0:T(8,128)(2,1)S(1)}, bf16[2,96,192]{2,1,0:T(8,128)(2,1)S(1)}, u32[]{:S(2)}, u32[]{:S(2)}) collective-permute-start(bf16[2,96,192]{2,1,0:T(8,128)(2,1)S(1)} %get-tuple-element.211), channel_id=1, source_target_pairs={{0,4},{1,5},{2,6},{3,7},{4,0},{5,1},{6,2},{7,3},{8,12},{9,13},{10,... | collective-permute-start | bytes 221192 | tf_op jit(solution)/shard_map/ppermute | solution.py:46
  113.7 5.8 %collective-permute-done.19.refs_1_.refs_2_ = bf16[2,128,576]{2,1,0:T(8,128)(2,1)S(1)} collective-permute-done((bf16[2,128,576]{2,1,0:T(8,128)(2,1)S(1)}, bf16[2,128,576]{2,1,0:T(8,128)(2,1)S(1)}, u32[]{:S(2)}, u32[]{:S(2)}) %collective-permute-start.19) | collective-permute-done | bytes 294944 | tf_op jit(solution)/shard_map/ppermute | solution.py:46
  120.2 3.7 %collective-permute-done.42 = f32[24,128]{1,0:T(8,128)S(1)} collective-permute-done((f32[24,128]{1,0:T(8,128)S(1)}, f32[24,128]{1,0:T(8,128)S(1)}, u32[]{:S(2)}, u32[]{:S(2)}) %collective-permute-start.42) | collective-permute-done | bytes 12320 | tf_op jit(solution)/shard_map/ppermute | solution.py:46
  124.7 2.0 %collective-permute-start.38 = (bf16[2,128,576]{2,1,0:T(8,128)(2,1)S(1)}, bf16[2,128,576]{2,1,0:T(8,128)(2,1)S(1)}, u32[]{:S(2)}, u32[]{:S(2)}) collective-permute-start(bf16[2,128,576]{2,1,0:T(8,128)(2,1)S(1)} %forwarded.1), channel_id=1, source_target_pairs={{0,2},{1,3},{2,0},{3,1},{4,6},{5,7},{6,4},{7,5},{8,10},{9,11},{10,... | collective-permute-start | bytes 884744 | tf_op jit(solution)/shard_map/ppermute | solution.py:46
  128.7 3.8 %collective-permute-start.46 = (bf16[96,512]{1,0:T(8,128)(2,1)S(1)}, bf16[96,512]{1,0:T(8,128)(2,1)S(1)}, u32[]{:S(2)}, u32[]{:S(2)}) collective-permute-start(bf16[96,512]{1,0:T(8,128)(2,1)S(1)} %get-tuple-element.227), channel_id=1, source_target_pairs={{0,0},{1,1},{2,16},{3,17},{4,4},{5,5},{6,20},{7,21},{8,8},{9,9},{1... | collective-permute-start | bytes 294920 | tf_op jit(solution)/shard_map/ppermute | solution.py:46
  132.4 2.7 %collective-permute-start.47 = (bf16[96,512]{1,0:T(8,128)(2,1)S(1)}, bf16[96,512]{1,0:T(8,128)(2,1)S(1)}, u32[]{:S(2)}, u32[]{:S(2)}) collective-permute-start(bf16[96,512]{1,0:T(8,128)(2,1)S(1)} %get-tuple-element.228), channel_id=1, source_target_pairs={{0,4},{1,5},{2,20},{3,21},{4,0},{5,1},{6,16},{7,17},{8,12},{9,13},... | collective-permute-start | bytes 294920 | tf_op jit(solution)/shard_map/ppermute | solution.py:46
  135.2 1.9 %collective-permute-start.44 = (bf16[96,576]{1,0:T(8,128)(2,1)S(1)}, bf16[96,576]{1,0:T(8,128)(2,1)S(1)}, u32[]{:S(2)}, u32[]{:S(2)}) collective-permute-start(bf16[96,576]{1,0:T(8,128)(2,1)S(1)} %bitcast.36), channel_id=1, source_target_pairs={{0,0},{1,1},{2,8},{3,9},{4,16},{5,17},{6,24},{7,25},{8,2},{9,3},{1... | collective-permute-start | bytes 331784 | tf_op jit(solution)/shard_map/ppermute | solution.py:46
  138.3 3.0 %collective-permute-done.46.refs_1_ = bf16[96,512]{1,0:T(8,128)(2,1)S(1)} collective-permute-done((bf16[96,512]{1,0:T(8,128)(2,1)S(1)}, bf16[96,512]{1,0:T(8,128)(2,1)S(1)}, u32[]{:S(2)}, u32[]{:S(2)}) %collective-permute-start.46) | collective-permute-done | bytes 98336 | tf_op jit(solution)/shard_map/ppermute | solution.py:46
  142.7 2.6 %collective-permute-done.44 = bf16[96,576]{1,0:T(8,128)(2,1)S(1)} collective-permute-done((bf16[96,576]{1,0:T(8,128)(2,1)S(1)}, bf16[96,576]{1,0:T(8,128)(2,1)S(1)}, u32[]{:S(2)}, u32[]{:S(2)}) %collective-permute-start.44) | collective-permute-done | bytes 110624 | tf_op jit(solution)/shard_map/ppermute | solution.py:46
  146.1 4.0 %input_grad.1 = f32[128,768]{1,0:T(8,128)} custom-call(s32[6]{0:T(128)S(1)} %stack.24.refs_0_, bf16[2,128,576]{2,1,0:T(8,128)(2,1)S(1)} %collective-permute-done.18.refs_0_.refs_1_, bf16[2,128,576]{2,1,0:T(8,128)(2,1)S(1)} %collective-permute-done.19.refs_1_.refs_2_, bf16[2,128,576]{2,1,0:T(8,128)(2,1)S(1)} %collective-permute-done.38.refs_3_, ...), custom_call_target="tpu_custom_call" | custom-call | flops 11500000 | bytes 1024 | tf_op jit(solution)/shard_map/input_grad/pallas_call | solution.py:132
  (122 shorter events, 45.8 us)
Async XLA Ops:
  2.3 14.0 %collective-permute-start.2 = (bf16[144,768]{1,0:T(8,128)(2,1)}, bf16[144,768]{1,0:T(8,128)(2,1)S(1)}, u32[]{:S(2)}, u32[]{:S(2)}) collective-permute-start(bf16[144,768]{1,0:T(8,128)(2,1)} %pack.1), channel_id=1, source_target_pairs={{0,4},{1,12},{2,6},{3,14},{4,0},{5,8},{6,2},{7,10},{8,5},{9,13},{1... | collective-permute-start | bytes 663560 | tf_op jit(solution)/shard_map/ppermute | solution.py:46
  5.0 12.4 %collective-permute-start = (bf16[144,768]{1,0:T(8,128)(2,1)}, bf16[144,768]{1,0:T(8,128)(2,1)S(1)}, u32[]{:S(2)}, u32[]{:S(2)}) collective-permute-start(bf16[144,768]{1,0:T(8,128)(2,1)} %pack.1), channel_id=1, source_target_pairs={{0,0},{1,8},{2,2},{3,10},{4,4},{5,12},{6,6},{7,14},{8,1},{9,9},{10... | collective-permute-start | bytes 663560 | tf_op jit(solution)/shard_map/ppermute | solution.py:46
  6.6 10.8 %collective-permute-start.1 = (bf16[144,768]{1,0:T(8,128)(2,1)}, bf16[144,768]{1,0:T(8,128)(2,1)S(1)}, u32[]{:S(2)}, u32[]{:S(2)}) collective-permute-start(bf16[144,768]{1,0:T(8,128)(2,1)} %pack.1), channel_id=1, source_target_pairs={{0,2},{1,10},{2,0},{3,8},{4,6},{5,14},{6,4},{7,12},{8,3},{9,11},{1... | collective-permute-start | bytes 663560 | tf_op jit(solution)/shard_map/ppermute | solution.py:46
  16.4 7.3 %collective-permute-start.3 = (bf16[1,144,768]{2,1,0:T(8,128)(2,1)S(1)}, bf16[1,144,768]{2,1,0:T(8,128)(2,1)S(1)}, u32[]{:S(2)}, u32[]{:S(2)}) collective-permute-start(bf16[1,144,768]{2,1,0:T(8,128)(2,1)S(1)} %bitcast.32), channel_id=1, source_target_pairs={{0,2},{1,3},{2,0},{3,1},{4,6},{5,7},{6,4},{7,5},{8,10},{9,11},{10,... | collective-permute-start | bytes 663560 | tf_op jit(solution)/shard_map/ppermute | solution.py:46
  19.6 9.9 %collective-permute-start.4 = (bf16[3,1,128,512]{3,2,1,0:T(8,128)(2,1)S(1)}, bf16[3,1,128,512]{3,2,1,0:T(8,128)(2,1)S(1)}, u32[]{:S(2)}, u32[]{:S(2)}) collective-permute-start(bf16[3,1,128,512]{3,2,1,0:T(8,128)(2,1)S(1)} %get-tuple-element.125.refs_1_), channel_id=1, source_target_pairs={{0,8},{1,9},{2,10},{3,11},{4,12},{5,13},{6,14},{7,15},{8,0},{9,1},... | collective-permute-start | bytes 1179656 | tf_op jit(solution)/shard_map/ppermute | solution.py:46
  25.5 11.3 %collective-permute-start.6 = (bf16[128,768]{1,0:T(8,128)(2,1)S(1)}, bf16[128,768]{1,0:T(8,128)(2,1)S(1)}, u32[]{:S(2)}, u32[]{:S(2)}) collective-permute-start(bf16[128,768]{1,0:T(8,128)(2,1)S(1)} %bitcast.27), channel_id=1, source_target_pairs={{0,2},{1,3},{2,0},{3,1},{4,6},{5,7},{6,4},{7,5},{8,10},{9,11},{10,... | collective-permute-start | bytes 589832 | tf_op jit(solution)/shard_map/ppermute | solution.py:46
  26.8 12.2 %collective-permute-start.7 = (bf16[128,768]{1,0:T(8,128)(2,1)S(1)}, bf16[128,768]{1,0:T(8,128)(2,1)S(1)}, u32[]{:S(2)}, u32[]{:S(2)}) collective-permute-start(bf16[128,768]{1,0:T(8,128)(2,1)S(1)} %bitcast.28), channel_id=1, source_target_pairs={{0,4},{1,5},{2,6},{3,7},{4,0},{5,1},{6,2},{7,3},{8,12},{9,13},{10,... | collective-permute-start | bytes 589832 | tf_op jit(solution)/shard_map/ppermute | solution.py:46
  39.0 8.2 %collective-permute-start.10 = (bf16[128,192]{1,0:T(8,128)(2,1)S(1)}, bf16[128,192]{1,0:T(8,128)(2,1)S(1)}, u32[]{:S(2)}, u32[]{:S(2)}) collective-permute-start(bf16[128,192]{1,0:T(8,128)(2,1)S(1)} %get-tuple-element.136), channel_id=1, source_target_pairs={{0,4},{1,12},{2,6},{3,14},{4,0},{5,8},{6,2},{7,10},{8,5},{9,13},{1... | collective-permute-start | bytes 147464 | tf_op jit(solution)/shard_map/ppermute | solution.py:46
  39.2 8.0 %collective-permute-start.11 = (bf16[128,192]{1,0:T(8,128)(2,1)S(1)}, bf16[128,192]{1,0:T(8,128)(2,1)S(1)}, u32[]{:S(2)}, u32[]{:S(2)}) collective-permute-start(bf16[128,192]{1,0:T(8,128)(2,1)S(1)} %get-tuple-element.137), channel_id=1, source_target_pairs={{0,6},{1,14},{2,4},{3,12},{4,2},{5,10},{6,0},{7,8},{8,7},{9,15},{1... | collective-permute-start | bytes 147464 | tf_op jit(solution)/shard_map/ppermute | solution.py:46
  51.0 15.6 %collective-permute-start.20 = (bf16[128,768]{1,0:T(8,128)(2,1)S(1)}, bf16[128,768]{1,0:T(8,128)(2,1)S(1)}, u32[]{:S(2)}, u32[]{:S(2)}) collective-permute-start(bf16[128,768]{1,0:T(8,128)(2,1)S(1)} %get-tuple-element.176.refs_1_), channel_id=1, source_target_pairs={{0,4},{1,5},{2,6},{3,7},{4,0},{5,1},{6,2},{7,3},{8,12},{9,13},{10,... | collective-permute-start | bytes 589832 | tf_op jit(solution)/shard_map/ppermute | solution.py:46
  52.1 18.7 %collective-permute-start.16 = (bf16[128,768]{1,0:T(8,128)(2,1)S(1)}, bf16[128,768]{1,0:T(8,128)(2,1)S(1)}, u32[]{:S(2)}, u32[]{:S(2)}) collective-permute-start(bf16[128,768]{1,0:T(8,128)(2,1)S(1)} %collective-permute-done.7.refs_11_), channel_id=1, source_target_pairs={{0,2},{1,3},{2,0},{3,1},{4,6},{5,7},{6,4},{7,5},{8,10},{9,11},{10,... | collective-permute-start | bytes 589832 | tf_op jit(solution)/shard_map/ppermute | solution.py:46
  60.5 21.1 %collective-permute-start.23 = (bf16[128,1152]{1,0:T(8,128)(2,1)S(1)}, bf16[128,1152]{1,0:T(8,128)(2,1)S(1)}, u32[]{:S(2)}, u32[]{:S(2)}) collective-permute-start(bf16[128,1152]{1,0:T(8,128)(2,1)S(1)} %get-tuple-element.171), channel_id=1, source_target_pairs={{0,16},{1,17},{2,18},{3,19},{4,20},{5,21},{6,22},{7,23},{8,24},{9,... | collective-permute-start | bytes 884744 | tf_op jit(solution)/shard_map/ppermute | solution.py:46
  61.0 6.0 %collective-permute-start.14 = (bf16[128,192]{1,0:T(8,128)(2,1)S(1)}, bf16[128,192]{1,0:T(8,128)(2,1)S(1)}, u32[]{:S(2)}, u32[]{:S(2)}) collective-permute-start(bf16[128,192]{1,0:T(8,128)(2,1)S(1)} %get-tuple-element.145), channel_id=1, source_target_pairs={{0,4},{1,12},{2,6},{3,14},{4,0},{5,8},{6,2},{7,10},{8,5},{9,13},{1... | collective-permute-start | bytes 147464 | tf_op jit(solution)/shard_map/ppermute | solution.py:46
  64.7 6.2 %collective-permute-start.15 = (bf16[128,192]{1,0:T(8,128)(2,1)S(1)}, bf16[128,192]{1,0:T(8,128)(2,1)S(1)}, u32[]{:S(2)}, u32[]{:S(2)}) collective-permute-start(bf16[128,192]{1,0:T(8,128)(2,1)S(1)} %get-tuple-element.146), channel_id=1, source_target_pairs={{0,6},{1,14},{2,4},{3,12},{4,2},{5,10},{6,0},{7,8},{8,7},{9,15},{1... | collective-permute-start | bytes 147464 | tf_op jit(solution)/shard_map/ppermute | solution.py:46
  66.6 14.9 %collective-permute-start.21 = (bf16[128,768]{1,0:T(8,128)(2,1)S(1)}, bf16[128,768]{1,0:T(8,128)(2,1)S(1)}, u32[]{:S(2)}, u32[]{:S(2)}) collective-permute-start(bf16[128,768]{1,0:T(8,128)(2,1)S(1)} %get-tuple-element.176.refs_1_), channel_id=1, source_target_pairs={{0,2},{1,3},{2,0},{3,1},{4,6},{5,7},{6,4},{7,5},{8,10},{9,11},{10,... | collective-permute-start | bytes 589832 | tf_op jit(solution)/shard_map/ppermute | solution.py:46
  67.0 14.6 %collective-permute-start.22 = (bf16[128,768]{1,0:T(8,128)(2,1)S(1)}, bf16[128,768]{1,0:T(8,128)(2,1)S(1)}, u32[]{:S(2)}, u32[]{:S(2)}) collective-permute-start(bf16[128,768]{1,0:T(8,128)(2,1)S(1)} %collective-permute-done.20.refs_3_), channel_id=1, source_target_pairs={{0,2},{1,3},{2,0},{3,1},{4,6},{5,7},{6,4},{7,5},{8,10},{9,11},{10,... | collective-permute-start | bytes 589832 | tf_op jit(solution)/shard_map/ppermute | solution.py:46
  77.0 7.1 %collective-permute-start.17 = (bf16[1,4,128,384]{3,2,1,0:T(8,128)(2,1)S(1)}, bf16[1,4,128,384]{3,2,1,0:T(8,128)(2,1)S(1)}, u32[]{:S(2)}, u32[]{:S(2)}) collective-permute-start(bf16[1,4,128,384]{3,2,1,0:T(8,128)(2,1)S(1)} %get-tuple-element.162), channel_id=1, source_target_pairs={{0,8},{1,9},{2,10},{3,11},{4,12},{5,13},{6,14},{7,15},{8,0},{9,1},... | collective-permute-start | bytes 1179656 | tf_op jit(solution)/shard_map/ppermute | solution.py:46
  92.1 15.4 %collective-permute-start.36 = (bf16[2,64,2304]{2,1,0:T(8,128)(2,1)S(1)}, bf16[2,64,2304]{2,1,0:T(8,128)(2,1)S(1)}, u32[]{:S(2)}, u32[]{:S(2)}) collective-permute-start(bf16[2,64,2304]{2,1,0:T(8,128)(2,1)S(1)} %get-tuple-element.188), channel_id=1, source_target_pairs={{0,16},{1,17},{2,18},{3,19},{4,20},{5,21},{6,22},{7,23},{8,24},{9,... | collective-permute-start | bytes 1769480 | tf_op jit(solution)/shard_map/ppermute | solution.py:46
  96.2 8.5 %collective-permute-start.35 = (bf16[4,96,192]{2,1,0:T(8,128)(2,1)S(1)}, bf16[4,96,192]{2,1,0:T(8,128)(2,1)S(1)}, u32[]{:S(2)}, u32[]{:S(2)}) collective-permute-start(bf16[4,96,192]{2,1,0:T(8,128)(2,1)S(1)} %get-tuple-element.202), channel_id=1, source_target_pairs={{0,2},{1,3},{2,0},{3,1},{4,6},{5,7},{6,4},{7,5},{8,10},{9,11},{10,... | collective-permute-start | bytes 442376 | tf_op jit(solution)/shard_map/ppermute | solution.py:46
  96.9 12.6 %collective-permute-start.37 = (bf16[224,576]{1,0:T(8,128)(2,1)S(1)}, bf16[224,576]{1,0:T(8,128)(2,1)S(1)}, u32[]{:S(2)}, u32[]{:S(2)}) collective-permute-start(bf16[224,576]{1,0:T(8,128)(2,1)S(1)} %get-tuple-element.207), channel_id=1, source_target_pairs={{0,1},{1,0},{2,3},{3,2},{4,5},{5,4},{6,7},{7,6},{8,9},{9,8},{10,11... | collective-permute-start | bytes 774152 | tf_op jit(solution)/shard_map/ppermute | solution.py:46
  98.8 20.6 %collective-permute-start.19 = (bf16[2,128,576]{2,1,0:T(8,128)(2,1)S(1)}, bf16[2,128,576]{2,1,0:T(8,128)(2,1)S(1)}, u32[]{:S(2)}, u32[]{:S(2)}) collective-permute-start(bf16[2,128,576]{2,1,0:T(8,128)(2,1)S(1)} %get-tuple-element.164.refs_2_), channel_id=1, source_target_pairs={{0,4},{1,12},{2,6},{3,14},{4,0},{5,8},{6,2},{7,10},{8,5},{9,13},{1... | collective-permute-start | bytes 884744 | tf_op jit(solution)/shard_map/ppermute | solution.py:46
  101.7 17.8 %collective-permute-start.18 = (bf16[2,128,576]{2,1,0:T(8,128)(2,1)S(1)}, bf16[2,128,576]{2,1,0:T(8,128)(2,1)S(1)}, u32[]{:S(2)}, u32[]{:S(2)}) collective-permute-start(bf16[2,128,576]{2,1,0:T(8,128)(2,1)S(1)} %get-tuple-element.163.refs_1_), channel_id=1, source_target_pairs={{0,0},{1,8},{2,2},{3,10},{4,4},{5,12},{6,6},{7,14},{8,1},{9,9},{10... | collective-permute-start | bytes 884744 | tf_op jit(solution)/shard_map/ppermute | solution.py:46
  108.3 19.0 %collective-permute-start.41 = (bf16[1,64,2304]{2,1,0:T(8,128)(2,1)S(1)}, bf16[1,64,2304]{2,1,0:T(8,128)(2,1)S(1)}, u32[]{:S(2)}, u32[]{:S(2)}) collective-permute-start(bf16[1,64,2304]{2,1,0:T(8,128)(2,1)S(1)} %get-tuple-element.226), channel_id=1, source_target_pairs={{0,1},{1,0},{2,3},{3,2},{4,5},{5,4},{6,7},{7,6},{8,9},{9,8},{10,11... | collective-permute-start | bytes 884744 | tf_op jit(solution)/shard_map/ppermute | solution.py:46
  110.2 9.4 %collective-permute-start.39 = (bf16[128,576]{1,0:T(8,128)(2,1)S(1)}, bf16[128,576]{1,0:T(8,128)(2,1)S(1)}, u32[]{:S(2)}, u32[]{:S(2)}) collective-permute-start(bf16[128,576]{1,0:T(8,128)(2,1)S(1)} %get-tuple-element.216), channel_id=1, source_target_pairs={{0,16},{1,17},{2,18},{3,19},{4,20},{5,21},{6,22},{7,23},{8,24},{9,... | collective-permute-start | bytes 442376 | tf_op jit(solution)/shard_map/ppermute | solution.py:46
  111.7 15.0 %collective-permute-start.40 = (bf16[2,96,192]{2,1,0:T(8,128)(2,1)S(1)}, bf16[2,96,192]{2,1,0:T(8,128)(2,1)S(1)}, u32[]{:S(2)}, u32[]{:S(2)}) collective-permute-start(bf16[2,96,192]{2,1,0:T(8,128)(2,1)S(1)} %get-tuple-element.211), channel_id=1, source_target_pairs={{0,4},{1,5},{2,6},{3,7},{4,0},{5,1},{6,2},{7,3},{8,12},{9,13},{10,... | collective-permute-start | bytes 221192 | tf_op jit(solution)/shard_map/ppermute | solution.py:46
  123.9 11.3 %collective-permute-start.43 = (f32[24,128]{1,0:T(8,128)S(1)}, f32[24,128]{1,0:T(8,128)S(1)}, u32[]{:S(2)}, u32[]{:S(2)}) collective-permute-start(f32[24,128]{1,0:T(8,128)S(1)} %add.18), channel_id=1, source_target_pairs={{0,4},{1,5},{2,6},{3,7},{4,0},{5,1},{6,2},{7,3},{8,12},{9,13},{10,... | collective-permute-start | bytes 36872 | tf_op jit(solution)/shard_map/ppermute | solution.py:46
  124.7 21.4 %collective-permute-start.38 = (bf16[2,128,576]{2,1,0:T(8,128)(2,1)S(1)}, bf16[2,128,576]{2,1,0:T(8,128)(2,1)S(1)}, u32[]{:S(2)}, u32[]{:S(2)}) collective-permute-start(bf16[2,128,576]{2,1,0:T(8,128)(2,1)S(1)} %forwarded.1), channel_id=1, source_target_pairs={{0,2},{1,3},{2,0},{3,1},{4,6},{5,7},{6,4},{7,5},{8,10},{9,11},{10,... | collective-permute-start | bytes 884744 | tf_op jit(solution)/shard_map/ppermute | solution.py:46
  128.0 10.3 %collective-permute-start.48 = (bf16[256,192]{1,0:T(8,128)(2,1)S(1)}, bf16[256,192]{1,0:T(8,128)(2,1)S(1)}, u32[]{:S(2)}, u32[]{:S(2)}) collective-permute-start(bf16[256,192]{1,0:T(8,128)(2,1)S(1)} %get-tuple-element.229), channel_id=1, source_target_pairs={{0,0},{1,8},{2,4},{3,12},{4,1},{5,9},{6,5},{7,13},{8,2},{9,10},{10... | collective-permute-start | bytes 294920 | tf_op jit(solution)/shard_map/ppermute | solution.py:46
  128.7 12.7 %collective-permute-start.46 = (bf16[96,512]{1,0:T(8,128)(2,1)S(1)}, bf16[96,512]{1,0:T(8,128)(2,1)S(1)}, u32[]{:S(2)}, u32[]{:S(2)}) collective-permute-start(bf16[96,512]{1,0:T(8,128)(2,1)S(1)} %get-tuple-element.227), channel_id=1, source_target_pairs={{0,0},{1,1},{2,16},{3,17},{4,4},{5,5},{6,20},{7,21},{8,8},{9,9},{1... | collective-permute-start | bytes 294920 | tf_op jit(solution)/shard_map/ppermute | solution.py:46
  132.4 8.9 %collective-permute-start.47 = (bf16[96,512]{1,0:T(8,128)(2,1)S(1)}, bf16[96,512]{1,0:T(8,128)(2,1)S(1)}, u32[]{:S(2)}, u32[]{:S(2)}) collective-permute-start(bf16[96,512]{1,0:T(8,128)(2,1)S(1)} %get-tuple-element.228), channel_id=1, source_target_pairs={{0,4},{1,5},{2,20},{3,21},{4,0},{5,1},{6,16},{7,17},{8,12},{9,13},... | collective-permute-start | bytes 294920 | tf_op jit(solution)/shard_map/ppermute | solution.py:46
  135.2 10.2 %collective-permute-start.44 = (bf16[96,576]{1,0:T(8,128)(2,1)S(1)}, bf16[96,576]{1,0:T(8,128)(2,1)S(1)}, u32[]{:S(2)}, u32[]{:S(2)}) collective-permute-start(bf16[96,576]{1,0:T(8,128)(2,1)S(1)} %bitcast.36), channel_id=1, source_target_pairs={{0,0},{1,1},{2,8},{3,9},{4,16},{5,17},{6,24},{7,25},{8,2},{9,3},{1... | collective-permute-start | bytes 331784 | tf_op jit(solution)/shard_map/ppermute | solution.py:46
  138.3 11.8 %collective-permute-start.45 = (bf16[1,96,192]{2,1,0:T(8,128)(2,1)S(1)}, bf16[1,96,192]{2,1,0:T(8,128)(2,1)S(1)}, u32[]{:S(2)}, u32[]{:S(2)}) collective-permute-start(bf16[1,96,192]{2,1,0:T(8,128)(2,1)S(1)} %get-tuple-element.224), channel_id=1, source_target_pairs={{0,1},{1,0},{2,3},{3,2},{4,5},{5,4},{6,7},{7,6},{8,9},{9,8},{10,11... | collective-permute-start | bytes 110600 | tf_op jit(solution)/shard_map/ppermute | solution.py:46
  (29 other events, 194.1 us)
